TPU v7x, 128 devices: a whole 4x4x4 slice. The times are simulated.
128 devices in a mesh: dp: 2 (over y_hi), seq: 16 (over z, x), chan: 4 (over y_lo, core).
Axes of the slice: x: 4, y: 4 (y_hi: 2, y_lo: 2; y = y_hi * 2 + y_lo), z: 4, core: 2. Of those that a mesh axis runs over, the one named last changes fastest.
Arguments:
- inputs: float32 [2, 256, 16384], P('dp', 'chan', 'seq'), may hold values from -6 to 6
- cotangent: float32 [2, 256, 16384], P('dp', 'chan', 'seq'), may hold values from -6 to 6
- conv_weight: float32 [3, 256], P(None, 'chan'), may hold values from -3.5 to 3.5
- kernel: float32 [256, 16384], P(('chan', 'seq')), may hold values from -3 to 3
- skip_gain: float32 [256], P(('chan', 'seq')), may hold values from 0.5 to 1.5
- mix_weight: float32 [256, 256], P(None, 'chan'), may hold values from -0.375 to 0.375
Outputs:
- outputs: float32 [2, 256, 16384], P('dp', 'chan', 'seq')
- grad_inputs: float32 [2, 256, 16384], P('dp', 'chan', 'seq')
- grad_kernel: float32 [256, 16384], P(('chan', 'seq'))
- grad_skip: float32 [256], P(('chan', 'seq'))
- grad_mix: float32 [256, 256], P(None, 'chan')
- grad_conv: float32 [3, 256], P(None, 'chan')
All inputs are finite; a program needn't handle non-finite values.
Results may differ from a plain program's by a relative error of at most 0.00028.
Values sent between devices are 32-bit elements; how exact they have to be, the bound alone decides.
No kernel may reach another device: no remote copies, remote signals or barrier semaphores. Data moves between devices by JAX's collectives and lax.ppermute only.
A program may use at most 128 MiB of HBM per device.

v0:
```python
import math

import jax
import jax.numpy as jnp
from jax import lax
from jax.sharding import PartitionSpec as P

HIGH = lax.Precision.HIGHEST


def shifted(value, axis, steps):
    count = lax.axis_size(axis)
    first, last = (max(0, -steps), min(count, count - steps))
    return lax.ppermute(value, axis, [(source, source + steps) for source in range(first, last)])


def tables(extent, direction):
    index = jnp.arange(extent, dtype=jnp.int32)
    product = index[:, None] * index[None, :] % extent
    angle = direction * 2.0 * math.pi * product.astype(jnp.float32) / extent
    return (jnp.cos(angle), jnp.sin(angle))


def mat_left(table, values):
    return jnp.einsum("kn,cnm->ckm", table, values, precision=HIGH)


def mat_right(values, table):
    return jnp.einsum("ckm,mj->ckj", values, table, precision=HIGH)


def transform(real_part, imag_part, direction):
    rows_in, extent = real_part.shape
    first = 2 ** ((extent.bit_length() - 1) // 2)
    second = extent // first
    cos_one, sin_one = tables(first, direction)
    cos_two, sin_two = tables(second, direction)
    twist = (
        jnp.arange(first, dtype=jnp.int32)[:, None]
        * jnp.arange(second, dtype=jnp.int32)[None, :]
        % extent
    )
    twist_angle = direction * 2.0 * math.pi * twist.astype(jnp.float32) / extent
    twist_cos, twist_sin = (jnp.cos(twist_angle), jnp.sin(twist_angle))
    real_grid = real_part.reshape(rows_in, first, second)
    if imag_part is None:
        step_real = mat_left(cos_one, real_grid)
        step_imag = mat_left(sin_one, real_grid)
    else:
        imag_grid = imag_part.reshape(rows_in, first, second)
        step_real = mat_left(cos_one, real_grid) - mat_left(sin_one, imag_grid)
        step_imag = mat_left(cos_one, imag_grid) + mat_left(sin_one, real_grid)
    turned_real = step_real * twist_cos - step_imag * twist_sin
    turned_imag = step_real * twist_sin + step_imag * twist_cos
    final_real = mat_right(turned_real, cos_two) - mat_right(turned_imag, sin_two)
    final_imag = mat_right(turned_real, sin_two) + mat_right(turned_imag, cos_two)
    final_real = jnp.transpose(final_real, (0, 2, 1)).reshape(rows_in, extent)
    final_imag = jnp.transpose(final_imag, (0, 2, 1)).reshape(rows_in, extent)
    return (final_real, final_imag)


def forward_spectrum(signal):
    padded = jnp.concatenate([signal, jnp.zeros_like(signal)], axis=1)
    return transform(padded, None, -1.0)


def inverse_real(real_part, imag_part, length):
    extent = real_part.shape[1]
    back_real, back_imag = transform(real_part, imag_part, 1.0)
    return back_real[:, :length] / extent


def shards(inputs, cotangent, conv_weight, kernel, skip_gain, mix_weight):
    signal = inputs[0]
    grad_out = cotangent[0]
    width = signal.shape[1]
    before = shifted(signal[:, width - 2 :], "seq", 1)
    padded = jnp.concatenate([before, signal], axis=1)
    conv = (
        conv_weight[0][:, None] * padded[:, :width]
        + conv_weight[1][:, None] * padded[:, 1 : width + 1]
    )
    conv = conv + conv_weight[2][:, None] * padded[:, 2:]
    long_in = lax.all_to_all(conv[None], "seq", split_axis=1, concat_axis=2, tiled=True)[0]
    length = long_in.shape[1]
    sig_real, sig_imag = forward_spectrum(long_in)
    ker_real, ker_imag = forward_spectrum(kernel)
    prod_real = sig_real * ker_real - sig_imag * ker_imag
    prod_imag = sig_real * ker_imag + sig_imag * ker_real
    long_out = inverse_real(prod_real, prod_imag, length) + skip_gain[:, None] * long_in
    mixed_in = lax.all_to_all(long_out[None], "seq", split_axis=2, concat_axis=1, tiled=True)[0]
    activated, gelu_back = jax.vjp(jax.nn.gelu, mixed_in)
    gathered = lax.all_gather(activated, "chan", axis=0, tiled=True)
    outputs = signal + jnp.einsum("co,ct->ot", mix_weight, gathered, precision=HIGH)
    grad_weight = jnp.einsum("ct,ot->co", gathered, grad_out, precision=HIGH)
    grad_act = lax.psum_scatter(
        jnp.einsum("co,ot->ct", mix_weight, grad_out, precision=HIGH),
        "chan",
        scatter_dimension=0,
        tiled=True,
    )
    grad_mixed = gelu_back(grad_act)[0]
    grad_long = lax.all_to_all(grad_mixed[None], "seq", split_axis=1, concat_axis=2, tiled=True)[0]
    grad_real, grad_imag = forward_spectrum(grad_long)
    corr_real = ker_real * grad_real + ker_imag * grad_imag
    corr_imag = ker_real * grad_imag - ker_imag * grad_real
    grad_conv_long = inverse_real(corr_real, corr_imag, length) + skip_gain[:, None] * grad_long
    cross_real = sig_real * grad_real + sig_imag * grad_imag
    cross_imag = sig_real * grad_imag - sig_imag * grad_real
    kernel_local = inverse_real(cross_real, cross_imag, length)
    skip_local = jnp.sum(grad_long * long_in, axis=1)
    grad_kernel, grad_skip = lax.psum((kernel_local, skip_local), "dp")
    grad_conv_in = lax.all_to_all(
        grad_conv_long[None], "seq", split_axis=2, concat_axis=1, tiled=True
    )[0]
    after = shifted(grad_conv_in[:, :2], "seq", -1)
    extended = jnp.concatenate([grad_conv_in, after], axis=1)
    grad_inputs = grad_out + conv_weight[2][:, None] * extended[:, :width]
    grad_inputs = grad_inputs + conv_weight[1][:, None] * extended[:, 1 : width + 1]
    grad_inputs = grad_inputs + conv_weight[0][:, None] * extended[:, 2:]
    taps_local = jnp.stack(
        [jnp.sum(grad_conv_in * padded[:, offset : offset + width], axis=1) for offset in range(3)],
        axis=0,
    )
    grad_mix, grad_conv = lax.psum((grad_weight, taps_local), ("dp", "seq"))
    return (outputs[None], grad_inputs[None], grad_kernel, grad_skip, grad_mix, grad_conv)


def solution(mesh):
    placed = (
        P("dp", "chan", "seq"),
        P("dp", "chan", "seq"),
        P(None, "chan"),
        P(("chan", "seq"), None),
        P(("chan", "seq")),
        P(None, "chan"),
    )
    return jax.shard_map(
        shards,
        mesh=mesh,
        in_specs=placed,
        out_specs=(
            P("dp", "chan", "seq"),
            P("dp", "chan", "seq"),
            P(("chan", "seq"), None),
            P(("chan", "seq")),
            P(None, "chan"),
            P(None, "chan"),
        ),
        check_vma=False,
    )
```

profile of v0, /device:TPU:0, one launch (start us, length us, event | category | flops | bytes accessed | tf_op | source)
XLA Modules:
  0.0 800.5 jit_solution(12288578697394821372)
XLA Ops:
  8.1 3.5 collective-permute-start
  11.6 3.0 fusion.63
  18.5 1.9 fusion.74
  20.4 2.7 fusion.85
  23.1 1.9 convolution_add_fusion.4
  26.7 7.8 all-to-all-start
  34.5 2.9 convolution_subtract_fusion.7
  37.5 5.6 all-to-all-done
  45.8 1.9 fusion.87
  47.7 1.9 fusion.76
  49.6 1.9 convolution_subtract_fusion.8
  51.5 2.3 convolution_add_fusion.5
  56.4 1.9 fusion.139
  60.8 2.2 fusion.5
  64.1 1.9 fusion.34
  66.0 2.7 fusion.8
  71.3 12.1 %copy.104 = f32[1,4,16384]{1,0,2:T(1,128)} copy(f32[1,4,16384]{2,1,0:T(4,128)S(1)} %fusion.60) | data formatting | bytes 524288 | tf_op jit(solution)/shard_map/broadcast_in_dim | solution.py:91
  83.9 74.6 %reduce.2 = f32[16384,4]{1,0:T(8,128)} reduce(f32[16384,1,4]{2,1,0:T(1,128)} %bitcast.233, f32[]{:T(128)} %broadcast.324), dimensions={1}, to_apply=%bitcast.206.reduce_sub_computation | reduce | bytes 524292
  158.6 8.5 %reshape.166 = f32[16,1,4096]{2,1,0:T(1,128)S(1)} reshape(f32[16384,4]{1,0:T(8,128)} %reduce.2) | data formatting | bytes 524288
  167.0 11.6 %all_to_all.60 = f32[16,1,4096]{2,1,0:T(1,128)S(1)} all-to-all(f32[16,1,4096]{2,1,0:T(1,128)S(1)} %reshape.166), channel_id=1, replica_groups=mesh['dp'=2,'seq'=16,'chan'=4] {'seq'}, dimensions={0} | all-to-all | bytes 524288 | tf_op jit(solution)/shard_map/all_to_all | solution.py:91
  179.9 15.6 %reshape.167 = f32[16384,1,4]{2,1,0:T(1,128)} reshape(f32[16,4096]{1,0:T(8,128)S(1)} %reduce.3) | data formatting | bytes 524288
  195.5 5.2 copy.105
  200.9 1.9 fusion.51
  203.7 3.9 all-to-all-start.2
  208.5 7.4 all-to-all-done.2
  219.1 1.9 fusion.81
  221.0 1.9 fusion.71
  222.8 1.4 multiply_reduce_fusion.3
  224.2 1.9 convolution_add_fusion.3
  226.2 3.4 add_bitcast_fusion
  231.0 1.3 fusion.135
  237.0 1.9 fusion.27
  238.9 1.9 fusion.7
  241.5 12.1 %copy.123 = f32[1,4,16384]{1,0,2:T(1,128)} copy(f32[1,4,16384]{2,1,0:T(4,128)S(1)} %fusion.58) | data formatting | bytes 524288 | tf_op jit(solution)/shard_map/broadcast_in_dim | solution.py:114
  253.6 74.5 %reduce.4 = f32[16384,4]{1,0:T(8,128)} reduce(f32[16384,1,4]{2,1,0:T(1,128)} %bitcast.234, f32[]{:T(128)} %broadcast.324), dimensions={1}, to_apply=%bitcast.208.reduce_sub_computation | reduce | bytes 524292
  328.1 9.2 %reshape.168 = f32[16,1,4096]{2,1,0:T(1,128)} reshape(f32[16384,4]{1,0:T(8,128)} %reduce.4) | data formatting | bytes 524288
  337.3 3.5 all-to-all-start.3
  346.3 1.9 fusion.20
  348.2 1.9 fusion.6
  351.4 6.9 psum.29
  359.9 15.6 %reshape.169 = f32[16384,1,4]{2,1,0:T(1,128)} reshape(f32[16,4096]{1,0:T(8,128)S(1)} %reduce.5) | data formatting | bytes 524288
  375.5 5.2 copy.124
  382.7 98.7 %psum.31 = f32[3,64]{1,0:T(4,128)} all-reduce(f32[3,64]{1,0:T(4,128)S(1)} %pad_maximum_fusion.1), channel_id=1, replica_groups=mesh['dp'=2,'seq'=16,'chan'=4] {'dp','seq'}, use_global_device_ids=true, to_apply=%region_8.9 | all-reduce | flops 192 | bytes 1536 | tf_op jit(solution)/shard_map/psum | solution.py:125
  482.4 2.9 fusion.61
  485.4 2.7 fusion.10
  488.1 302.3 %all-reduce.8.cloned.1.call-done = f32[256,64]{0,1:T(8,128)} async-done(((f32[256,64]{0,1:T(8,128)}), f32[256,64]{0,1:T(8,128)}) %all-reduce.8.cloned.1.call-update) | async-done | bytes 65552 | tf_op jit(solution)/shard_map/psum | solution.py:125
  790.4 1.7 copy.219
  792.1 1.5 copy.220
  (113 shorter events, 43.0 us)
Async XLA Ops:
  7.2 4.4 copy-start
  7.2 18.3 %copy-start.5 = (f32[1,64,1024]{2,1,0:T(8,128)S(1)}, f32[1,64,1024]{2,1,0:T(8,128)}, u32[]{:S(2)}) copy-start(f32[1,64,1024]{2,1,0:T(8,128)} %param.6) | copy-start | bytes 786436
  7.2 15.9 %copy-start.16 = (f32[3,64]{1,0:T(4,128)S(1)}, f32[3,64]{1,0:T(4,128)}, u32[]{:S(2)}) copy-start(f32[3,64]{1,0:T(4,128)} %param.8) | copy-start | bytes 2308
  7.2 193.6 %reduce-scatter.2.cloned.1.call-start = ((), (), s32[]{:S(2)}) async-start(), calls=%async_computation.6 | async-start | bytes 1310720 | tf_op jit(solution)/shard_map/reduce_scatter | solution.py:96
  8.1 17.4 %collective-permute-start = (f32[64,2]{1,0:T(8,128)S(1)}, f32[64,2]{1,0:T(8,128)S(1)}, u32[]{:S(2)}, u32[]{:S(2)}) collective-permute-start(f32[64,2]{1,0:T(8,128)S(1)} %slice.53), channel_id=1, source_target_pairs={{0,4},{4,8},{8,12},{12,16},{16,20},{20,24},{24,28},{28,32},{32,36}... | collective-permute-start | bytes 1544 | tf_op jit(solution)/shard_map/ppermute | solution.py:14
  26.7 16.3 %all-to-all-start = ((f32[1,64,1024]{2,0,1:T(1,128)}), f32[1,64,1024]{2,0,1:T(1,128)S(1)}, u32[]{:S(2)}, u32[]{:S(2)}) async-start(f32[1,64,1024]{2,0,1:T(1,128)} %copy.81), calls=%async_computation | async-start | bytes 524288 | tf_op jit(solution)/shard_map/all_to_all | solution.py:84
  43.0 4.7 copy-start.6
  43.4 4.3 copy-start.10
  51.5 6.8 copy-start.1
  53.8 1.2 copy-start.3
  55.0 15.3 %copy-start.15 = (f32[4]{0:T(128)S(1)}, f32[4]{0:T(128)}, u32[]{:S(2)}) copy-start(f32[4]{0:T(128)} %param.10) | copy-start | bytes 52
  200.7 25.4 %copy-start.2 = (f32[4,128,256]{2,1,0:T(8,128)S(1)}, f32[4,128,256]{2,1,0:T(8,128)}, u32[]{:S(2)}) copy-start(f32[4,128,256]{2,1,0:T(8,128)} %copy-done.1) | copy-start | bytes 1572868
  200.7 25.4 %copy-start.4 = (f32[4,128,256]{2,1,0:T(8,128)S(1)}, f32[4,128,256]{2,1,0:T(8,128)}, u32[]{:S(2)}) copy-start(f32[4,128,256]{2,1,0:T(8,128)} %copy-done.3) | copy-start | bytes 1572868
  203.7 12.2 %all-to-all-start.2 = ((f32[1,64,1024]{2,0,1:T(1,128)}), f32[1,64,1024]{2,0,1:T(1,128)S(1)}, u32[]{:S(2)}, u32[]{:S(2)}) async-start(f32[1,64,1024]{2,0,1:T(1,128)} %copy.106), calls=%async_computation.3 | async-start | bytes 524288 | tf_op jit(solution)/shard_map/all_to_all | solution.py:103
  207.7 274.7 %all-gather.2.cloned.1.call-start = ((), (), s32[]{:S(2)}) async-start(), calls=%async_computation.5 | async-start | bytes 1310720 | tf_op jit(solution)/shard_map/all_gather | solution.py:93
  215.9 0.7 copy-start.7
  216.6 2.4 copy-start.8
  229.5 11.8 %copy-start.9 = (f32[1,4,16,1024]{3,1,2,0:T(4,128)S(1)}, f32[1,4,16,1024]{3,1,2,0:T(4,128)}, u32[]{:S(2)}) copy-start(f32[1,4,16,1024]{3,1,2,0:T(4,128)} %copy-done.8) | copy-start | bytes 786436
  328.1 13.0 %copy-start.13 = (f32[4,256,128]{1,2,0:T(8,128)S(1)}, f32[4,256,128]{1,2,0:T(8,128)}, u32[]{:S(2)}) copy-start(f32[4,256,128]{1,2,0:T(8,128)} %get-tuple-element.8) | copy-start | bytes 1572868
  328.1 14.5 %copy-start.12 = (f32[4,256,128]{1,2,0:T(8,128)S(1)}, f32[4,256,128]{1,2,0:T(8,128)}, u32[]{:S(2)}) copy-start(f32[4,256,128]{1,2,0:T(8,128)} %get-tuple-element.9) | copy-start | bytes 1572868
  337.3 21.3 %all-to-all-start.3 = ((f32[16,1,4096]{2,1,0:T(1,128)}), f32[16,1,4096]{2,1,0:T(1,128)S(1)}, u32[]{:S(2)}, u32[]{:S(2)}) async-start(f32[16,1,4096]{2,1,0:T(1,128)} %reshape.168), calls=%async_computation.4 | async-start | bytes 524288 | tf_op jit(solution)/shard_map/all_to_all | solution.py:113
  340.8 147.3 %all-reduce.6.cloned.1.call-start = ((), (), s32[]{:S(2)}) async-start(), calls=%async_computation.7 | async-start | bytes 524288 | tf_op jit(solution)/shard_map/psum | solution.py:112
  358.3 432.1 %all-reduce.8.cloned.1.call-start = ((), (), s32[]{:S(2)}) async-start(), calls=%async_computation.8 | async-start | bytes 131072 | tf_op jit(solution)/shard_map/psum | solution.py:125
  359.9 21.0 %copy-start.14 = (f32[1,16,4,1024]{3,2,1,0:T(4,128)S(1)}, f32[1,16,4,1024]{3,2,1,0:T(4,128)}, u32[]{:S(2)}) copy-start(f32[1,16,4,1024]{3,2,1,0:T(4,128)} %squeeze.26) | copy-start | bytes 786436
  359.9 121.6 %copy-start.11 = (f32[1,64,1024]{2,1,0:T(8,128)S(1)}, f32[1,64,1024]{2,1,0:T(8,128)}, u32[]{:S(2)}) copy-start(f32[1,64,1024]{2,1,0:T(8,128)} %param.7) | copy-start | bytes 786436
  381.1 100.4 %collective-permute-start.1 = (f32[64,2]{1,0:T(8,128)S(1)}, f32[64,2]{1,0:T(8,128)S(1)}, u32[]{:S(2)}, u32[]{:S(2)}) collective-permute-start(f32[64,2]{1,0:T(8,128)S(1)} %slice.58), channel_id=1, source_target_pairs={{4,0},{8,4},{12,8},{16,12},{20,16},{24,20},{28,24},{32,28},{36,32}... | collective-permute-start | bytes 1544 | tf_op jit(solution)/shard_map/ppermute | solution.py:14
Sparse Core Ops, SparseCore 0:
  14.7 22.1 reduce-scatter.1
  210.9 21.9 all-gather.1
  358.4 32.9 all-reduce.5
  485.5 304.8 all-reduce.7
where the time goes:
time: 810 us; the launch traced here: 801 us
  waiting for transfers between devices  315 us (39%)
  other arithmetic  161 us (20%)
  blocking collectives  117 us (14%)
  local copies, waits for them, and re-layouts  102 us (13%)
  matrix products  69.4 us (9%)
  starting transfers between devices  20.7 us (3%)
  between operations  14.9 us (2%)
    psum x1, waiting for transfers between devices, shards(): grad_mix, grad_conv = lax.psum((grad_weight, taps_local), ('dp', 'seq'))  302 us
    unnamed x2, other arithmetic  149 us
    psum x1, blocking collectives, shards(): grad_mix, grad_conv = lax.psum((grad_weight, taps_local), ('dp', 'seq'))  98.7 us
    unnamed x46, local copies, waits for them, and re-layouts  54.3 us
    dot_general x18, matrix products, mat_right(): return jnp.einsum('ckm,mj->ckj', values, table, precision=HIGH)  38.3 us
    dot_general x18, matrix products, mat_left(): return jnp.einsum('kn,cnm->ckm', table, values, precision=HIGH)  22.5 us
  transfers between devices with their start and end apart: 9, of which 3 were waited for; matrix products, arithmetic and copies ran while one was open for 41% of the time, Pallas kernels for 0%

commit v1 on v0

v1 whole, which is shorter than its diff:
```python
import functools
import math

import jax
import jax.numpy as jnp
import ml_dtypes
import numpy as np
from jax import lax
from jax.experimental import pallas as pl
from jax.experimental.pallas import tpu as pltpu
from jax.sharding import PartitionSpec as P

SIDE = 128
LENGTH = SIDE * SIDE
F32 = jnp.float32
BF16 = jnp.bfloat16
GELU_SCALE = math.sqrt(2.0 / math.pi)
GELU_CUBE = 0.044715
VMEM = pl.BlockSpec(memory_space=pltpu.VMEM)
SMEM = pl.BlockSpec(memory_space=pltpu.SMEM)


def two_parts(table):
    high = table.astype(ml_dtypes.bfloat16)
    low = (table - high.astype(np.float64)).astype(ml_dtypes.bfloat16)
    return high, low


@functools.cache
def tables():
    one = np.arange(SIDE, dtype=np.float64)
    turn = 2.0 * np.pi * np.outer(one + 0.25, one) / SIDE
    rows = np.concatenate([np.cos(turn), -np.sin(turn)], axis=0)
    high, low = two_parts(rows)
    into_rows = np.concatenate([high, low, high], axis=1)
    high, low = two_parts(rows.T / LENGTH)
    back_rows = np.concatenate([high, low, high], axis=1)
    turn = 2.0 * np.pi * np.outer(one, one) / SIDE
    real, imag = np.cos(turn), -np.sin(turn)
    lanes = np.block([[real, imag], [-imag, real]])
    high, low = two_parts(lanes)
    into_lanes = np.concatenate([high, low, high], axis=0)
    high, low = two_parts(lanes.T)
    back_lanes = np.concatenate([high, low, high], axis=0)
    turn = 2.0 * np.pi * np.outer(one + 0.25, one) / LENGTH
    twist = np.stack([np.cos(turn), -np.sin(turn)]).astype(np.float32)
    return into_rows, into_lanes, back_rows, back_lanes, twist


def parts(value):
    high = value.astype(BF16)
    low = (value - high.astype(F32)).astype(BF16)
    return high, low


def dot(left, right, dims=((1,), (0,))):
    return lax.dot_general(left, right, (dims, ((), ())), preferred_element_type=F32)


def forward(pair, into_rows, into_lanes, twist):
    cos, sin = twist[0], twist[1]
    high, low = parts(jnp.concatenate(pair, axis=1))
    step = dot(into_rows[...], jnp.concatenate([high, high, low], axis=0))
    turned = []
    for at in range(len(pair)):
        real = step[:SIDE, at * SIDE : (at + 1) * SIDE]
        imag = step[SIDE:, at * SIDE : (at + 1) * SIDE]
        turned.append(jnp.concatenate([real * cos - imag * sin, real * sin + imag * cos], axis=1))
    high, low = parts(jnp.concatenate(turned, axis=0))
    return dot(jnp.concatenate([high, high, low], axis=1), into_lanes[...])


def backward(spectrum, back_rows, back_lanes, twist):
    cos, sin = twist[0], twist[1]
    count = spectrum.shape[0] // SIDE
    high, low = parts(spectrum)
    step = dot(jnp.concatenate([high, high, low], axis=1), back_lanes[...])
    turned = []
    for at in range(count):
        real = step[at * SIDE : (at + 1) * SIDE, :SIDE]
        imag = step[at * SIDE : (at + 1) * SIDE, SIDE:]
        turned.append(jnp.concatenate([real * cos + imag * sin, imag * cos - real * sin], axis=0))
    high, low = parts(jnp.concatenate(turned, axis=1))
    result = dot(back_rows[...], jnp.concatenate([high, high, low], axis=0))
    return [result[:, at * SIDE : (at + 1) * SIDE] for at in range(count)]


def times(left, right):
    lr, li, rr, ri = left[:, :SIDE], left[:, SIDE:], right[:, :SIDE], right[:, SIDE:]
    return jnp.concatenate([lr * rr - li * ri, lr * ri + li * rr], axis=1)


def times_conj(left, right):
    lr, li, rr, ri = left[:, :SIDE], left[:, SIDE:], right[:, :SIDE], right[:, SIDE:]
    return jnp.concatenate([lr * rr + li * ri, li * rr - lr * ri], axis=1)


def delayed(value, steps):
    row = lax.broadcasted_iota(jnp.int32, value.shape, 0)
    lane = lax.broadcasted_iota(jnp.int32, value.shape, 1)
    turned = pltpu.roll(value, steps, 1)
    above = jnp.where(row == 0, 0.0, pltpu.roll(turned, 1, 0))
    return jnp.where(lane < steps, above, turned)


def advanced(value, steps):
    row = lax.broadcasted_iota(jnp.int32, value.shape, 0)
    lane = lax.broadcasted_iota(jnp.int32, value.shape, 1)
    turned = pltpu.roll(value, SIDE - steps, 1)
    below = jnp.where(row == SIDE - 1, 0.0, pltpu.roll(turned, SIDE - 1, 0))
    return jnp.where(lane >= SIDE - steps, below, turned)


def blocks_kernel(signal, out):
    for at in range(8):
        out[pl.ds(at, 64, stride=8), :] = signal[:, at * SIDE : (at + 1) * SIDE]


def from_blocks(ref):
    return jnp.concatenate([ref[pl.ds(at, 64, stride=8), :] for at in range(8)], axis=1)


def spectrum_kernel(kernel, into_rows, into_lanes, twist, out, rows):
    for at in range(SIDE):
        rows[pl.ds(at, 4, stride=SIDE), :] = kernel[:, at * SIDE : (at + 1) * SIDE]
    for pair in range(2):
        both = [rows[(2 * pair + at) * SIDE : (2 * pair + at + 1) * SIDE, :] for at in range(2)]
        out[pair * 2 * SIDE : (pair + 1) * 2 * SIDE, :] = forward(both, into_rows, into_lanes, twist)


def grad_act_kernel(cot0, cot1, cot2, cot3, mix0, mix1, mix2, mix3, out, mix):
    for at, ref in enumerate((mix0, mix1, mix2, mix3)):
        mix[:, at * 64 : (at + 1) * 64] = ref[...]
    weight_high, weight_low = parts(mix[...])
    weights = jnp.concatenate([weight_high, weight_low, weight_high], axis=1)
    for at in range(8):
        high, low = parts(
            jnp.concatenate([ref[:, at * SIDE : (at + 1) * SIDE] for ref in (cot0, cot1, cot2, cot3)], axis=0)
        )
        out[pl.ds(at, 64, stride=8), :] = dot(weights, jnp.concatenate([high, high, low], axis=0))


def channel(ref, at):
    return ref[:, at * 8 : (at + 1) * 8, :].reshape(SIDE, SIDE)


def tapped(value, gains, at):
    return (
        gains[2, at] * value + gains[1, at] * delayed(value, 1) + gains[0, at] * delayed(value, 2)
    )


def forward_kernel(gains, signal, kernel_spec, into_rows, into_lanes, back_rows, back_lanes, twist, spec, long_conv, act):
    for pair in range(2):
        both = [channel(signal, 2 * pair + at) for at in range(2)]
        place = slice(pair * 2 * SIDE, (pair + 1) * 2 * SIDE)
        spectrum = forward(both, into_rows, into_lanes, twist)
        spec[place, :] = spectrum
        result = backward(times(spectrum, kernel_spec[place, :]), back_rows, back_lanes, twist)
        for at in range(2):
            index = 2 * pair + at
            whole = result[at] + gains[3, index] * both[at]
            long_conv[index] = whole
            value = tapped(whole, gains, index)
            inner = GELU_SCALE * (value + GELU_CUBE * value * value * value)
            active = 0.5 * value * (1.0 + jnp.tanh(inner))
            act[:, index * 8 : (index + 1) * 8, :] = active.reshape(16, 8, SIDE)


def backward_kernel(place_at, gains, grad_act, signal, spec, kernel_spec, long_conv, into_rows, into_lanes, back_rows, back_lanes, twist, grad_in, grad_kernel, small, rows):
    first = 4 * place_at[0]
    line = lax.broadcasted_iota(jnp.int32, (8, SIDE), 0)
    lane = lax.broadcasted_iota(jnp.int32, (8, SIDE), 1)
    sums = jnp.zeros((8, SIDE), F32)
    for pair in range(2):
        place = slice(pair * 2 * SIDE, (pair + 1) * 2 * SIDE)
        grads = []
        for at in range(2):
            index = 2 * pair + at
            whole = long_conv[index]
            later = [delayed(whole, 2), delayed(whole, 1), whole]
            value = sum(gains[tap, index] * later[tap] for tap in range(3))
            square = value * value
            tanh = jnp.tanh(GELU_SCALE * (value + GELU_CUBE * value * square))
            slope = 0.5 * (1.0 + tanh) + 0.5 * value * (1.0 - tanh * tanh) * (
                GELU_SCALE * (1.0 + 3.0 * GELU_CUBE * square)
            )
            grad = channel(grad_act, index) * slope
            for tap in range(3):
                here = (line == tap) & (lane == first + index)
                sums = sums + jnp.where(here, jnp.sum(grad * later[tap]), 0.0)
            grad = (
                gains[2, index] * grad
                + gains[1, index] * advanced(grad, 1)
                + gains[0, index] * advanced(grad, 2)
            )
            here = (line == 3) & (lane == index)
            sums = sums + jnp.where(here, jnp.sum(grad * channel(signal, index)), 0.0)
            grads.append(grad)
        spectrum = forward(grads, into_rows, into_lanes, twist)
        result = backward(times_conj(spectrum, kernel_spec[place, :]), back_rows, back_lanes, twist)
        for at in range(2):
            index = 2 * pair + at
            whole = result[at] + gains[3, index] * grads[at]
            grad_in[:, index * 8 : (index + 1) * 8, :] = whole.reshape(16, 8, SIDE)
        result = backward(times_conj(spectrum, spec[place, :]), back_rows, back_lanes, twist)
        for at in range(2):
            index = 2 * pair + at
            rows[index * SIDE : (index + 1) * SIDE, :] = result[at]
    for at in range(SIDE):
        grad_kernel[:, at * SIDE : (at + 1) * SIDE] = rows[pl.ds(at, 4, stride=SIDE), :]
    small[...] = sums


def grad_mix_kernel(act, cot0, cot1, cot2, cot3, out):
    high, low = parts(from_blocks(act))
    left = jnp.concatenate([high, high, low], axis=1)
    high, low = parts(jnp.concatenate([ref[...] for ref in (cot0, cot1, cot2, cot3)], axis=0))
    result = dot(left, jnp.concatenate([high, low, high], axis=1), ((1,), (1,)))
    for at in range(4):
        out[at, :, :64] = result[:32, at * 64 : (at + 1) * 64]
        out[at, :, 64:] = result[32:, at * 64 : (at + 1) * 64]


def outputs_kernel(place_at, signal, act0, act1, act2, act3, mix, out):
    me = place_at[1]
    high, low = parts(
        jnp.concatenate(
            [mix[pl.ds(pl.multiple_of(64 * jnp.bitwise_xor(me, at), 64), 64), :] for at in range(4)], axis=0
        )
    )
    weights = jnp.concatenate([high, low, high], axis=0)
    for at in range(8):
        high, low = parts(
            jnp.concatenate([ref[pl.ds(at, 64, stride=8), :] for ref in (act0, act1, act2, act3)], axis=0)
        )
        mixed = dot(weights, jnp.concatenate([high, high, low], axis=0), ((0,), (0,)))
        lanes = slice(at * SIDE, (at + 1) * SIDE)
        out[:, lanes] = signal[:, lanes] + mixed


def grad_inputs_kernel(cotangent, grad_in, out):
    for at in range(8):
        lanes = slice(at * SIDE, (at + 1) * SIDE)
        out[:, lanes] = cotangent[:, lanes] + grad_in[pl.ds(at, 64, stride=8), :]


def final_kernel(place_at, total0, total1, total2, total3, out):
    me = place_at[1]
    for at in range(4):
        whole = total0[at] + total1[at] + total2[at] + total3[at]
        start = pl.multiple_of(64 * jnp.bitwise_xor(me, at), 64)
        out[pl.ds(start, 32), :] = whole[:, :64]
        out[pl.ds(start + 32, 32), :] = whole[:, 64:]


def call(kernel, outs, *args, scalars=0, scratch=()):
    shapes = [jax.ShapeDtypeStruct(shape, F32) for shape in outs]
    return pl.pallas_call(
        kernel,
        out_shape=shapes if len(shapes) > 1 else shapes[0],
        in_specs=[SMEM] * scalars + [VMEM] * (len(args) - scalars),
        out_specs=[VMEM] * len(shapes) if len(shapes) > 1 else VMEM,
        scratch_shapes=[pltpu.VMEM(shape, F32) for shape in scratch],
        compiler_params=pltpu.CompilerParams(vmem_limit_bytes=48 * 1024 * 1024),
        name=kernel.__name__,
    )(*args)


def swapped(value, axes, flip):
    count = lax.axis_size(axes)
    return lax.ppermute(value, axes, [(at, at ^ flip) for at in range(count)])


def turned(value):
    return lax.all_to_all(value.reshape(16, 32, SIDE), "seq", 0, 0, tiled=True)


def shards(inputs, cotangent, conv_weight, kernel, skip_gain, mix_weight):
    signal = inputs[0]
    grad_out = cotangent[0]
    seq, chan = lax.axis_index("seq"), lax.axis_index("chan")
    place_at = jnp.stack([seq, chan]).astype(jnp.int32)
    gains = jnp.concatenate([lax.dynamic_slice(conv_weight, (0, 4 * seq), (3, 4)), skip_gain[None]], axis=0)
    into_rows, into_lanes, back_rows, back_lanes, twist = (jnp.asarray(table) for table in tables())

    signal_in = turned(call(blocks_kernel, [(512, SIDE)], signal))

    cot2 = swapped(grad_out, "chan", 2)
    cot1 = swapped(grad_out, "chan", 1)
    cot3 = swapped(cot2, "chan", 1)
    cots = (grad_out, cot1, cot2, cot3)
    mixes = []
    for flip in range(4):
        block = lax.dynamic_slice(mix_weight, (64 * jnp.bitwise_xor(chan, flip), 0), (64, 64))
        mixes.append(swapped(block, "chan", flip) if flip else block)
    grad_act = turned(call(grad_act_kernel, [(512, SIDE)], *cots, *mixes, scratch=[(64, 256)]))

    kernel_spec = call(
        spectrum_kernel, [(512, 256)], kernel, into_rows, into_lanes, twist, scratch=[(512, SIDE)]
    )
    spec, long_conv, act = call(
        forward_kernel,
        [(512, 256), (4, SIDE, SIDE), (16, 32, SIDE)],
        gains, signal_in, kernel_spec, into_rows, into_lanes, back_rows, back_lanes, twist,
        scalars=1,
    )
    act0 = turned(act).reshape(512, SIDE)
    grad_in, kernel_local, small = call(
        backward_kernel,
        [(16, 32, SIDE), (4, LENGTH), (8, SIDE)],
        place_at, gains, grad_act, signal_in, spec, kernel_spec, long_conv,
        into_rows, into_lanes, back_rows, back_lanes, twist,
        scalars=2, scratch=[(512, SIDE)],
    )
    grad_mixes = call(grad_mix_kernel, [(4, 32, SIDE)], act0, *cots)
    act2 = swapped(act0, "chan", 2)
    act1 = swapped(act0, "chan", 1)
    act3 = swapped(act2, "chan", 1)
    grad_conv_long = turned(grad_in).reshape(512, SIDE)

    grad_kernel = kernel_local + swapped(kernel_local, "dp", 1)
    sums = small + swapped(small, "dp", 1)
    grad_skip = sums[3, :4]

    blocks = [
        sum(swapped(grad_mixes[at], ("dp", "chan"), 4 * far + at) if far or at else grad_mixes[at] for far in range(2))
        for at in range(4)
    ]
    total = jnp.concatenate([jnp.stack(blocks), jnp.pad(sums, ((0, 24), (0, 0)))[None]], axis=0)
    total = total + swapped(total, "seq", 4) + swapped(total, "seq", 8) + swapped(total, "seq", 12)
    totals = [total] + [swapped(total, "seq", at) for at in (1, 2, 3)]
    grad_mix = call(final_kernel, [(256, 64)], place_at, *totals, scalars=1)
    grad_conv = sum(one[4, :3, :64] for one in totals)

    outputs = call(outputs_kernel, [(64, 1024)], place_at, signal, act0, act1, act2, act3, mix_weight, scalars=1)
    grad_inputs = call(grad_inputs_kernel, [(64, 1024)], grad_out, grad_conv_long)
    return (outputs[None], grad_inputs[None], grad_kernel, grad_skip, grad_mix, grad_conv)


def solution(mesh):
    placed = (
        P("dp", "chan", "seq"),
        P("dp", "chan", "seq"),
        P(None, "chan"),
        P(("chan", "seq"), None),
        P(("chan", "seq")),
        P(None, "chan"),
    )
    return jax.shard_map(
        shards,
        mesh=mesh,
        in_specs=placed,
        out_specs=(
            P("dp", "chan", "seq"),
            P("dp", "chan", "seq"),
            P(("chan", "seq"), None),
            P(("chan", "seq")),
            P(None, "chan"),
            P(None, "chan"),
        ),
        check_vma=False,
    )
```

time: 810 us -> 106 us (0.13)
  waiting for transfers between devices: 315 us -> 30.8 us
  other arithmetic: 161 us -> 5.75 us
  blocking collectives: 117 us -> 0 us
  local copies, waits for them, and re-layouts: 102 us -> 7.64 us
  matrix products: 69.4 us -> 0 us
  starting transfers between devices: 20.7 us -> 45.6 us
  between operations: 14.9 us -> 0.88 us
  Pallas kernels: 0 us -> 13.9 us
    psum x2 -> x0, waiting for transfers between devices: 302 us -> none  [the longest x1 302 us: shards(): grad_mix, grad_conv = lax.psum((grad_weight, taps_local), ('dp', 'seq'))]
    unnamed x2 -> x3, other arithmetic: 149 us -> 2.69 us
    psum x2 -> x0, blocking collectives: 106 us -> none  [the longest x1 98.7 us: shards(): grad_mix, grad_conv = lax.psum((grad_weight, taps_local), ('dp', 'seq'))]
    dot_general x39 -> x0, matrix products: 69.4 us -> none  [the longest x18 38.3 us: mat_right(): return jnp.einsum('ckm,mj->ckj', values, table, precision=HIGH)]
    unnamed x46 -> x38, local copies, waits for them, and re-layouts: 54.3 us -> 7.04 us
    broadcast_in_dim x4 -> x0, local copies, waits for them, and re-layouts: 26.2 us -> none  [the longest x1 12.1 us: shards(): long_out[None]]
    ppermute x2 -> x24, starting transfers between devices: 4.76 us -> 26.2 us  [swapped(): return lax.ppermute(value, axes, [(at, at ^ flip) for at in range(count)])]
    ppermute x2 -> x24, waiting for transfers between devices: 0.01 us -> 14.6 us  [swapped(): return lax.ppermute(value, axes, [(at, at ^ flip) for at in range(count)])]
  transfers between devices with their start and end apart: 9 -> 28, of which waited for: 3 -> 10; matrix products, arithmetic and copies ran while one was open for 41% -> 6% of each run, Pallas kernels for 0% -> 13%
where the time goes in v1:
time: 106 us; the launch traced here: 105 us
  starting transfers between devices  45.6 us (43%)
  waiting for transfers between devices  30.8 us (29%)
  Pallas kernels  13.9 us (13%)
  local copies, waits for them, and re-layouts  7.64 us (7%)
  other arithmetic  5.75 us (5%)
    ppermute x24, starting transfers between devices, swapped(): return lax.ppermute(value, axes, [(at, at ^ flip) for at in range(count)])  26.2 us
    all_to_all x4, starting transfers between devices, turned(): return lax.all_to_all(value.reshape(16, 32, SIDE), 'seq', 0, 0, tiled=True)  19.4 us
    all_to_all x4, waiting for transfers between devices, turned(): return lax.all_to_all(value.reshape(16, 32, SIDE), 'seq', 0, 0, tiled=True)  16.1 us
    ppermute x24, waiting for transfers between devices, swapped(): return lax.ppermute(value, axes, [(at, at ^ flip) for at in range(count)])  14.6 us
    pallas_call x9, Pallas kernels, call(): pl.pallas_call(kernel, out_shape=shapes if len(shapes) > 1 else shapes[0]...  13.9 us
    unnamed x38, local copies, waits for them, and re-layouts  7.04 us
    unnamed x3, other arithmetic  2.69 us
  transfers between devices with their start and end apart: 28, of which 10 were waited for; matrix products, arithmetic and copies ran while one was open for 6% of the time, Pallas kernels for 13%

profile of v1, /device:TPU:0, one launch (start us, length us, event | category | flops | bytes accessed | tf_op | source)
XLA Modules:
  0.0 104.5 jit_solution(7461173688874391692)
XLA Ops:
  0.6 1.7 %collective-permute-start.4 = (f32[64,1024]{1,0:T(8,128)}, f32[64,1024]{1,0:T(8,128)S(1)}, u32[]{:S(2)}, u32[]{:S(2)}) collective-permute-start(f32[64,1024]{1,0:T(8,128)} %bitcast.39), channel_id=1, source_target_pairs={{0,2},{1,3},{2,0},{3,1},{4,6},{5,7},{6,4},{7,5},{8,10},{9,11},{10,... | collective-permute-start | bytes 786440 | tf_op jit(solution)/shard_map/ppermute | solution.py:272
  2.4 0.9 copy-done.6
  3.3 0.8 blocks_kernel.1
  4.1 8.0 %all-to-all-start = ((f32[16,32,128]{2,1,0:T(8,128)}), f32[16,32,128]{2,1,0:T(8,128)S(1)}, u32[]{:S(2)}, u32[]{:S(2)}) async-start(f32[16,32,128]{2,1,0:T(8,128)} %bitcast.4), calls=%async_computation | async-start | bytes 524288 | tf_op jit(solution)/shard_map/all_to_all | solution.py:276
  12.3 0.5 collective-permute-start.5
  13.0 0.9 copy-done.15
  14.0 1.0 %spectrum_kernel.1.kernel_spec = f32[512,256]{1,0:T(8,128)S(1)} custom-call(f32[4,16384]{1,0:T(4,128)S(1)} %copy-done.15, bf16[256,384]{1,0:T(8,128)(2,1)S(1)} %copy-done.3, bf16[768,256]{1,0:T(8,128)(2,1)S(1)} %copy-done.1, f32[2,128,128]{2,1,0:T(8,128)S(1)} %copy-done.5), custom_call_target="tpu_custom_call" | custom-call | tf_op jit(solution)/shard_map/spectrum_kernel/pallas_call | solution.py:259
  15.0 5.8 %all-to-all-done.signal = f32[16,32,128]{2,1,0:T(8,128)S(1)} async-done(((f32[16,32,128]{2,1,0:T(8,128)}), f32[16,32,128]{2,1,0:T(8,128)S(1)}, u32[]{:S(2)}, u32[]{:S(2)}) %all-to-all-start) | async-done | bytes 262176 | tf_op jit(solution)/shard_map/all_to_all | solution.py:276
  20.8 2.7 %forward_kernel.1 = (f32[512,256]{1,0:T(8,128)S(1)}, f32[4,128,128]{2,1,0:T(8,128)S(1)}, f32[16,32,128]{2,1,0:T(8,128)S(1)}) custom-call(f32[4,4]{1,0:T(4,128)S(1)} %pad_maximum_fusion.gains, f32[16,32,128]{2,1,0:T(8,128)S(1)} %all-to-all-done.signal, f32[512,256]{1,0:T(8,128)S(1)} %spectrum_kernel.1.kernel_spec, bf16[256,384]{1,0:T(8,128)(2,1)S(1)} %copy-done.3, ...), custom_call_target="tpu_custom_call" | custom-call | tf_op jit(solution)/shard_map/forward_kernel/pallas_call | solution.py:259
  23.6 0.8 copy-done.9
  24.4 0.7 copy-done.11
  25.1 0.7 copy-done.14
  25.8 3.5 %all-to-all-start.1 = ((f32[16,32,128]{2,1,0:T(8,128)}), f32[16,32,128]{2,1,0:T(8,128)S(1)}, u32[]{:S(2)}, u32[]{:S(2)}) async-start(f32[16,32,128]{2,1,0:T(8,128)} %copy-done.14), calls=%async_computation.1 | async-start | bytes 524288 | tf_op jit(solution)/shard_map/all_to_all | solution.py:276
  29.3 0.9 copy.17.mix
  30.3 7.7 %all-to-all-done.1 = f32[16,32,128]{2,1,0:T(8,128)S(1)} async-done(((f32[16,32,128]{2,1,0:T(8,128)}), f32[16,32,128]{2,1,0:T(8,128)S(1)}, u32[]{:S(2)}, u32[]{:S(2)}) %all-to-all-start.1) | async-done | bytes 262176 | tf_op jit(solution)/shard_map/all_to_all | solution.py:276
  38.0 0.7 grad_mix_kernel.1
  38.6 3.0 %collective-permute-start.11 = (f32[32,128]{1,0:T(8,128)S(1)}, f32[32,128]{1,0:T(8,128)S(1)}, u32[]{:S(2)}, u32[]{:S(2)}) collective-permute-start(f32[32,128]{1,0:T(8,128)S(1)} %slice_bitcast_fusion.3), channel_id=1, source_target_pairs={{0,64},{1,65},{2,66},{3,67},{64,0},{65,1},{66,2},{67,3},{4,68},{5,... | collective-permute-start | bytes 49160 | tf_op jit(solution)/shard_map/ppermute | solution.py:272
  42.0 1.6 %collective-permute-start.8 = (f32[64,64]{1,0:T(8,128)S(1)}, f32[64,64]{1,0:T(8,128)S(1)}, u32[]{:S(2)}, u32[]{:S(2)}) collective-permute-start(f32[64,64]{1,0:T(8,128)S(1)} %get-tuple-element.24), channel_id=1, source_target_pairs={{0,3},{1,2},{2,1},{3,0},{4,7},{5,6},{6,5},{7,4},{8,11},{9,10},{10,... | collective-permute-start | bytes 49160 | tf_op jit(solution)/shard_map/ppermute | solution.py:272
  44.0 0.6 slice_bitcast_fusion
  44.6 3.2 %collective-permute-start.13 = (f32[32,128]{1,0:T(8,128)}, f32[32,128]{1,0:T(8,128)}, u32[]{:S(2)}, u32[]{:S(2)}) collective-permute-start(f32[32,128]{1,0:T(8,128)} %get-tuple-element.31), channel_id=1, source_target_pairs={{0,65},{1,64},{2,67},{3,66},{64,1},{65,0},{66,3},{67,2},{4,69},{5,... | collective-permute-start | bytes 49160 | tf_op jit(solution)/shard_map/ppermute | solution.py:272
  47.9 1.2 %grad_act_kernel.1 = f32[512,128]{1,0:T(8,128)} custom-call(f32[64,1024]{1,0:T(8,128)S(1)} %bitcast.42, f32[64,1024]{1,0:T(8,128)S(1)} %collective-permute-done.3.cot1, f32[64,1024]{1,0:T(8,128)S(1)} %collective-permute-done.4.cot2, f32[64,1024]{1,0:T(8,128)S(1)} %collective-permute-done.5.cot3, f32[64,64]{1,0:T(8,128)S(1)} %get-tuple-element.27.mix0, ...), custom_call_target="tpu_custom_call" | custom-call | tf_op jit(solution)/shard_map/grad_act_kernel/pallas_call | solution.py:259
  49.0 3.7 %all-to-all-start.2 = ((f32[16,32,128]{2,1,0:T(8,128)}), f32[16,32,128]{2,1,0:T(8,128)S(1)}, u32[]{:S(2)}, u32[]{:S(2)}) async-start(f32[16,32,128]{2,1,0:T(8,128)} %bitcast.8), calls=%async_computation.2 | async-start | bytes 524288 | tf_op jit(solution)/shard_map/all_to_all | solution.py:276
  52.8 1.0 collective-permute-start.15
  54.1 3.0 %collective-permute-start.17 = (f32[32,128]{1,0:T(8,128)}, f32[32,128]{1,0:T(8,128)}, u32[]{:S(2)}, u32[]{:S(2)}) collective-permute-start(f32[32,128]{1,0:T(8,128)} %get-tuple-element.28), channel_id=1, source_target_pairs={{0,67},{1,66},{2,65},{3,64},{64,3},{65,2},{66,1},{67,0},{4,71},{5,... | collective-permute-start | bytes 49160 | tf_op jit(solution)/shard_map/ppermute | solution.py:272
  57.2 1.3 %bitcast_dynamic-update-slice_fusion.3 = f32[5,32,128]{2,1,0:T(8,128)} fusion(f32[5,32,128]{2,1,0:T(8,128)} %get-tuple-element.29, f32[32,128]{1,0:T(8,128)} %collective-permute-done.12, f32[32,128]{1,0:T(8,128)} %collective-permute-done.13), kind=kLoop, calls=%fused_computation.8 | loop fusion | flops 4096 | bytes 49152
  58.5 0.6 bitcast_dynamic-update-slice_fusion.2
  59.1 2.7 %all-to-all-done.2.grad_act = f32[16,32,128]{2,1,0:T(8,128)S(1)} async-done(((f32[16,32,128]{2,1,0:T(8,128)}), f32[16,32,128]{2,1,0:T(8,128)S(1)}, u32[]{:S(2)}, u32[]{:S(2)}) %all-to-all-start.2) | async-done | bytes 262176 | tf_op jit(solution)/shard_map/all_to_all | solution.py:276
  61.8 0.9 copy-done.12
  62.7 4.4 %backward_kernel.1 = (f32[16,32,128]{2,1,0:T(8,128)S(1)}, f32[4,16384]{1,0:T(4,128)}, f32[8,128]{1,0:T(8,128)S(1)}) custom-call(s32[2]{0:T(128)S(1)} %pad_add_fusion.place_at, f32[4,4]{1,0:T(4,128)S(1)} %pad_maximum_fusion.gains, f32[16,32,128]{2,1,0:T(8,128)S(1)} %all-to-all-done.2.grad_act, f32[16,32,128]{2,1,0:T(8,128)S(1)} %all-to-all-done.signal, ...), custom_call_target="tpu_custom_call" | custom-call | tf_op jit(solution)/shard_map/backward_kernel/pallas_call | solution.py:259
  67.6 0.7 bitcast_dynamic-update-slice_fusion.1
  68.4 3.9 %collective-permute-done.10 = f32[8,128]{1,0:T(8,128)S(1)} collective-permute-done((f32[8,128]{1,0:T(8,128)S(1)}, f32[8,128]{1,0:T(8,128)S(1)}, u32[]{:S(2)}, u32[]{:S(2)}) %collective-permute-start.10) | collective-permute-done | bytes 4128 | tf_op jit(solution)/shard_map/ppermute | solution.py:272
  72.3 2.2 %collective-permute-start.19 = (f32[5,32,128]{2,1,0:T(8,128)S(1)}, f32[5,32,128]{2,1,0:T(8,128)S(1)}, u32[]{:S(2)}, u32[]{:S(2)}) collective-permute-start(f32[5,32,128]{2,1,0:T(8,128)S(1)} %bitcast_dynamic-update-slice_fusion), channel_id=1, source_target_pairs={{0,32},{4,36},{8,40},{12,44},{16,48},{20,52},{24,56},{28,60},{32,0... | collective-permute-start | bytes 245768 | tf_op jit(solution)/shard_map/ppermute | solution.py:272
  74.6 2.4 %collective-permute-start.20 = (f32[5,32,128]{2,1,0:T(8,128)S(1)}, f32[5,32,128]{2,1,0:T(8,128)S(1)}, u32[]{:S(2)}, u32[]{:S(2)}) collective-permute-start(f32[5,32,128]{2,1,0:T(8,128)S(1)} %bitcast_dynamic-update-slice_fusion), channel_id=1, source_target_pairs={{0,48},{4,52},{8,56},{12,60},{16,32},{20,36},{24,40},{28,44},{32,1... | collective-permute-start | bytes 245768 | tf_op jit(solution)/shard_map/ppermute | solution.py:272
  77.0 1.3 %collective-permute-done.19 = f32[5,32,128]{2,1,0:T(8,128)S(1)} collective-permute-done((f32[5,32,128]{2,1,0:T(8,128)S(1)}, f32[5,32,128]{2,1,0:T(8,128)S(1)}, u32[]{:S(2)}, u32[]{:S(2)}) %collective-permute-start.19) | collective-permute-done | bytes 81952 | tf_op jit(solution)/shard_map/ppermute | solution.py:272
  78.3 1.9 %collective-permute-done.20 = f32[5,32,128]{2,1,0:T(8,128)S(1)} collective-permute-done((f32[5,32,128]{2,1,0:T(8,128)S(1)}, f32[5,32,128]{2,1,0:T(8,128)S(1)}, u32[]{:S(2)}, u32[]{:S(2)}) %collective-permute-start.20) | collective-permute-done | bytes 81952 | tf_op jit(solution)/shard_map/ppermute | solution.py:272
  80.3 1.1 %collective-permute-start.21 = (f32[5,32,128]{2,1,0:T(8,128)S(1)}, f32[5,32,128]{2,1,0:T(8,128)S(1)}, u32[]{:S(2)}, u32[]{:S(2)}) collective-permute-start(f32[5,32,128]{2,1,0:T(8,128)S(1)} %add_add_fusion.total0), channel_id=1, source_target_pairs={{0,4},{4,0},{8,12},{12,8},{16,20},{20,16},{24,28},{28,24},{32,36},... | collective-permute-start | bytes 245768 | tf_op jit(solution)/shard_map/ppermute | solution.py:272
  81.3 2.0 %collective-permute-done.1.act2 = f32[512,128]{1,0:T(8,128)S(1)} collective-permute-done((f32[512,128]{1,0:T(8,128)S(1)}, f32[512,128]{1,0:T(8,128)S(1)}, u32[]{:S(2)}, u32[]{:S(2)}) %collective-permute-start.1) | collective-permute-done | bytes 262176 | tf_op jit(solution)/shard_map/ppermute | solution.py:272
  83.8 4.1 %all-to-all-start.3 = ((f32[16,32,128]{2,1,0:T(8,128)}), f32[16,32,128]{2,1,0:T(8,128)S(1)}, u32[]{:S(2)}, u32[]{:S(2)}) async-start(f32[16,32,128]{2,1,0:T(8,128)} %copy-done.13), calls=%async_computation.3 | async-start | bytes 524288 | tf_op jit(solution)/shard_map/all_to_all | solution.py:276
  88.0 3.4 %collective-permute-start.22 = (f32[5,32,128]{2,1,0:T(8,128)S(1)}, f32[5,32,128]{2,1,0:T(8,128)S(1)}, u32[]{:S(2)}, u32[]{:S(2)}) collective-permute-start(f32[5,32,128]{2,1,0:T(8,128)S(1)} %add_add_fusion.total0), channel_id=1, source_target_pairs={{0,8},{4,12},{8,0},{12,4},{16,24},{20,28},{24,16},{28,20},{32,40},... | collective-permute-start | bytes 245768 | tf_op jit(solution)/shard_map/ppermute | solution.py:272
  91.4 1.2 %collective-permute-start.23 = (f32[5,32,128]{2,1,0:T(8,128)S(1)}, f32[5,32,128]{2,1,0:T(8,128)S(1)}, u32[]{:S(2)}, u32[]{:S(2)}) collective-permute-start(f32[5,32,128]{2,1,0:T(8,128)S(1)} %add_add_fusion.total0), channel_id=1, source_target_pairs={{0,12},{4,8},{8,4},{12,0},{16,28},{20,24},{24,20},{28,16},{32,44},... | collective-permute-start | bytes 245768 | tf_op jit(solution)/shard_map/ppermute | solution.py:272
  93.1 3.7 %collective-permute-done.22.total2 = f32[5,32,128]{2,1,0:T(8,128)S(1)} collective-permute-done((f32[5,32,128]{2,1,0:T(8,128)S(1)}, f32[5,32,128]{2,1,0:T(8,128)S(1)}, u32[]{:S(2)}, u32[]{:S(2)}) %collective-permute-start.22) | collective-permute-done | bytes 81952 | tf_op jit(solution)/shard_map/ppermute | solution.py:272
  96.7 1.4 %collective-permute-done.23.total3 = f32[5,32,128]{2,1,0:T(8,128)S(1)} collective-permute-done((f32[5,32,128]{2,1,0:T(8,128)S(1)}, f32[5,32,128]{2,1,0:T(8,128)S(1)}, u32[]{:S(2)}, u32[]{:S(2)}) %collective-permute-start.23) | collective-permute-done | bytes 81952 | tf_op jit(solution)/shard_map/ppermute | solution.py:272
  98.1 0.6 final_kernel.1
  98.8 0.7 copy.22
  99.5 0.6 fusion
  100.1 0.8 grad_inputs_kernel.1
  101.0 1.8 %outputs_kernel.1 = f32[64,1024]{1,0:T(8,128)} custom-call(s32[2]{0:T(128)S(1)} %pad_add_fusion.place_at, f32[64,1024]{1,0:T(8,128)S(1)} %bitcast.45, f32[512,128]{1,0:T(8,128)S(1)} %bitcast.38, f32[512,128]{1,0:T(8,128)S(1)} %collective-permute-done.act1, f32[512,128]{1,0:T(8,128)S(1)} %collective-permute-done.1.act2, ...), custom_call_target="tpu_custom_call" | custom-call | tf_op jit(solution)/shard_map/outputs_kernel/pallas_call | solution.py:259
  102.8 1.7 %add.63 = f32[4,16384]{1,0:T(4,128)} add(f32[4,16384]{1,0:T(4,128)} %get-tuple-element.16, f32[4,16384]{1,0:T(4,128)S(1)} %collective-permute-done.9) | non-fusion elementwise | flops 65536 | bytes 786432 | tf_op jit(solution)/shard_map/add | solution.py:322
  (70 shorter events, 3.3 us)
Async XLA Ops:
  0.6 11.6 %copy-start = (f32[3,64]{1,0:T(4,128)S(1)}, f32[3,64]{1,0:T(4,128)}, u32[]{:S(2)}) copy-start(f32[3,64]{1,0:T(4,128)} %param.13) | copy-start | bytes 2308
  0.6 11.7 %collective-permute-start.4 = (f32[64,1024]{1,0:T(8,128)}, f32[64,1024]{1,0:T(8,128)S(1)}, u32[]{:S(2)}, u32[]{:S(2)}) collective-permute-start(f32[64,1024]{1,0:T(8,128)} %bitcast.39), channel_id=1, source_target_pairs={{0,2},{1,3},{2,0},{3,1},{4,6},{5,7},{6,4},{7,5},{8,10},{9,11},{10,... | collective-permute-start | bytes 786440 | tf_op jit(solution)/shard_map/ppermute | solution.py:272
  2.4 0.9 copy-start.6
  3.3 8.8 %copy-start.2 = (f32[1,64,1024]{2,1,0:T(8,128)S(1)}, f32[1,64,1024]{2,1,0:T(8,128)}, u32[]{:S(2)}) copy-start(f32[1,64,1024]{2,1,0:T(8,128)} %param.12) | copy-start | bytes 786436
  3.3 9.6 %copy-start.3 = (bf16[256,384]{1,0:T(8,128)(2,1)S(1)}, bf16[256,384]{1,0:T(8,128)(2,1)}, u32[]{:S(2)}) copy-start(bf16[256,384]{1,0:T(8,128)(2,1)} %constant.35.clone.into_rows) | copy-start | bytes 589828
  4.1 8.9 %copy-start.1 = (bf16[768,256]{1,0:T(8,128)(2,1)S(1)}, bf16[768,256]{1,0:T(8,128)(2,1)}, u32[]{:S(2)}) copy-start(bf16[768,256]{1,0:T(8,128)(2,1)} %constant.36.clone.into_lanes) | copy-start | bytes 1179652
  4.1 8.9 %copy-start.5 = (f32[2,128,128]{2,1,0:T(8,128)S(1)}, f32[2,128,128]{2,1,0:T(8,128)}, u32[]{:S(2)}) copy-start(f32[2,128,128]{2,1,0:T(8,128)} %constant.39.clone.twist) | copy-start | bytes 393220
  4.1 16.7 %all-to-all-start = ((f32[16,32,128]{2,1,0:T(8,128)}), f32[16,32,128]{2,1,0:T(8,128)S(1)}, u32[]{:S(2)}, u32[]{:S(2)}) async-start(f32[16,32,128]{2,1,0:T(8,128)} %bitcast.4), calls=%async_computation | async-start | bytes 524288 | tf_op jit(solution)/shard_map/all_to_all | solution.py:276
  12.1 18.1 %collective-permute-start.3 = (f32[64,1024]{1,0:T(8,128)S(1)}, f32[64,1024]{1,0:T(8,128)S(1)}, u32[]{:S(2)}, u32[]{:S(2)}) collective-permute-start(f32[64,1024]{1,0:T(8,128)S(1)} %bitcast.40), channel_id=1, source_target_pairs={{0,1},{1,0},{2,3},{3,2},{4,5},{5,4},{6,7},{7,6},{8,9},{9,8},{10,11... | collective-permute-start | bytes 786440 | tf_op jit(solution)/shard_map/ppermute | solution.py:272
  12.3 0.7 copy-start.17
  12.3 25.6 %collective-permute-start.5 = (f32[64,1024]{1,0:T(8,128)S(1)}, f32[64,1024]{1,0:T(8,128)S(1)}, u32[]{:S(2)}, u32[]{:S(2)}) collective-permute-start(f32[64,1024]{1,0:T(8,128)S(1)} %collective-permute-done.4.cot2), channel_id=1, source_target_pairs={{0,1},{1,0},{2,3},{3,2},{4,5},{5,4},{6,7},{7,6},{8,9},{9,8},{10,11... | collective-permute-start | bytes 786440 | tf_op jit(solution)/shard_map/ppermute | solution.py:272
  13.0 1.0 copy-start.15
  14.0 6.9 %copy-start.4 = (bf16[768,256]{1,0:T(8,128)(2,1)S(1)}, bf16[768,256]{1,0:T(8,128)(2,1)}, u32[]{:S(2)}) copy-start(bf16[768,256]{1,0:T(8,128)(2,1)} %constant.38.clone.back_lanes) | copy-start | bytes 1179652
  14.0 6.9 %copy-start.8 = (bf16[128,768]{1,0:T(8,128)(2,1)S(1)}, bf16[128,768]{1,0:T(8,128)(2,1)}, u32[]{:S(2)}) copy-start(bf16[128,768]{1,0:T(8,128)(2,1)} %constant.37.clone.back_rows) | copy-start | bytes 589828
  23.6 0.8 copy-start.9
  24.4 0.7 copy-start.11
  25.1 0.7 copy-start.14
  25.8 12.2 %all-to-all-start.1 = ((f32[16,32,128]{2,1,0:T(8,128)}), f32[16,32,128]{2,1,0:T(8,128)S(1)}, u32[]{:S(2)}, u32[]{:S(2)}) async-start(f32[16,32,128]{2,1,0:T(8,128)} %copy-done.14), calls=%async_computation.1 | async-start | bytes 524288 | tf_op jit(solution)/shard_map/all_to_all | solution.py:276
  38.6 5.3 %collective-permute-start.11 = (f32[32,128]{1,0:T(8,128)S(1)}, f32[32,128]{1,0:T(8,128)S(1)}, u32[]{:S(2)}, u32[]{:S(2)}) collective-permute-start(f32[32,128]{1,0:T(8,128)S(1)} %slice_bitcast_fusion.3), channel_id=1, source_target_pairs={{0,64},{1,65},{2,66},{3,67},{64,0},{65,1},{66,2},{67,3},{4,68},{5,... | collective-permute-start | bytes 49160 | tf_op jit(solution)/shard_map/ppermute | solution.py:272
  41.6 6.2 %collective-permute-start.6 = (f32[64,64]{1,0:T(8,128)S(1)}, f32[64,64]{1,0:T(8,128)S(1)}, u32[]{:S(2)}, u32[]{:S(2)}) collective-permute-start(f32[64,64]{1,0:T(8,128)S(1)} %get-tuple-element.26), channel_id=1, source_target_pairs={{0,1},{1,0},{2,3},{3,2},{4,5},{5,4},{6,7},{7,6},{8,9},{9,8},{10,11... | collective-permute-start | bytes 49160 | tf_op jit(solution)/shard_map/ppermute | solution.py:272
  41.7 6.1 %collective-permute-start.7 = (f32[64,64]{1,0:T(8,128)S(1)}, f32[64,64]{1,0:T(8,128)S(1)}, u32[]{:S(2)}, u32[]{:S(2)}) collective-permute-start(f32[64,64]{1,0:T(8,128)S(1)} %get-tuple-element.25), channel_id=1, source_target_pairs={{0,2},{1,3},{2,0},{3,1},{4,6},{5,7},{6,4},{7,5},{8,10},{9,11},{10,... | collective-permute-start | bytes 49160 | tf_op jit(solution)/shard_map/ppermute | solution.py:272
  42.0 5.9 %collective-permute-start.8 = (f32[64,64]{1,0:T(8,128)S(1)}, f32[64,64]{1,0:T(8,128)S(1)}, u32[]{:S(2)}, u32[]{:S(2)}) collective-permute-start(f32[64,64]{1,0:T(8,128)S(1)} %get-tuple-element.24), channel_id=1, source_target_pairs={{0,3},{1,2},{2,1},{3,0},{4,7},{5,6},{6,5},{7,4},{8,11},{9,10},{10,... | collective-permute-start | bytes 49160 | tf_op jit(solution)/shard_map/ppermute | solution.py:272
  44.6 9.5 %collective-permute-start.12 = (f32[32,128]{1,0:T(8,128)}, f32[32,128]{1,0:T(8,128)}, u32[]{:S(2)}, u32[]{:S(2)}) collective-permute-start(f32[32,128]{1,0:T(8,128)} %get-tuple-element.31), channel_id=1, source_target_pairs={{0,1},{1,0},{2,3},{3,2},{64,65},{65,64},{66,67},{67,66},{4,5},{5,4... | collective-permute-start | bytes 49160 | tf_op jit(solution)/shard_map/ppermute | solution.py:272
  44.6 12.6 %collective-permute-start.13 = (f32[32,128]{1,0:T(8,128)}, f32[32,128]{1,0:T(8,128)}, u32[]{:S(2)}, u32[]{:S(2)}) collective-permute-start(f32[32,128]{1,0:T(8,128)} %get-tuple-element.31), channel_id=1, source_target_pairs={{0,65},{1,64},{2,67},{3,66},{64,1},{65,0},{66,3},{67,2},{4,69},{5,... | collective-permute-start | bytes 49160 | tf_op jit(solution)/shard_map/ppermute | solution.py:272
  49.0 12.8 %copy-start.10 = (f32[512,256]{1,0:T(8,128)S(1)}, f32[512,256]{1,0:T(8,128)}, u32[]{:S(2)}) copy-start(f32[512,256]{1,0:T(8,128)} %copy-done.9) | copy-start | bytes 1572868
  49.0 12.8 %all-to-all-start.2 = ((f32[16,32,128]{2,1,0:T(8,128)}), f32[16,32,128]{2,1,0:T(8,128)S(1)}, u32[]{:S(2)}, u32[]{:S(2)}) async-start(f32[16,32,128]{2,1,0:T(8,128)} %bitcast.8), calls=%async_computation.2 | async-start | bytes 524288 | tf_op jit(solution)/shard_map/all_to_all | solution.py:276
  52.7 5.8 %collective-permute-start.14 = (f32[32,128]{1,0:T(8,128)}, f32[32,128]{1,0:T(8,128)S(1)}, u32[]{:S(2)}, u32[]{:S(2)}) collective-permute-start(f32[32,128]{1,0:T(8,128)} %get-tuple-element.30), channel_id=1, source_target_pairs={{0,2},{1,3},{2,0},{3,1},{64,66},{65,67},{66,64},{67,65},{4,6},{5,7... | collective-permute-start | bytes 49160 | tf_op jit(solution)/shard_map/ppermute | solution.py:272
  52.8 5.7 %collective-permute-start.15 = (f32[32,128]{1,0:T(8,128)}, f32[32,128]{1,0:T(8,128)S(1)}, u32[]{:S(2)}, u32[]{:S(2)}) collective-permute-start(f32[32,128]{1,0:T(8,128)} %get-tuple-element.30), channel_id=1, source_target_pairs={{0,66},{1,67},{2,64},{3,65},{64,2},{65,3},{66,0},{67,1},{4,70},{5,... | collective-permute-start | bytes 49160 | tf_op jit(solution)/shard_map/ppermute | solution.py:272
  53.8 13.8 %collective-permute-start.16 = (f32[32,128]{1,0:T(8,128)}, f32[32,128]{1,0:T(8,128)}, u32[]{:S(2)}, u32[]{:S(2)}) collective-permute-start(f32[32,128]{1,0:T(8,128)} %get-tuple-element.28), channel_id=1, source_target_pairs={{0,3},{1,2},{2,1},{3,0},{64,67},{65,66},{66,65},{67,64},{4,7},{5,6... | collective-permute-start | bytes 49160 | tf_op jit(solution)/shard_map/ppermute | solution.py:272
  54.1 13.5 %collective-permute-start.17 = (f32[32,128]{1,0:T(8,128)}, f32[32,128]{1,0:T(8,128)}, u32[]{:S(2)}, u32[]{:S(2)}) collective-permute-start(f32[32,128]{1,0:T(8,128)} %get-tuple-element.28), channel_id=1, source_target_pairs={{0,67},{1,66},{2,65},{3,64},{64,3},{65,2},{66,1},{67,0},{4,71},{5,... | collective-permute-start | bytes 49160 | tf_op jit(solution)/shard_map/ppermute | solution.py:272
  61.8 1.0 copy-start.12
  62.7 4.9 %copy-start.16 = (f32[5,32,128]{2,1,0:T(8,128)S(1)}, f32[5,32,128]{2,1,0:T(8,128)}, u32[]{:S(2)}) copy-start(f32[5,32,128]{2,1,0:T(8,128)} %bitcast_dynamic-update-slice_fusion.2) | copy-start | bytes 245764
  67.2 16.7 %copy-start.13 = (f32[16,32,128]{2,1,0:T(8,128)}, f32[16,32,128]{2,1,0:T(8,128)S(1)}, u32[]{:S(2)}) copy-start(f32[16,32,128]{2,1,0:T(8,128)S(1)} %get-tuple-element.15) | copy-start | bytes 786436
  67.2 5.1 %collective-permute-start.10 = (f32[8,128]{1,0:T(8,128)S(1)}, f32[8,128]{1,0:T(8,128)S(1)}, u32[]{:S(2)}, u32[]{:S(2)}) collective-permute-start(f32[8,128]{1,0:T(8,128)S(1)} %get-tuple-element.17), channel_id=1, source_target_pairs={{0,64},{64,0},{1,65},{65,1},{2,66},{66,2},{3,67},{67,3},{4,68},{68... | collective-permute-start | bytes 12296 | tf_op jit(solution)/shard_map/ppermute | solution.py:272
  72.3 4.7 %collective-permute-start.18 = (f32[5,32,128]{2,1,0:T(8,128)S(1)}, f32[5,32,128]{2,1,0:T(8,128)S(1)}, u32[]{:S(2)}, u32[]{:S(2)}) collective-permute-start(f32[5,32,128]{2,1,0:T(8,128)S(1)} %bitcast_dynamic-update-slice_fusion), channel_id=1, source_target_pairs={{0,16},{4,20},{8,24},{12,28},{16,0},{20,4},{24,8},{28,12},{32,48},... | collective-permute-start | bytes 245768 | tf_op jit(solution)/shard_map/ppermute | solution.py:272
  72.3 6.0 %collective-permute-start.19 = (f32[5,32,128]{2,1,0:T(8,128)S(1)}, f32[5,32,128]{2,1,0:T(8,128)S(1)}, u32[]{:S(2)}, u32[]{:S(2)}) collective-permute-start(f32[5,32,128]{2,1,0:T(8,128)S(1)} %bitcast_dynamic-update-slice_fusion), channel_id=1, source_target_pairs={{0,32},{4,36},{8,40},{12,44},{16,48},{20,52},{24,56},{28,60},{32,0... | collective-permute-start | bytes 245768 | tf_op jit(solution)/shard_map/ppermute | solution.py:272
  74.6 5.7 %collective-permute-start.20 = (f32[5,32,128]{2,1,0:T(8,128)S(1)}, f32[5,32,128]{2,1,0:T(8,128)S(1)}, u32[]{:S(2)}, u32[]{:S(2)}) collective-permute-start(f32[5,32,128]{2,1,0:T(8,128)S(1)} %bitcast_dynamic-update-slice_fusion), channel_id=1, source_target_pairs={{0,48},{4,52},{8,56},{12,60},{16,32},{20,36},{24,40},{28,44},{32,1... | collective-permute-start | bytes 245768 | tf_op jit(solution)/shard_map/ppermute | solution.py:272
  77.0 6.4 %collective-permute-start.1 = (f32[512,128]{1,0:T(8,128)S(1)}, f32[512,128]{1,0:T(8,128)S(1)}, u32[]{:S(2)}, u32[]{:S(2)}) collective-permute-start(f32[512,128]{1,0:T(8,128)S(1)} %bitcast.36), channel_id=1, source_target_pairs={{0,2},{1,3},{2,0},{3,1},{4,6},{5,7},{6,4},{7,5},{8,10},{9,11},{10,... | collective-permute-start | bytes 786440 | tf_op jit(solution)/shard_map/ppermute | solution.py:272
  80.3 11.2 %collective-permute-start.21 = (f32[5,32,128]{2,1,0:T(8,128)S(1)}, f32[5,32,128]{2,1,0:T(8,128)S(1)}, u32[]{:S(2)}, u32[]{:S(2)}) collective-permute-start(f32[5,32,128]{2,1,0:T(8,128)S(1)} %add_add_fusion.total0), channel_id=1, source_target_pairs={{0,4},{4,0},{8,12},{12,8},{16,20},{20,16},{24,28},{28,24},{32,36},... | collective-permute-start | bytes 245768 | tf_op jit(solution)/shard_map/ppermute | solution.py:272
  81.3 19.5 %collective-permute-start = (f32[512,128]{1,0:T(8,128)S(1)}, f32[512,128]{1,0:T(8,128)S(1)}, u32[]{:S(2)}, u32[]{:S(2)}) collective-permute-start(f32[512,128]{1,0:T(8,128)S(1)} %bitcast.37), channel_id=1, source_target_pairs={{0,1},{1,0},{2,3},{3,2},{4,5},{5,4},{6,7},{7,6},{8,9},{9,8},{10,11... | collective-permute-start | bytes 786440 | tf_op jit(solution)/shard_map/ppermute | solution.py:272
  83.4 17.5 %collective-permute-start.2 = (f32[512,128]{1,0:T(8,128)S(1)}, f32[512,128]{1,0:T(8,128)S(1)}, u32[]{:S(2)}, u32[]{:S(2)}) collective-permute-start(f32[512,128]{1,0:T(8,128)S(1)} %collective-permute-done.1.act2), channel_id=1, source_target_pairs={{0,1},{1,0},{2,3},{3,2},{4,5},{5,4},{6,7},{7,6},{8,9},{9,8},{10,11... | collective-permute-start | bytes 786440 | tf_op jit(solution)/shard_map/ppermute | solution.py:272
  83.4 19.4 %collective-permute-start.9 = (f32[4,16384]{1,0:T(4,128)}, f32[4,16384]{1,0:T(4,128)S(1)}, u32[]{:S(2)}, u32[]{:S(2)}) collective-permute-start(f32[4,16384]{1,0:T(4,128)} %get-tuple-element.16), channel_id=1, source_target_pairs={{0,64},{64,0},{1,65},{65,1},{2,66},{66,2},{3,67},{67,3},{4,68},{68... | collective-permute-start | bytes 786440 | tf_op jit(solution)/shard_map/ppermute | solution.py:272
  83.8 16.3 %all-to-all-start.3 = ((f32[16,32,128]{2,1,0:T(8,128)}), f32[16,32,128]{2,1,0:T(8,128)S(1)}, u32[]{:S(2)}, u32[]{:S(2)}) async-start(f32[16,32,128]{2,1,0:T(8,128)} %copy-done.13), calls=%async_computation.3 | async-start | bytes 524288 | tf_op jit(solution)/shard_map/all_to_all | solution.py:276
  88.0 8.8 %collective-permute-start.22 = (f32[5,32,128]{2,1,0:T(8,128)S(1)}, f32[5,32,128]{2,1,0:T(8,128)S(1)}, u32[]{:S(2)}, u32[]{:S(2)}) collective-permute-start(f32[5,32,128]{2,1,0:T(8,128)S(1)} %add_add_fusion.total0), channel_id=1, source_target_pairs={{0,8},{4,12},{8,0},{12,4},{16,24},{20,28},{24,16},{28,20},{32,40},... | collective-permute-start | bytes 245768 | tf_op jit(solution)/shard_map/ppermute | solution.py:272
  91.4 6.7 %collective-permute-start.23 = (f32[5,32,128]{2,1,0:T(8,128)S(1)}, f32[5,32,128]{2,1,0:T(8,128)S(1)}, u32[]{:S(2)}, u32[]{:S(2)}) collective-permute-start(f32[5,32,128]{2,1,0:T(8,128)S(1)} %add_add_fusion.total0), channel_id=1, source_target_pairs={{0,12},{4,8},{8,4},{12,0},{16,28},{20,24},{24,20},{28,16},{32,44},... | collective-permute-start | bytes 245768 | tf_op jit(solution)/shard_map/ppermute | solution.py:272
  100.1 1.0 copy-start.7

commit v2 on v1

v2 whole, which is shorter than its diff:
```python
import functools
import math

import jax
import jax.numpy as jnp
import ml_dtypes
import numpy as np
from jax import lax
from jax.experimental import pallas as pl
from jax.experimental.pallas import tpu as pltpu
from jax.sharding import PartitionSpec as P

SIDE = 128
LENGTH = SIDE * SIDE
F32 = jnp.float32
BF16 = jnp.bfloat16
GELU_SCALE = math.sqrt(2.0 / math.pi)
GELU_CUBE = 0.044715
VMEM = pl.BlockSpec(memory_space=pltpu.VMEM)
SMEM = pl.BlockSpec(memory_space=pltpu.SMEM)
HBM = pl.BlockSpec(memory_space=pltpu.HBM)


def two_parts(table):
    high = table.astype(ml_dtypes.bfloat16)
    low = (table - high.astype(np.float64)).astype(ml_dtypes.bfloat16)
    return high, low


@functools.cache
def tables():
    one = np.arange(SIDE, dtype=np.float64)
    turn = 2.0 * np.pi * np.outer(one + 0.25, one) / SIDE
    rows = np.concatenate([np.cos(turn), -np.sin(turn)], axis=0)
    high, low = two_parts(rows)
    into_rows = np.concatenate([high, low, high], axis=1)
    high, low = two_parts(rows.T / LENGTH)
    back_rows = np.concatenate([high, low, high], axis=1)
    turn = 2.0 * np.pi * np.outer(one, one) / SIDE
    real, imag = np.cos(turn), -np.sin(turn)
    lanes = np.block([[real, imag], [-imag, real]])
    high, low = two_parts(lanes)
    into_lanes = np.concatenate([high, low, high], axis=0)
    high, low = two_parts(lanes.T)
    back_lanes = np.concatenate([high, low, high], axis=0)
    turn = 2.0 * np.pi * np.outer(one + 0.25, one) / LENGTH
    twist = np.stack([np.cos(turn), -np.sin(turn)]).astype(np.float32)
    return into_rows, into_lanes, back_rows, back_lanes, twist


def parts(value):
    high = value.astype(BF16)
    low = (value - high.astype(F32)).astype(BF16)
    return high, low


def dot(left, right, dims=((1,), (0,))):
    return lax.dot_general(left, right, (dims, ((), ())), preferred_element_type=F32)


def forward(pair, into_rows, into_lanes, twist):
    cos, sin = twist[0], twist[1]
    high, low = parts(jnp.concatenate(pair, axis=1))
    step = dot(into_rows[...], jnp.concatenate([high, high, low], axis=0))
    turned = []
    for at in range(len(pair)):
        real = step[:SIDE, at * SIDE : (at + 1) * SIDE]
        imag = step[SIDE:, at * SIDE : (at + 1) * SIDE]
        turned.append(jnp.concatenate([real * cos - imag * sin, real * sin + imag * cos], axis=1))
    high, low = parts(jnp.concatenate(turned, axis=0))
    return dot(jnp.concatenate([high, high, low], axis=1), into_lanes[...])


def backward(spectrum, back_rows, back_lanes, twist):
    cos, sin = twist[0], twist[1]
    count = spectrum.shape[0] // SIDE
    high, low = parts(spectrum)
    step = dot(jnp.concatenate([high, high, low], axis=1), back_lanes[...])
    turned = []
    for at in range(count):
        real = step[at * SIDE : (at + 1) * SIDE, :SIDE]
        imag = step[at * SIDE : (at + 1) * SIDE, SIDE:]
        turned.append(jnp.concatenate([real * cos + imag * sin, imag * cos - real * sin], axis=0))
    high, low = parts(jnp.concatenate(turned, axis=1))
    result = dot(back_rows[...], jnp.concatenate([high, high, low], axis=0))
    return [result[:, at * SIDE : (at + 1) * SIDE] for at in range(count)]


def times(left, right):
    lr, li, rr, ri = left[:, :SIDE], left[:, SIDE:], right[:, :SIDE], right[:, SIDE:]
    return jnp.concatenate([lr * rr - li * ri, lr * ri + li * rr], axis=1)


def times_conj(left, right):
    lr, li, rr, ri = left[:, :SIDE], left[:, SIDE:], right[:, :SIDE], right[:, SIDE:]
    return jnp.concatenate([lr * rr + li * ri, li * rr - lr * ri], axis=1)


def delayed(value, steps):
    row = lax.broadcasted_iota(jnp.int32, value.shape, 0)
    lane = lax.broadcasted_iota(jnp.int32, value.shape, 1)
    turned = pltpu.roll(value, steps, 1)
    above = jnp.where(row == 0, 0.0, pltpu.roll(turned, 1, 0))
    return jnp.where(lane < steps, above, turned)


def advanced(value, steps):
    row = lax.broadcasted_iota(jnp.int32, value.shape, 0)
    lane = lax.broadcasted_iota(jnp.int32, value.shape, 1)
    turned = pltpu.roll(value, SIDE - steps, 1)
    below = jnp.where(row == SIDE - 1, 0.0, pltpu.roll(turned, SIDE - 1, 0))
    return jnp.where(lane >= SIDE - steps, below, turned)


def blocks_kernel(signal, out):
    for at in range(8):
        out[pl.ds(at, 64, stride=8), :] = signal[:, at * SIDE : (at + 1) * SIDE]


def from_blocks(ref):
    return jnp.concatenate([ref[pl.ds(at, 64, stride=8), :] for at in range(8)], axis=1)


def spectrum_kernel(kernel, into_rows, into_lanes, twist, out, rows):
    for at in range(SIDE):
        rows[pl.ds(at, 4, stride=SIDE), :] = kernel[:, at * SIDE : (at + 1) * SIDE]
    for pair in range(2):
        both = [rows[(2 * pair + at) * SIDE : (2 * pair + at + 1) * SIDE, :] for at in range(2)]
        out[pair * 2 * SIDE : (pair + 1) * 2 * SIDE, :] = forward(both, into_rows, into_lanes, twist)


def mix_pair(place_at, mix, mix_far):
    chan = place_at[1]
    start = pl.multiple_of(128 * lax.shift_right_logical(chan, 1), 128)
    both = jnp.concatenate([mix[:, pl.ds(start, 128)], mix_far[...]], axis=0)
    return pltpu.roll(both, 64 * jnp.bitwise_and(chan, 1), 1)


def grad_act_kernel(place_at, cot, cot_far, mix, mix_far, own, other):
    weight_high, weight_low = parts(mix_pair(place_at, mix, mix_far).T)
    weights = jnp.concatenate([weight_high, weight_low, weight_high], axis=1)
    for at in range(8):
        lanes = slice(at * SIDE, (at + 1) * SIDE)
        high, low = parts(jnp.concatenate([cot[:, lanes], cot_far[:, lanes]], axis=0))
        result = dot(weights, jnp.concatenate([high, high, low], axis=0))
        own[pl.ds(at, 64, stride=8), :] = result[:64]
        other[pl.ds(at, 64, stride=8), :] = result[64:]


def channel(ref, at):
    return ref[:, at * 8 : (at + 1) * 8, :].reshape(SIDE, SIDE)


def gains_of(place_at, taps, at):
    index = 4 * place_at[0] + at
    return taps[0, index], taps[1, index], taps[2, index]


def moved(copies):
    for one in copies:
        one.start()
    return copies


def forward_kernel(
    place_at, taps, skip, signal, kernel_spec, into_rows, into_lanes, back_rows, back_lanes, twist,
    spec, long_conv, act_out, act, sems,
):
    copies = []
    for pair in range(2):
        both = [channel(signal, 2 * pair + at) for at in range(2)]
        place = slice(pair * 2 * SIDE, (pair + 1) * 2 * SIDE)
        spectrum = forward(both, into_rows, into_lanes, twist)
        spec[place, :] = spectrum
        result = backward(times(spectrum, kernel_spec[place, :]), back_rows, back_lanes, twist)
        for at in range(2):
            index = 2 * pair + at
            gains = gains_of(place_at, taps, index)
            whole = result[at] + skip[index] * both[at]
            long_conv[index] = whole
            value = gains[2] * whole + gains[1] * delayed(whole, 1) + gains[0] * delayed(whole, 2)
            inner = GELU_SCALE * (value + GELU_CUBE * value * value * value)
            active = 0.5 * value * (1.0 + jnp.tanh(inner))
            act[:, index * 8 : (index + 1) * 8, :] = active.reshape(16, 8, SIDE)
        rows = pl.ds(pair * 16, 16)
        copies += moved([pltpu.make_async_copy(act.at[:, rows, :], act_out.at[:, rows, :], sems.at[pair])])
    for one in copies:
        one.wait()


def join_kernel(act, own, near, out, total, sem):
    total[...] = (own[...] + near[...]).reshape(16, 32, SIDE)
    copy = pltpu.make_async_copy(total, out.at[:, pl.ds(32, 32), :], sem)
    copy.start()
    copy.wait()


def slope_kernel(place_at, taps, grad_act, signal, long_conv, grads, small):
    first = 4 * place_at[0]
    line = lax.broadcasted_iota(jnp.int32, (8, SIDE), 0)
    lane = lax.broadcasted_iota(jnp.int32, (8, SIDE), 1)
    sums = jnp.zeros((8, SIDE), F32)
    for index in range(4):
        gains = gains_of(place_at, taps, index)
        whole = long_conv[index]
        later = [delayed(whole, 2), delayed(whole, 1), whole]
        value = gains[2] * whole + gains[1] * later[1] + gains[0] * later[0]
        square = value * value
        tanh = jnp.tanh(GELU_SCALE * (value + GELU_CUBE * value * square))
        slope = 0.5 * (1.0 + tanh) + 0.5 * value * (1.0 - tanh * tanh) * (
            GELU_SCALE * (1.0 + 3.0 * GELU_CUBE * square)
        )
        grad = channel(grad_act, 4 + index) * slope
        for tap in range(3):
            here = (line == tap) & (lane == first + index)
            sums = sums + jnp.where(here, jnp.sum(grad * later[tap]), 0.0)
        grad = gains[2] * grad + gains[1] * advanced(grad, 1) + gains[0] * advanced(grad, 2)
        here = (line == 3) & (lane == index)
        sums = sums + jnp.where(here, jnp.sum(grad * channel(signal, index)), 0.0)
        grads[index] = grad
    small[...] = sums


def backward_kernel(
    skip, grads, spec, kernel_spec, into_rows, into_lanes, back_rows, back_lanes, twist,
    grad_out, kernel_out, grad_in, rows, sems,
):
    copies = []
    for pair in range(2):
        place = slice(pair * 2 * SIDE, (pair + 1) * 2 * SIDE)
        both = [grads[2 * pair + at] for at in range(2)]
        spectrum = forward(both, into_rows, into_lanes, twist)
        result = backward(times_conj(spectrum, kernel_spec[place, :]), back_rows, back_lanes, twist)
        for at in range(2):
            index = 2 * pair + at
            whole = result[at] + skip[index] * both[at]
            grad_in[:, index * 8 : (index + 1) * 8, :] = whole.reshape(16, 8, SIDE)
        lines = pl.ds(pair * 16, 16)
        copies += moved([pltpu.make_async_copy(grad_in.at[:, lines, :], grad_out.at[:, lines, :], sems.at[pair])])
        result = backward(times_conj(spectrum, spec[place, :]), back_rows, back_lanes, twist)
        for at in range(2):
            index = 2 * pair + at
            rows[index * SIDE : (index + 1) * SIDE, :] = result[at]
    for at in range(SIDE):
        kernel_out[:, at * SIDE : (at + 1) * SIDE] = rows[pl.ds(at, 4, stride=SIDE), :]
    for one in copies:
        one.wait()


def tail_kernel(place_at, act, act_near, cot, cot_far, signal, mix, mix_far, small, mine, theirs, out, out_far):
    active = jnp.concatenate([from_blocks(act), from_blocks(act_near)], axis=0)
    act_high, act_low = parts(active)
    high, low = parts(jnp.concatenate([cot[...], cot_far[...]], axis=0))
    result = dot(
        jnp.concatenate([high, low, high], axis=1),
        jnp.concatenate([act_high, act_high, act_low], axis=1),
        ((1,), (1,)),
    )
    mine[:64, :] = result[:64]
    mine[64:, :] = small[...]
    theirs[...] = result[64:]
    high, low = parts(mix_pair(place_at, mix, mix_far))
    mixed = dot(
        jnp.concatenate([high, low, high], axis=1),
        jnp.concatenate([act_high, act_high, act_low], axis=0),
    )
    out[...] = signal[...] + mixed[:64]
    out_far[...] = mixed[64:]


def merge_kernel(mine, mine_far, theirs, theirs_far, out):
    out[:64, :] = mine[:64, :] + mine_far[:64, :]
    out[64:128, :] = theirs[...] + theirs_far[...]
    out[128:, :] = mine[64:, :] + mine_far[64:, :]


def grad_inputs_kernel(cotangent, grad_in, out):
    for at in range(8):
        lanes = slice(at * SIDE, (at + 1) * SIDE)
        out[:, lanes] = cotangent[:, lanes] + grad_in[pl.ds(at, 64, stride=8), :]


def final_kernel(place_at, total0, total1, total2, total3, out, taps):
    chan = place_at[1]
    whole = total0[...] + total1[...] + total2[...] + total3[...]
    turn = 64 * jnp.bitwise_and(chan, 1)
    start = 128 * lax.shift_right_logical(chan, 1)
    out[:, pl.ds(pl.multiple_of(start, 128), 128)] = pltpu.roll(whole[:64], turn, 1)
    out[:, pl.ds(pl.multiple_of(128 - start, 128), 128)] = pltpu.roll(whole[64:128], turn, 1)
    taps[...] = whole[128:131, :64]


def call(kernel, outs, *args, scalars=0, far=(), far_outs=(), scratch=(), after=(), aliases=()):
    shapes = [jax.ShapeDtypeStruct(shape, F32) for shape in outs]
    count = len(args)

    def body(*refs):
        kernel(*refs[:count], *refs[count + len(after) :])

    ins = [SMEM if at < scalars else HBM if at in far else VMEM for at in range(count)]
    places = [HBM if at in far_outs else VMEM for at in range(len(outs))]
    return pl.pallas_call(
        body,
        out_shape=shapes if len(shapes) > 1 else shapes[0],
        in_specs=ins + [pl.BlockSpec(memory_space=pl.ANY)] * len(after),
        out_specs=places if len(shapes) > 1 else places[0],
        scratch_shapes=[shape if not isinstance(shape, tuple) else pltpu.VMEM(shape, F32) for shape in scratch],
        compiler_params=pltpu.CompilerParams(vmem_limit_bytes=20 * 1024 * 1024),
        input_output_aliases=dict(aliases),
        name=kernel.__name__,
    )(*args, *after)


def swapped(value, axes, flip):
    count = lax.axis_size(axes)
    return lax.ppermute(value, axes, [(at, at ^ flip) for at in range(count)])


def turned(value):
    return lax.all_to_all(value, "seq", 0, 0, tiled=True)


def shards(inputs, cotangent, conv_weight, kernel, skip_gain, mix_weight):
    signal = inputs[0]
    grad_out = cotangent[0]
    seq, chan = lax.axis_index("seq"), lax.axis_index("chan")
    place_at = jnp.stack([seq, chan]).astype(jnp.int32)
    into_rows, into_lanes, back_rows, back_lanes, twist = (jnp.asarray(table) for table in tables())
    mix = mix_weight.T

    cot_far = swapped(grad_out, "chan", 2)
    far = jnp.bitwise_xor(lax.shift_right_logical(chan, 1), 1)
    mix_far = swapped(lax.dynamic_slice(mix, (0, 128 * far), (64, 128)), "chan", 2)
    signal_blocks = call(blocks_kernel, [(512, SIDE)], signal)
    signal_in = turned(signal_blocks.reshape(16, 32, SIDE))
    kernel_spec = call(
        spectrum_kernel, [(512, 256)], kernel, into_rows, into_lanes, twist,
        scratch=[(512, SIDE)], after=[signal_blocks],
    )
    grad_own, grad_other = call(
        grad_act_kernel, [(512, SIDE)] * 2, place_at, grad_out, cot_far, mix, mix_far,
        scalars=1, after=[kernel_spec, signal_in],
    )
    grad_near = swapped(grad_other, "chan", 1)
    spec, long_conv, act = call(
        forward_kernel,
        [(512, 256), (4, SIDE, SIDE), (16, 64, SIDE)],
        place_at, conv_weight, skip_gain, signal_in, kernel_spec,
        into_rows, into_lanes, back_rows, back_lanes, twist,
        scalars=3, far_outs=(2,), after=[grad_own],
        scratch=[(16, 32, SIDE), pltpu.SemaphoreType.DMA((2,))],
    )
    act = call(
        join_kernel, [(16, 64, SIDE)], act, grad_own, grad_near,
        far=(0,), far_outs=(0,), aliases={0: 0}, scratch=[(16, 32, SIDE), pltpu.SemaphoreType.DMA],
    )
    act_in = turned(act)
    act_own = act_in[:, :32].reshape(512, SIDE)
    act_near = swapped(act_own, "chan", 1)
    grads, small = call(
        slope_kernel, [(4, SIDE, SIDE), (8, SIDE)], place_at, conv_weight, act_in, signal_in, long_conv, scalars=2
    )
    mine, theirs, out_own, out_far = call(
        tail_kernel,
        [(72, SIDE), (64, SIDE), (64, 1024), (64, 1024)],
        place_at, act_own, act_near, grad_out, cot_far, signal, mix, mix_far, small,
        scalars=1,
    )
    grad_long, kernel_local = call(
        backward_kernel,
        [(16, 32, SIDE), (4, LENGTH)],
        skip_gain, grads, spec, kernel_spec, into_rows, into_lanes, back_rows, back_lanes, twist,
        scalars=1, far_outs=(0,), after=[mine],
        scratch=[(16, 32, SIDE), (512, SIDE), pltpu.SemaphoreType.DMA((2,))],
    )
    both = ("dp", "chan")
    total = call(
        merge_kernel, [(136, SIDE)], mine, swapped(mine, both, 4), swapped(theirs, both, 2), swapped(theirs, both, 6),
        after=[kernel_local],
    )
    grad_skip = total[131, :4]
    outputs = out_own + swapped(out_far, "chan", 2)
    grad_in = turned(grad_long).reshape(512, SIDE)
    grad_inputs = call(grad_inputs_kernel, [(64, 1024)], grad_out, grad_in)
    grad_kernel = kernel_local + swapped(kernel_local, "dp", 1)
    total = total + swapped(total, "seq", 4) + swapped(total, "seq", 8) + swapped(total, "seq", 12)
    grad_mix, grad_conv = call(
        final_kernel, [(64, 256), (3, 64)], place_at, total, *(swapped(total, "seq", at) for at in (1, 2, 3)),
        scalars=1, after=[grad_inputs, grad_kernel, outputs],
    )
    return (outputs[None], grad_inputs[None], grad_kernel, grad_skip, grad_mix.T, grad_conv)


def solution(mesh):
    placed = (
        P("dp", "chan", "seq"),
        P("dp", "chan", "seq"),
        P(None, "chan"),
        P(("chan", "seq"), None),
        P(("chan", "seq")),
        P(None, "chan"),
    )
    return jax.shard_map(
        shards,
        mesh=mesh,
        in_specs=placed,
        out_specs=(
            P("dp", "chan", "seq"),
            P("dp", "chan", "seq"),
            P(("chan", "seq"), None),
            P(("chan", "seq")),
            P(None, "chan"),
            P(None, "chan"),
        ),
        check_vma=False,
    )
```

time: 106 us -> 75.7 us (0.71); the launches traced: 105 us -> 75.3 us
  waiting for transfers between devices: 30.8 us -> 13 us
  starting transfers between devices: 45.6 us -> 29.3 us
  blocking collectives: 0 us -> 14.5 us
  other arithmetic: 5.75 us -> 0.2 us
  local copies, waits for them, and re-layouts: 7.64 us -> 3.15 us
    all_to_all x0 -> x1, blocking collectives: none -> 14.5 us  [turned(): return lax.all_to_all(value, 'seq', 0, 0, tiled=True)]
    ppermute x24 -> x15, waiting for transfers between devices: 14.6 us -> 3.24 us  [swapped(): return lax.ppermute(value, axes, [(at, at ^ flip) for at in range(count)])]
    ppermute x24 -> x15, starting transfers between devices: 26.2 us -> 17.7 us  [swapped(): return lax.ppermute(value, axes, [(at, at ^ flip) for at in range(count)])]
    all_to_all x4 -> x2, starting transfers between devices: 19.4 us -> 11.5 us  [turned(): return lax.all_to_all(value, 'seq', 0, 0, tiled=True)]
    all_to_all x4 -> x2, waiting for transfers between devices: 16.1 us -> 9.71 us  [turned(): return lax.all_to_all(value, 'seq', 0, 0, tiled=True)]
    unnamed x38 -> x30, local copies, waits for them, and re-layouts: 7.04 us -> 2.61 us
    unnamed x3 -> x0, other arithmetic: 2.69 us -> none
    add x1, other arithmetic: 1.74 us -> 0.07 us  [shards(): grad_kernel = kernel_local + swapped(kernel_local, 'dp', 1)]
  transfers between devices with their start and end apart: 28 -> 17, of which waited for: 10 -> 4; matrix products, arithmetic and copies ran while one was open for 6% -> 1% of each run, Pallas kernels for 13% -> 14%
where the time goes in v2:
time: 75.7 us; the launch traced here: 75.3 us
  starting transfers between devices  29.3 us (39%)
  blocking collectives  14.5 us (19%)
  Pallas kernels  14.2 us (19%)
  waiting for transfers between devices  13 us (17%)
  local copies, waits for them, and re-layouts  3.15 us (4%)
  between operations  0.94 us (1%)
    ppermute x15, starting transfers between devices, swapped(): return lax.ppermute(value, axes, [(at, at ^ flip) for at in range(count)])  17.7 us
    all_to_all x1, blocking collectives, turned(): return lax.all_to_all(value, 'seq', 0, 0, tiled=True)  14.5 us
    pallas_call x11, Pallas kernels, call(): pl.pallas_call(body, out_shape=shapes if len(shapes) > 1 else shapes[0],...  14.2 us
    all_to_all x2, starting transfers between devices, turned(): return lax.all_to_all(value, 'seq', 0, 0, tiled=True)  11.5 us
    all_to_all x2, waiting for transfers between devices, turned(): return lax.all_to_all(value, 'seq', 0, 0, tiled=True)  9.71 us
    ppermute x15, waiting for transfers between devices, swapped(): return lax.ppermute(value, axes, [(at, at ^ flip) for at in range(count)])  3.24 us
    unnamed x30, local copies, waits for them, and re-layouts  2.61 us
  transfers between devices with their start and end apart: 17, of which 4 were waited for; matrix products, arithmetic and copies ran while one was open for 1% of the time, Pallas kernels for 14%

profile of v2, /device:TPU:0, one launch (start us, length us, event | category | flops | bytes accessed | tf_op | source)
XLA Modules:
  0.0 75.3 jit_solution(999393931512200209)
XLA Ops:
  0.6 1.7 %collective-permute-start = (f32[64,1024]{1,0:T(8,128)}, f32[64,1024]{1,0:T(8,128)S(1)}, u32[]{:S(2)}, u32[]{:S(2)}) collective-permute-start(f32[64,1024]{1,0:T(8,128)} %bitcast.15), channel_id=1, source_target_pairs={{0,2},{1,3},{2,0},{3,1},{4,6},{5,7},{6,4},{7,5},{8,10},{9,11},{10,... | collective-permute-start | bytes 786440 | tf_op jit(solution)/shard_map/ppermute | solution.py:316
  2.4 0.9 %copy-done.5 = f32[1,64,1024]{2,1,0:T(8,128)S(1)} copy-done((f32[1,64,1024]{2,1,0:T(8,128)S(1)}, f32[1,64,1024]{2,1,0:T(8,128)}, u32[]{:S(2)}) %copy-start.5) | copy-done | bytes 262168
  3.3 0.8 %blocks_kernel.1.refs_4_ = f32[512,128]{1,0:T(8,128)} custom-call(f32[64,1024]{1,0:T(8,128)S(1)} %bitcast.19), custom_call_target="tpu_custom_call" | custom-call | tf_op jit(solution)/shard_map/blocks_kernel/pallas_call | solution.py:302
  4.1 8.0 %all-to-all-start = ((f32[16,32,128]{2,1,0:T(8,128)}), f32[16,32,128]{2,1,0:T(8,128)S(1)}, u32[]{:S(2)}, u32[]{:S(2)}) async-start(f32[16,32,128]{2,1,0:T(8,128)} %bitcast.3), calls=%async_computation | async-start | bytes 524288 | tf_op jit(solution)/shard_map/all_to_all | solution.py:320
  12.1 0.5 collective-permute-start.1
  12.7 0.1 pad_add_fusion.refs_0_
  12.8 0.0 copy-start.1
  12.8 1.0 %spectrum_kernel.1.refs_5_.refs_4_.refs_3_ = f32[512,256]{1,0:T(8,128)S(1)} custom-call(f32[4,16384]{1,0:T(4,128)S(1)} %copy-done.12, bf16[256,384]{1,0:T(8,128)(2,1)S(1)} %copy-done.2, bf16[768,256]{1,0:T(8,128)(2,1)S(1)} %copy-done, f32[2,128,128]{2,1,0:T(8,128)S(1)} %copy-done.4, f32[512,128]{1,0:T(8,128)} %blocks_kernel.1.refs_4_), custom_call_target="tpu_custom_call" | custom-call | tf_op jit(solution)/shard_map/spectrum_kernel/pallas_call | solution.py:302
  13.8 2.3 %collective-permute-done.1.refs_4_.refs_7_ = f32[64,128]{1,0:T(8,128)S(1)} collective-permute-done((f32[64,128]{1,0:T(8,128)S(1)}, f32[64,128]{1,0:T(8,128)S(1)}, u32[]{:S(2)}, u32[]{:S(2)}) %collective-permute-start.1) | collective-permute-done | bytes 32800 | tf_op jit(solution)/shard_map/ppermute | solution.py:316
  16.1 4.7 %all-to-all-done.refs_6_.refs_3_ = f32[16,32,128]{2,1,0:T(8,128)S(1)} async-done(((f32[16,32,128]{2,1,0:T(8,128)}), f32[16,32,128]{2,1,0:T(8,128)S(1)}, u32[]{:S(2)}, u32[]{:S(2)}) %all-to-all-start) | async-done | bytes 262176 | tf_op jit(solution)/shard_map/all_to_all | solution.py:320
  20.8 0.0 copy-start.10
  20.8 1.0 %grad_act_kernel.1 = (f32[512,128]{1,0:T(8,128)S(1)}, f32[512,128]{1,0:T(8,128)S(1)}) custom-call(s32[2]{0:T(128)S(1)} %pad_add_fusion.refs_0_, f32[64,1024]{1,0:T(8,128)S(1)} %bitcast.16, f32[64,1024]{1,0:T(8,128)S(1)} %collective-permute-done.refs_2_.refs_4_, f32[64,256]{1,0:T(8,128)S(1)} %bitcast.26, ...), custom_call_target="tpu_custom_call" | custom-call | tf_op jit(solution)/shard_map/grad_act_kernel/pallas_call | solution.py:302
  21.9 0.0 copy-start.13
  21.9 0.0 copy-start.14
  21.9 0.1 collective-permute-start.2
  22.0 0.5 copy-done.13
  22.6 3.1 %forward_kernel.1 = (f32[512,256]{1,0:T(8,128)S(1)}, f32[4,128,128]{2,1,0:T(8,128)S(1)}, f32[16,64,128]{2,1,0:T(8,128)S(1)}) custom-call(s32[2]{0:T(128)S(1)} %pad_add_fusion.refs_0_, f32[3,64]{1,0:T(4,128)S(1)} %copy-done.13, f32[4]{0:T(128)S(1)} %copy-done.14, f32[16,32,128]{2,1,0:T(8,128)S(1)} %all-to-all-done.refs_6_.refs_3_, ...), custom_call_target="tpu_custom_call" | custom-call | tf_op jit(solution)/shard_map/forward_kernel/pallas_call | solution.py:302
  25.6 0.1 join_kernel.1
  25.7 14.5 %all_to_all.15.refs_2_ = f32[16,64,128]{2,1,0:T(8,128)S(1)} all-to-all(f32[16,64,128]{2,1,0:T(8,128)S(1)} %join_kernel.1), channel_id=1, replica_groups=mesh['dp'=2,'seq'=16,'chan'=4] {'seq'}, dimensions={0} | all-to-all | bytes 1048576 | tf_op jit(solution)/shard_map/all_to_all | solution.py:320
  40.3 0.1 collective-permute-start.3
  40.4 0.0 copy-start.6
  40.4 1.5 %slope_kernel.1 = (f32[4,128,128]{2,1,0:T(8,128)S(1)}, f32[8,128]{1,0:T(8,128)S(1)}) custom-call(s32[2]{0:T(128)S(1)} %pad_add_fusion.refs_0_, f32[3,64]{1,0:T(4,128)S(1)} %copy-done.13, f32[16,64,128]{2,1,0:T(8,128)S(1)} %all_to_all.15.refs_2_, f32[16,32,128]{2,1,0:T(8,128)S(1)} %all-to-all-done.refs_6_.refs_3_, f32[4,128,128]{2,1,0:T(8,128)S(1)} %get-tuple-element.24.refs_4_), custom_call_target="tpu_custom_call" | custom-call | tf_op jit(solution)/shard_map/slope_kernel/pallas_call | solution.py:302
  41.9 0.0 collective-permute-done.3.refs_2_
  41.9 1.1 %tail_kernel.1 = (f32[72,128]{1,0:T(8,128)S(1)}, f32[64,128]{1,0:T(8,128)S(1)}, f32[64,1024]{1,0:T(8,128)S(1)}, f32[64,1024]{1,0:T(8,128)S(1)}) custom-call(s32[2]{0:T(128)S(1)} %pad_add_fusion.refs_0_, f32[512,128]{1,0:T(8,128)S(1)} %bitcast.23, f32[512,128]{1,0:T(8,128)S(1)} %collective-permute-done.3.refs_2_, f32[64,1024]{1,0:T(8,128)S(1)} %bitcast.17, ...), custom_call_target="tpu_custom_call" | custom-call | tf_op jit(solution)/shard_map/tail_kernel/pallas_call | solution.py:302
  43.0 3.0 %collective-permute-start.6 = (f32[72,128]{1,0:T(8,128)S(1)}, f32[72,128]{1,0:T(8,128)S(1)}, u32[]{:S(2)}, u32[]{:S(2)}) collective-permute-start(f32[72,128]{1,0:T(8,128)S(1)} %get-tuple-element.30.refs_9_.refs_0_), channel_id=1, source_target_pairs={{0,64},{1,65},{2,66},{3,67},{64,0},{65,1},{66,2},{67,3},{4,68},{5,... | collective-permute-start | bytes 110600 | tf_op jit(solution)/shard_map/ppermute | solution.py:316
  46.0 0.2 collective-permute-start.8
  46.2 0.4 collective-permute-start.7
  46.6 3.7 %backward_kernel.1 = (f32[16,32,128]{2,1,0:T(8,128)}, f32[4,16384]{1,0:T(4,128)S(1)}) custom-call(f32[4]{0:T(128)S(1)} %copy-done.14, f32[4,128,128]{2,1,0:T(8,128)S(1)} %get-tuple-element.28.refs_1_, f32[512,256]{1,0:T(8,128)S(1)} %get-tuple-element.29.refs_2_, f32[512,256]{1,0:T(8,128)S(1)} %spectrum_kernel.1.refs_5_.refs_4_.refs_3_, ...), custom_call_target="tpu_custom_call" | custom-call | tf_op jit(solution)/shard_map/backward_kernel/pallas_call | solution.py:302
  50.3 0.8 %collective-permute-done.8.refs_3_ = f32[64,128]{1,0:T(8,128)S(1)} collective-permute-done((f32[64,128]{1,0:T(8,128)S(1)}, f32[64,128]{1,0:T(8,128)S(1)}, u32[]{:S(2)}, u32[]{:S(2)}) %collective-permute-start.8) | collective-permute-done | bytes 32800 | tf_op jit(solution)/shard_map/ppermute | solution.py:316
  51.1 0.9 %collective-permute-start.11 = (f32[136,128]{1,0:T(8,128)S(1)}, f32[136,128]{1,0:T(8,128)S(1)}, u32[]{:S(2)}, u32[]{:S(2)}) collective-permute-start(f32[136,128]{1,0:T(8,128)S(1)} %merge_kernel.1), channel_id=1, source_target_pairs={{0,48},{4,52},{8,56},{12,60},{16,32},{20,36},{24,40},{28,44},{32,1... | collective-permute-start | bytes 208904 | tf_op jit(solution)/shard_map/ppermute | solution.py:316
  52.1 0.6 collective-permute-start.10
  52.6 2.7 %collective-permute-start.9 = (f32[136,128]{1,0:T(8,128)S(1)}, f32[136,128]{1,0:T(8,128)S(1)}, u32[]{:S(2)}, u32[]{:S(2)}) collective-permute-start(f32[136,128]{1,0:T(8,128)S(1)} %merge_kernel.1), channel_id=1, source_target_pairs={{0,16},{4,20},{8,24},{12,28},{16,0},{20,4},{24,8},{28,12},{32,48},... | collective-permute-start | bytes 208904 | tf_op jit(solution)/shard_map/ppermute | solution.py:316
  55.3 3.3 %collective-permute-start.5 = (f32[4,16384]{1,0:T(4,128)S(1)}, f32[4,16384]{1,0:T(4,128)S(1)}, u32[]{:S(2)}, u32[]{:S(2)}) collective-permute-start(f32[4,16384]{1,0:T(4,128)S(1)} %get-tuple-element.32.refs_4_), channel_id=1, source_target_pairs={{0,64},{64,0},{1,65},{65,1},{2,66},{66,2},{3,67},{67,3},{4,68},{68... | collective-permute-start | bytes 786440 | tf_op jit(solution)/shard_map/ppermute | solution.py:316
  58.6 3.5 %all-to-all-start.2 = ((f32[16,32,128]{2,1,0:T(8,128)}), f32[16,32,128]{2,1,0:T(8,128)S(1)}, u32[]{:S(2)}, u32[]{:S(2)}) async-start(f32[16,32,128]{2,1,0:T(8,128)} %get-tuple-element.31), calls=%async_computation.2 | async-start | bytes 524288 | tf_op jit(solution)/shard_map/all_to_all | solution.py:320
  62.1 0.1 collective-permute-start.4
  62.3 3.0 %collective-permute-start.14 = (f32[136,128]{1,0:T(8,128)S(1)}, f32[136,128]{1,0:T(8,128)S(1)}, u32[]{:S(2)}, u32[]{:S(2)}) collective-permute-start(f32[136,128]{1,0:T(8,128)S(1)} %add_add_fusion.refs_1_), channel_id=1, source_target_pairs={{0,12},{4,8},{8,4},{12,0},{16,28},{20,24},{24,20},{28,16},{32,44},... | collective-permute-start | bytes 208904 | tf_op jit(solution)/shard_map/ppermute | solution.py:316
  65.3 0.8 %collective-permute-start.13 = (f32[136,128]{1,0:T(8,128)S(1)}, f32[136,128]{1,0:T(8,128)S(1)}, u32[]{:S(2)}, u32[]{:S(2)}) collective-permute-start(f32[136,128]{1,0:T(8,128)S(1)} %add_add_fusion.refs_1_), channel_id=1, source_target_pairs={{0,8},{4,12},{8,0},{12,4},{16,24},{20,28},{24,16},{28,20},{32,40},... | collective-permute-start | bytes 208904 | tf_op jit(solution)/shard_map/ppermute | solution.py:316
  66.2 0.3 collective-permute-start.12
  66.5 0.5 slice_bitcast_fusion
  67.0 5.1 %all-to-all-done.2 = f32[16,32,128]{2,1,0:T(8,128)S(1)} async-done(((f32[16,32,128]{2,1,0:T(8,128)}), f32[16,32,128]{2,1,0:T(8,128)S(1)}, u32[]{:S(2)}, u32[]{:S(2)}) %all-to-all-start.2) | async-done | bytes 262176 | tf_op jit(solution)/shard_map/all_to_all | solution.py:320
  72.0 0.8 %grad_inputs_kernel.1.refs_5_ = f32[64,1024]{1,0:T(8,128)} custom-call(f32[64,1024]{1,0:T(8,128)S(1)} %bitcast.18, f32[512,128]{1,0:T(8,128)S(1)} %bitcast.21), custom_call_target="tpu_custom_call" | custom-call | tf_op jit(solution)/shard_map/grad_inputs_kernel/pallas_call | solution.py:302
  72.8 0.1 add.20.refs_6_
  72.9 0.0 copy-start.8
  72.9 0.0 copy-start.7
  72.9 0.0 copy-start.9
  73.0 0.6 copy-done.8
  73.6 0.5 copy-done.7
  74.0 1.3 %final_kernel.1 = (f32[64,256]{1,0:T(8,128)}, f32[3,64]{1,0:T(4,128)}) custom-call(s32[2]{0:T(128)S(1)} %pad_add_fusion.refs_0_, f32[136,128]{1,0:T(8,128)S(1)} %add_add_fusion.refs_1_, f32[136,128]{1,0:T(8,128)S(1)} %collective-permute-done.12.refs_2_, f32[136,128]{1,0:T(8,128)S(1)} %collective-permute-done.13.refs_3_, ...), custom_call_target="tpu_custom_call" | custom-call | tf_op jit(solution)/shard_map/final_kernel/pallas_call | solution.py:302
  (35 shorter events, 0.2 us)
Async XLA Ops:
  0.6 20.2 %collective-permute-start = (f32[64,1024]{1,0:T(8,128)}, f32[64,1024]{1,0:T(8,128)S(1)}, u32[]{:S(2)}, u32[]{:S(2)}) collective-permute-start(f32[64,1024]{1,0:T(8,128)} %bitcast.15), channel_id=1, source_target_pairs={{0,2},{1,3},{2,0},{3,1},{4,6},{5,7},{6,4},{7,5},{8,10},{9,11},{10,... | collective-permute-start | bytes 786440 | tf_op jit(solution)/shard_map/ppermute | solution.py:316
  2.4 0.9 %copy-start.5 = (f32[1,64,1024]{2,1,0:T(8,128)S(1)}, f32[1,64,1024]{2,1,0:T(8,128)}, u32[]{:S(2)}) copy-start(f32[1,64,1024]{2,1,0:T(8,128)} %param.11) | copy-start | bytes 786436
  3.3 8.8 %copy-start.11 = (f32[256,64]{0,1:T(8,128)S(1)}, f32[256,64]{0,1:T(8,128)}, u32[]{:S(2)}) copy-start(f32[256,64]{0,1:T(8,128)} %param.16) | copy-start | bytes 196612
  3.3 9.4 %copy-start.4 = (f32[2,128,128]{2,1,0:T(8,128)S(1)}, f32[2,128,128]{2,1,0:T(8,128)}, u32[]{:S(2)}) copy-start(f32[2,128,128]{2,1,0:T(8,128)} %constant.31.clone.refs_3_.refs_9_.refs_8_) | copy-start | bytes 393220
  3.3 9.4 %copy-start.12 = (f32[4,16384]{1,0:T(4,128)S(1)}, f32[4,16384]{1,0:T(4,128)}, u32[]{:S(2)}) copy-start(f32[4,16384]{1,0:T(4,128)} %refs_0_.2) | copy-start | bytes 786436
  4.1 8.7 %copy-start = (bf16[768,256]{1,0:T(8,128)(2,1)S(1)}, bf16[768,256]{1,0:T(8,128)(2,1)}, u32[]{:S(2)}) copy-start(bf16[768,256]{1,0:T(8,128)(2,1)} %constant.28.clone.refs_2_.refs_6_.refs_5_) | copy-start | bytes 1179652
  4.1 8.7 %copy-start.2 = (bf16[256,384]{1,0:T(8,128)(2,1)S(1)}, bf16[256,384]{1,0:T(8,128)(2,1)}, u32[]{:S(2)}) copy-start(bf16[256,384]{1,0:T(8,128)(2,1)} %constant.27.clone.refs_1_.refs_5_.refs_4_) | copy-start | bytes 589828
  4.1 16.7 %all-to-all-start = ((f32[16,32,128]{2,1,0:T(8,128)}), f32[16,32,128]{2,1,0:T(8,128)S(1)}, u32[]{:S(2)}, u32[]{:S(2)}) async-start(f32[16,32,128]{2,1,0:T(8,128)} %bitcast.3), calls=%async_computation | async-start | bytes 524288 | tf_op jit(solution)/shard_map/all_to_all | solution.py:320
  12.1 4.0 %collective-permute-start.1 = (f32[64,128]{1,0:T(8,128)S(1)}, f32[64,128]{1,0:T(8,128)S(1)}, u32[]{:S(2)}, u32[]{:S(2)}) collective-permute-start(f32[64,128]{1,0:T(8,128)S(1)} %dynamic-slice_bitcast_fusion), channel_id=1, source_target_pairs={{0,2},{1,3},{2,0},{3,1},{4,6},{5,7},{6,4},{7,5},{8,10},{9,11},{10,... | collective-permute-start | bytes 98312 | tf_op jit(solution)/shard_map/ppermute | solution.py:316
  12.8 8.0 %copy-start.1 = (f32[1,64,1024]{2,1,0:T(8,128)S(1)}, f32[1,64,1024]{2,1,0:T(8,128)}, u32[]{:S(2)}) copy-start(f32[1,64,1024]{2,1,0:T(8,128)} %param.12) | copy-start | bytes 786436
  20.8 1.2 %copy-start.3 = (bf16[768,256]{1,0:T(8,128)(2,1)S(1)}, bf16[768,256]{1,0:T(8,128)(2,1)}, u32[]{:S(2)}) copy-start(bf16[768,256]{1,0:T(8,128)(2,1)} %constant.30.clone.refs_8_.refs_7_) | copy-start | bytes 1179652
  20.8 1.2 %copy-start.10 = (bf16[128,768]{1,0:T(8,128)(2,1)S(1)}, bf16[128,768]{1,0:T(8,128)(2,1)}, u32[]{:S(2)}) copy-start(bf16[128,768]{1,0:T(8,128)(2,1)} %constant.29.clone.refs_7_.refs_6_) | copy-start | bytes 589828
  21.9 0.7 copy-start.13
  21.9 0.7 copy-start.14
  21.9 3.7 %collective-permute-start.2 = (f32[512,128]{1,0:T(8,128)S(1)}, f32[512,128]{1,0:T(8,128)S(1)}, u32[]{:S(2)}, u32[]{:S(2)}) collective-permute-start(f32[512,128]{1,0:T(8,128)S(1)} %get-tuple-element.23), channel_id=1, source_target_pairs={{0,1},{1,0},{2,3},{3,2},{4,5},{5,4},{6,7},{7,6},{8,9},{9,8},{10,11... | collective-permute-start | bytes 786440 | tf_op jit(solution)/shard_map/ppermute | solution.py:316
  40.3 1.6 %collective-permute-start.3 = (f32[512,128]{1,0:T(8,128)S(1)}, f32[512,128]{1,0:T(8,128)S(1)}, u32[]{:S(2)}, u32[]{:S(2)}) collective-permute-start(f32[512,128]{1,0:T(8,128)S(1)} %bitcast.22), channel_id=1, source_target_pairs={{0,1},{1,0},{2,3},{3,2},{4,5},{5,4},{6,7},{7,6},{8,9},{9,8},{10,11... | collective-permute-start | bytes 786440 | tf_op jit(solution)/shard_map/ppermute | solution.py:316
  40.4 1.5 %copy-start.6 = (f32[1,64,1024]{2,1,0:T(8,128)S(1)}, f32[1,64,1024]{2,1,0:T(8,128)}, u32[]{:S(2)}) copy-start(f32[1,64,1024]{2,1,0:T(8,128)} %param.11) | copy-start | bytes 786436
  43.0 8.1 %collective-permute-start.6 = (f32[72,128]{1,0:T(8,128)S(1)}, f32[72,128]{1,0:T(8,128)S(1)}, u32[]{:S(2)}, u32[]{:S(2)}) collective-permute-start(f32[72,128]{1,0:T(8,128)S(1)} %get-tuple-element.30.refs_9_.refs_0_), channel_id=1, source_target_pairs={{0,64},{1,65},{2,66},{3,67},{64,0},{65,1},{66,2},{67,3},{4,68},{5,... | collective-permute-start | bytes 110600 | tf_op jit(solution)/shard_map/ppermute | solution.py:316
  46.0 5.1 %collective-permute-start.8 = (f32[64,128]{1,0:T(8,128)S(1)}, f32[64,128]{1,0:T(8,128)S(1)}, u32[]{:S(2)}, u32[]{:S(2)}) collective-permute-start(f32[64,128]{1,0:T(8,128)S(1)} %get-tuple-element.33), channel_id=1, source_target_pairs={{0,66},{1,67},{2,64},{3,65},{64,2},{65,3},{66,0},{67,1},{4,70},{5,... | collective-permute-start | bytes 98312 | tf_op jit(solution)/shard_map/ppermute | solution.py:316
  46.2 4.9 %collective-permute-start.7 = (f32[64,128]{1,0:T(8,128)S(1)}, f32[64,128]{1,0:T(8,128)S(1)}, u32[]{:S(2)}, u32[]{:S(2)}) collective-permute-start(f32[64,128]{1,0:T(8,128)S(1)} %get-tuple-element.33), channel_id=1, source_target_pairs={{0,2},{1,3},{2,0},{3,1},{64,66},{65,67},{66,64},{67,65},{4,6},{5,7... | collective-permute-start | bytes 98312 | tf_op jit(solution)/shard_map/ppermute | solution.py:316
  51.1 11.1 %collective-permute-start.11 = (f32[136,128]{1,0:T(8,128)S(1)}, f32[136,128]{1,0:T(8,128)S(1)}, u32[]{:S(2)}, u32[]{:S(2)}) collective-permute-start(f32[136,128]{1,0:T(8,128)S(1)} %merge_kernel.1), channel_id=1, source_target_pairs={{0,48},{4,52},{8,56},{12,60},{16,32},{20,36},{24,40},{28,44},{32,1... | collective-permute-start | bytes 208904 | tf_op jit(solution)/shard_map/ppermute | solution.py:316
  52.1 10.2 %collective-permute-start.10 = (f32[136,128]{1,0:T(8,128)S(1)}, f32[136,128]{1,0:T(8,128)S(1)}, u32[]{:S(2)}, u32[]{:S(2)}) collective-permute-start(f32[136,128]{1,0:T(8,128)S(1)} %merge_kernel.1), channel_id=1, source_target_pairs={{0,32},{4,36},{8,40},{12,44},{16,48},{20,52},{24,56},{28,60},{32,0... | collective-permute-start | bytes 208904 | tf_op jit(solution)/shard_map/ppermute | solution.py:316
  52.6 9.6 %collective-permute-start.9 = (f32[136,128]{1,0:T(8,128)S(1)}, f32[136,128]{1,0:T(8,128)S(1)}, u32[]{:S(2)}, u32[]{:S(2)}) collective-permute-start(f32[136,128]{1,0:T(8,128)S(1)} %merge_kernel.1), channel_id=1, source_target_pairs={{0,16},{4,20},{8,24},{12,28},{16,0},{20,4},{24,8},{28,12},{32,48},... | collective-permute-start | bytes 208904 | tf_op jit(solution)/shard_map/ppermute | solution.py:316
  55.3 17.5 %collective-permute-start.5 = (f32[4,16384]{1,0:T(4,128)S(1)}, f32[4,16384]{1,0:T(4,128)S(1)}, u32[]{:S(2)}, u32[]{:S(2)}) collective-permute-start(f32[4,16384]{1,0:T(4,128)S(1)} %get-tuple-element.32.refs_4_), channel_id=1, source_target_pairs={{0,64},{64,0},{1,65},{65,1},{2,66},{66,2},{3,67},{67,3},{4,68},{68... | collective-permute-start | bytes 786440 | tf_op jit(solution)/shard_map/ppermute | solution.py:316
  58.6 13.4 %all-to-all-start.2 = ((f32[16,32,128]{2,1,0:T(8,128)}), f32[16,32,128]{2,1,0:T(8,128)S(1)}, u32[]{:S(2)}, u32[]{:S(2)}) async-start(f32[16,32,128]{2,1,0:T(8,128)} %get-tuple-element.31), calls=%async_computation.2 | async-start | bytes 524288 | tf_op jit(solution)/shard_map/all_to_all | solution.py:320
  62.1 10.7 %collective-permute-start.4 = (f32[64,1024]{1,0:T(8,128)S(1)}, f32[64,1024]{1,0:T(8,128)S(1)}, u32[]{:S(2)}, u32[]{:S(2)}) collective-permute-start(f32[64,1024]{1,0:T(8,128)S(1)} %get-tuple-element.27), channel_id=1, source_target_pairs={{0,2},{1,3},{2,0},{3,1},{4,6},{5,7},{6,4},{7,5},{8,10},{9,11},{10,... | collective-permute-start | bytes 786440 | tf_op jit(solution)/shard_map/ppermute | solution.py:316
  62.3 10.7 %collective-permute-start.14 = (f32[136,128]{1,0:T(8,128)S(1)}, f32[136,128]{1,0:T(8,128)S(1)}, u32[]{:S(2)}, u32[]{:S(2)}) collective-permute-start(f32[136,128]{1,0:T(8,128)S(1)} %add_add_fusion.refs_1_), channel_id=1, source_target_pairs={{0,12},{4,8},{8,4},{12,0},{16,28},{20,24},{24,20},{28,16},{32,44},... | collective-permute-start | bytes 208904 | tf_op jit(solution)/shard_map/ppermute | solution.py:316
  65.3 7.7 %collective-permute-start.13 = (f32[136,128]{1,0:T(8,128)S(1)}, f32[136,128]{1,0:T(8,128)S(1)}, u32[]{:S(2)}, u32[]{:S(2)}) collective-permute-start(f32[136,128]{1,0:T(8,128)S(1)} %add_add_fusion.refs_1_), channel_id=1, source_target_pairs={{0,8},{4,12},{8,0},{12,4},{16,24},{20,28},{24,16},{28,20},{32,40},... | collective-permute-start | bytes 208904 | tf_op jit(solution)/shard_map/ppermute | solution.py:316
  66.2 6.8 %collective-permute-start.12 = (f32[136,128]{1,0:T(8,128)S(1)}, f32[136,128]{1,0:T(8,128)S(1)}, u32[]{:S(2)}, u32[]{:S(2)}) collective-permute-start(f32[136,128]{1,0:T(8,128)S(1)} %add_add_fusion.refs_1_), channel_id=1, source_target_pairs={{0,4},{4,0},{8,12},{12,8},{16,20},{20,16},{24,28},{28,24},{32,36},... | collective-permute-start | bytes 208904 | tf_op jit(solution)/shard_map/ppermute | solution.py:316
  72.9 0.7 copy-start.8
  72.9 1.1 %copy-start.7 = (f32[64,1024]{1,0:T(8,128)S(1)}, f32[64,1024]{1,0:T(8,128)}, u32[]{:S(2)}) copy-start(f32[64,1024]{1,0:T(8,128)} %grad_inputs_kernel.1.refs_5_) | copy-start | bytes 786436
  72.9 2.4 %copy-start.9 = (f32[64,1024]{1,0:T(8,128)}, f32[64,1024]{1,0:T(8,128)S(1)}, u32[]{:S(2)}) copy-start(f32[64,1024]{1,0:T(8,128)S(1)} %add.19.refs_7_) | copy-start | bytes 786436

commit v3 on v2

v3 whole, which is shorter than its diff:
```python
import functools
import math

import jax
import jax.numpy as jnp
import ml_dtypes
import numpy as np
from jax import lax
from jax.experimental import pallas as pl
from jax.experimental.pallas import tpu as pltpu
from jax.sharding import PartitionSpec as P

SIDE = 128
LENGTH = SIDE * SIDE
F32 = jnp.float32
BF16 = jnp.bfloat16
GELU_SCALE = math.sqrt(2.0 / math.pi)
GELU_CUBE = 0.044715
VMEM = pl.BlockSpec(memory_space=pltpu.VMEM)
SMEM = pl.BlockSpec(memory_space=pltpu.SMEM)
HBM = pl.BlockSpec(memory_space=pltpu.HBM)


def two_parts(table):
    high = table.astype(ml_dtypes.bfloat16)
    low = (table - high.astype(np.float64)).astype(ml_dtypes.bfloat16)
    return high, low


@functools.cache
def tables():
    one = np.arange(SIDE, dtype=np.float64)
    turn = 2.0 * np.pi * np.outer(one + 0.25, one) / SIDE
    rows = np.concatenate([np.cos(turn), -np.sin(turn)], axis=0)
    high, low = two_parts(rows)
    into_rows = np.concatenate([high, low, high], axis=1)
    high, low = two_parts(rows.T / LENGTH)
    back_rows = np.concatenate([high, low, high], axis=1)
    turn = 2.0 * np.pi * np.outer(one, one) / SIDE
    real, imag = np.cos(turn), -np.sin(turn)
    lanes = np.block([[real, imag], [-imag, real]])
    high, low = two_parts(lanes)
    into_lanes = np.concatenate([high, low, high], axis=0)
    high, low = two_parts(lanes.T)
    back_lanes = np.concatenate([high, low, high], axis=0)
    turn = 2.0 * np.pi * np.outer(one + 0.25, one) / LENGTH
    twist = np.stack([np.cos(turn), -np.sin(turn)]).astype(np.float32)
    return into_rows, into_lanes, back_rows, back_lanes, twist


def parts(value):
    high = value.astype(BF16)
    low = (value - high.astype(F32)).astype(BF16)
    return high, low


def dot(left, right, dims=((1,), (0,))):
    return lax.dot_general(left, right, (dims, ((), ())), preferred_element_type=F32)


def forward(pair, into_rows, into_lanes, twist):
    cos, sin = twist[0], twist[1]
    high, low = parts(jnp.concatenate(pair, axis=1))
    step = dot(into_rows[...], jnp.concatenate([high, high, low], axis=0))
    turned = []
    for at in range(len(pair)):
        real = step[:SIDE, at * SIDE : (at + 1) * SIDE]
        imag = step[SIDE:, at * SIDE : (at + 1) * SIDE]
        turned.append(jnp.concatenate([real * cos - imag * sin, real * sin + imag * cos], axis=1))
    high, low = parts(jnp.concatenate(turned, axis=0))
    return dot(jnp.concatenate([high, high, low], axis=1), into_lanes[...])


def backward(spectrum, back_rows, back_lanes, twist):
    cos, sin = twist[0], twist[1]
    count = spectrum.shape[0] // SIDE
    high, low = parts(spectrum)
    step = dot(jnp.concatenate([high, high, low], axis=1), back_lanes[...])
    turned = []
    for at in range(count):
        real = step[at * SIDE : (at + 1) * SIDE, :SIDE]
        imag = step[at * SIDE : (at + 1) * SIDE, SIDE:]
        turned.append(jnp.concatenate([real * cos + imag * sin, imag * cos - real * sin], axis=0))
    high, low = parts(jnp.concatenate(turned, axis=1))
    result = dot(back_rows[...], jnp.concatenate([high, high, low], axis=0))
    return [result[:, at * SIDE : (at + 1) * SIDE] for at in range(count)]


def times(left, right):
    lr, li, rr, ri = left[:, :SIDE], left[:, SIDE:], right[:, :SIDE], right[:, SIDE:]
    return jnp.concatenate([lr * rr - li * ri, lr * ri + li * rr], axis=1)


def times_conj(left, right):
    lr, li, rr, ri = left[:, :SIDE], left[:, SIDE:], right[:, :SIDE], right[:, SIDE:]
    return jnp.concatenate([lr * rr + li * ri, li * rr - lr * ri], axis=1)


def delayed(value, steps):
    row = lax.broadcasted_iota(jnp.int32, value.shape, 0)
    lane = lax.broadcasted_iota(jnp.int32, value.shape, 1)
    turned = pltpu.roll(value, steps, 1)
    above = jnp.where(row == 0, 0.0, pltpu.roll(turned, 1, 0))
    return jnp.where(lane < steps, above, turned)


def advanced(value, steps):
    row = lax.broadcasted_iota(jnp.int32, value.shape, 0)
    lane = lax.broadcasted_iota(jnp.int32, value.shape, 1)
    turned = pltpu.roll(value, SIDE - steps, 1)
    below = jnp.where(row == SIDE - 1, 0.0, pltpu.roll(turned, SIDE - 1, 0))
    return jnp.where(lane >= SIDE - steps, below, turned)


def blocks_kernel(signal, out):
    for at in range(8):
        out[pl.ds(at, 64, stride=8), :] = signal[:, at * SIDE : (at + 1) * SIDE]


def from_blocks(ref):
    return jnp.concatenate([ref[pl.ds(at, 64, stride=8), :] for at in range(8)], axis=1)


def spectrum_kernel(place_at, taps, skip, kernel, into_rows, into_lanes, twist, out, gains, rows):
    for at in range(SIDE):
        rows[pl.ds(at, 4, stride=SIDE), :] = kernel[:, at * SIDE : (at + 1) * SIDE]
    line = lax.broadcasted_iota(jnp.int32, (SIDE, SIDE), 0)
    lane = lax.broadcasted_iota(jnp.int32, (SIDE, SIDE), 1)
    start = (line == 0) & (lane == 0)
    every = [
        rows[at * SIDE : (at + 1) * SIDE, :] + jnp.where(start, skip[at], 0.0) for at in range(4)
    ]
    out[...] = forward(every, into_rows, into_lanes, twist)
    line, lane = line[:16], lane[:16]
    first, chan = 4 * place_at[0], place_at[1]
    result = jnp.where(line == 3, jnp.bitwise_and(chan, 1).astype(F32), 0.0)
    result = jnp.where(line == 4, lax.shift_right_logical(chan, 1).astype(F32), result)
    result = jnp.where((line >= 8) & (line < 12) & (lane == first + line - 8), 1.0, result)
    for tap in range(3):
        for at in range(4):
            result = jnp.where((line == tap) & (lane == at), taps[tap, first + at], result)
    gains[...] = result


def weights_kernel(place_at, mix, mix_far, _rows, _lanes, into, back):
    chan = place_at[1]
    start = pl.multiple_of(128 * lax.shift_right_logical(chan, 1), 128)
    both = jnp.concatenate([mix[:, pl.ds(start, 128)], mix_far[...]], axis=0)
    both = pltpu.roll(both, 64 * jnp.bitwise_and(chan, 1), 1)
    high, low = parts(both)
    back[...] = jnp.concatenate([high, low, high], axis=1)
    high, low = parts(both.T)
    into[...] = jnp.concatenate([high, low, high], axis=1)


def grad_act_kernel(cot, cot_far, weights, own, other):
    for half in range(4):
        lanes = slice(half * 256, (half + 1) * 256)
        high, low = parts(jnp.concatenate([cot[:, lanes], cot_far[:, lanes]], axis=0))
        result = dot(weights[...], jnp.concatenate([high, high, low], axis=0))
        for at in range(2):
            place = pl.ds(2 * half + at, 64, stride=8)
            own[place, :] = result[:64, at * SIDE : (at + 1) * SIDE]
            other[place, :] = result[64:, at * SIDE : (at + 1) * SIDE]


def channel(ref, at):
    return ref[:, at * 8 : (at + 1) * 8, :].reshape(SIDE, SIDE)


def gains_of(gains, at):
    return [jnp.broadcast_to(gains[tap : tap + 1, at : at + 1], (SIDE, SIDE)) for tap in range(3)]


def moved(copies):
    for one in copies:
        one.start()
    return copies


def forward_kernel(
    gains, signal, kernel_spec, into_rows, into_lanes, back_rows, back_lanes, twist,
    spec, long_conv, slopes, act_out, act, sem,
):
    spectrum = forward([channel(signal, at) for at in range(4)], into_rows, into_lanes, twist)
    spec[...] = spectrum
    result = backward(times(spectrum, kernel_spec[...]), back_rows, back_lanes, twist)
    for index in range(4):
        taps = gains_of(gains, index)
        whole = result[index]
        long_conv[index] = whole
        value = taps[2] * whole + taps[1] * delayed(whole, 1) + taps[0] * delayed(whole, 2)
        square = value * value
        half = 0.5 + 0.5 * jnp.tanh(value * (GELU_SCALE + GELU_SCALE * GELU_CUBE * square))
        act[:, index * 8 : (index + 1) * 8, :] = (value * half).reshape(16, 8, SIDE)
        slopes[index] = half + half * (1.0 - half) * value * (
            2.0 * GELU_SCALE + 6.0 * GELU_SCALE * GELU_CUBE * square
        )
    copy = pltpu.make_async_copy(act, act_out.at[:, pl.ds(0, 32), :], sem)
    copy.start()
    copy.wait()


def join_kernel(act, own, near, out, total, sem):
    total[...] = (own[...] + near[...]).reshape(16, 32, SIDE)
    copy = pltpu.make_async_copy(total, out.at[:, pl.ds(32, 32), :], sem)
    copy.start()
    copy.wait()


def slope_kernel(gains, grad_act, signal, long_conv, slopes, grads, small):
    small[...] = jnp.zeros_like(small)
    for index in range(4):
        taps = gains_of(gains, index)
        grad = channel(grad_act, 4 + index) * slopes[index]
        later = [advanced(grad, 2), advanced(grad, 1), grad]
        grads[index] = taps[0] * later[0] + taps[1] * later[1] + taps[2] * later[2]
        pairs = [one * long_conv[index] for one in later] + [grads[index] * channel(signal, index)]
        sums = jnp.concatenate([jnp.sum(one, axis=0, keepdims=True) for one in pairs], axis=0)
        small[:4, :] = small[:4, :] + jnp.sum(sums, axis=1, keepdims=True) * gains[8 + index : 9 + index, :]


def backward_kernel(
    grads, spec, kernel_spec, into_rows, into_lanes, back_rows, back_lanes, twist,
    grad_out, kernel_out, grad_in, rows, sem,
):
    spectrum = forward([grads[at] for at in range(4)], into_rows, into_lanes, twist)
    result = backward(times_conj(spectrum, kernel_spec[...]), back_rows, back_lanes, twist)
    for at in range(4):
        grad_in[:, at * 8 : (at + 1) * 8, :] = result[at].reshape(16, 8, SIDE)
    copy = pltpu.make_async_copy(grad_in, grad_out, sem)
    copy.start()
    result = backward(times_conj(spectrum, spec[...]), back_rows, back_lanes, twist)
    for at in range(4):
        rows[at * SIDE : (at + 1) * SIDE, :] = result[at]
    for at in range(SIDE):
        kernel_out[:, at * SIDE : (at + 1) * SIDE] = rows[pl.ds(at, 4, stride=SIDE), :]
    copy.wait()


def tail_kernel(act, act_near, cot, cot_far, signal, weights, small, mine, theirs, out, out_far):
    active = jnp.concatenate([from_blocks(act), from_blocks(act_near)], axis=0)
    act_high, act_low = parts(active)
    high, low = parts(jnp.concatenate([cot[...], cot_far[...]], axis=0))
    result = dot(
        jnp.concatenate([high, low, high], axis=1),
        jnp.concatenate([act_high, act_high, act_low], axis=1),
        ((1,), (1,)),
    )
    mine[:64, :] = result[:64]
    mine[64:, :] = small[...]
    theirs[...] = result[64:]
    mixed = dot(weights[...], jnp.concatenate([act_high, act_high, act_low], axis=0))
    out[...] = signal[...] + mixed[:64]
    out_far[...] = mixed[64:]


def merge_kernel(mine, mine_far, theirs, theirs_far, out):
    out[:64, :] = mine[:64, :] + mine_far[:64, :]
    out[64:128, :] = theirs[...] + theirs_far[...]
    out[128:, :] = mine[64:, :] + mine_far[64:, :]


def finish_kernel(cotangent, grad_in, own, near, kernel_own, kernel_near, grad_inputs, outputs, grad_kernel, token):
    for at in range(8):
        lanes = slice(at * SIDE, (at + 1) * SIDE)
        grad_inputs[:, lanes] = cotangent[:, lanes] + grad_in[pl.ds(at, 64, stride=8), :]
    outputs[...] = own[...] + near[...]
    grad_kernel[...] = kernel_own[...] + kernel_near[...]
    token[...] = jnp.zeros_like(token)


def final_kernel(gains, total0, total1, total2, total3, out, taps, skip):
    core = jnp.broadcast_to(gains[3:4, :], (64, SIDE)) > 0.5
    place = jnp.broadcast_to(gains[4:5, :], (64, SIDE)) > 0.5
    whole = total0[...] + total1[...] + total2[...] + total3[...]
    near, far = [
        jnp.where(core, pltpu.roll(one, 64, 1), one) for one in (whole[:64], whole[64:128])
    ]
    out[:, :SIDE] = jnp.where(place, far, near)
    out[:, SIDE:] = jnp.where(place, near, far)
    taps[...] = whole[128:131, :64]
    own = jnp.sum(whole[131:132] * gains[8:12, :], axis=1, keepdims=True)
    line = lax.broadcasted_iota(jnp.int32, (4, SIDE), 0)
    lane = lax.broadcasted_iota(jnp.int32, (4, SIDE), 1)
    skip[...] = jnp.sum(jnp.where(line == lane, own, 0.0), axis=0, keepdims=True)[:, :4]


def call(kernel, outs, *args, scalars=0, far=(), far_outs=(), scratch=(), after=(), aliases=()):
    shapes = [shape if not isinstance(shape, tuple) else jax.ShapeDtypeStruct(shape, F32) for shape in outs]
    count = len(args)

    def body(*refs):
        kernel(*refs[:count], *refs[count + len(after) :])

    ins = [SMEM if at < scalars else HBM if at in far else VMEM for at in range(count)]
    places = [HBM if at in far_outs else VMEM for at in range(len(outs))]
    return pl.pallas_call(
        body,
        out_shape=shapes if len(shapes) > 1 else shapes[0],
        in_specs=ins + [pl.BlockSpec(memory_space=pl.ANY)] * len(after),
        out_specs=places if len(shapes) > 1 else places[0],
        scratch_shapes=[shape if not isinstance(shape, tuple) else pltpu.VMEM(shape, F32) for shape in scratch],
        compiler_params=pltpu.CompilerParams(vmem_limit_bytes=20 * 1024 * 1024),
        input_output_aliases=dict(aliases),
        name=kernel.__name__,
    )(*args, *after)


def swapped(value, axes, flip):
    count = lax.axis_size(axes)
    return lax.ppermute(value, axes, [(at, at ^ flip) for at in range(count)])


def turned(value):
    return lax.all_to_all(value, "seq", 0, 0, tiled=True)


def shards(inputs, cotangent, conv_weight, kernel, skip_gain, mix_weight):
    signal = inputs[0]
    grad_out = cotangent[0]
    seq, chan = lax.axis_index("seq"), lax.axis_index("chan")
    place_at = jnp.stack([seq, chan]).astype(jnp.int32)
    into_rows, into_lanes, back_rows, back_lanes, twist = (jnp.asarray(table) for table in tables())
    mix = mix_weight.T

    cot_far = swapped(grad_out, "chan", 2)
    far = jnp.bitwise_xor(lax.shift_right_logical(chan, 1), 1)
    mix_far = swapped(lax.dynamic_slice(mix, (0, 128 * far), (64, 128)), "chan", 2)
    signal_blocks = call(
        blocks_kernel, [(512, SIDE)], signal
    )
    signal_in = turned(signal_blocks.reshape(16, 32, SIDE))
    kernel_spec, gains = call(
        spectrum_kernel, [(512, 256), (16, SIDE)],
        place_at, conv_weight, skip_gain, kernel, into_rows, into_lanes, twist,
        scalars=3, scratch=[(512, SIDE)], after=[signal_blocks],
    )
    weights_into, weights_back = call(
        weights_kernel, [jax.ShapeDtypeStruct((SIDE, 3 * SIDE), BF16)] * 2, place_at, mix, mix_far,
        back_rows, back_lanes, scalars=1, after=[kernel_spec],
    )
    grad_own, grad_other = call(
        grad_act_kernel, [(512, SIDE)] * 2, grad_out, cot_far, weights_into, after=[signal_in]
    )
    grad_near = swapped(grad_other, "chan", 1)
    spec, long_conv, slopes, act = call(
        forward_kernel,
        [(512, 256), (4, SIDE, SIDE), (4, SIDE, SIDE), (16, 64, SIDE)],
        gains, signal_in, kernel_spec, into_rows, into_lanes, back_rows, back_lanes, twist,
        far_outs=(3,), after=[grad_own], scratch=[(16, 32, SIDE), pltpu.SemaphoreType.DMA],
    )
    act = call(
        join_kernel, [(16, 64, SIDE)], act, grad_own, grad_near,
        far=(0,), far_outs=(0,), aliases={0: 0}, scratch=[(16, 32, SIDE), pltpu.SemaphoreType.DMA],
    )
    act_in = turned(act)
    act_own = act_in[:, :32].reshape(512, SIDE)
    act_near = swapped(act_own, "chan", 1)
    grads, small = call(
        slope_kernel, [(4, SIDE, SIDE), (8, SIDE)], gains, act_in, signal_in, long_conv, slopes
    )
    mine, theirs, out_own, out_far = call(
        tail_kernel,
        [(72, SIDE), (64, SIDE), (64, 1024), (64, 1024)],
        act_own, act_near, grad_out, cot_far, signal, weights_back, small,
    )
    grad_long, kernel_local = call(
        backward_kernel,
        [(16, 32, SIDE), (4, LENGTH)],
        grads, spec, kernel_spec, into_rows, into_lanes, back_rows, back_lanes, twist,
        far_outs=(0,), after=[mine], scratch=[(16, 32, SIDE), (512, SIDE), pltpu.SemaphoreType.DMA],
    )
    both = ("dp", "chan")
    total = call(
        merge_kernel, [(136, SIDE)], mine, swapped(mine, both, 4), swapped(theirs, both, 2), swapped(theirs, both, 6),
        after=[kernel_local],
    )
    grad_in = turned(grad_long).reshape(512, SIDE)
    grad_inputs, outputs, grad_kernel, token = call(
        finish_kernel, [(64, 1024), (64, 1024), (4, LENGTH), (8, SIDE)],
        grad_out, grad_in, out_own, swapped(out_far, "chan", 2), kernel_local, swapped(kernel_local, "dp", 1),
    )
    total = total + swapped(total, "seq", 4) + swapped(total, "seq", 12) + swapped(total, "seq", 8)
    grad_mix, grad_conv, grad_skip = call(
        final_kernel, [(64, 256), (3, 64), (1, 4)], gains, total, *(swapped(total, "seq", at) for at in (1, 3, 2)),
        after=[token],
    )
    return (outputs[None], grad_inputs[None], grad_kernel, grad_skip[0], grad_mix.T, grad_conv)


def solution(mesh):
    placed = (
        P("dp", "chan", "seq"),
        P("dp", "chan", "seq"),
        P(None, "chan"),
        P(("chan", "seq"), None),
        P(("chan", "seq")),
        P(None, "chan"),
    )
    return jax.shard_map(
        shards,
        mesh=mesh,
        in_specs=placed,
        out_specs=(
            P("dp", "chan", "seq"),
            P("dp", "chan", "seq"),
            P(("chan", "seq"), None),
            P(("chan", "seq")),
            P(None, "chan"),
            P(None, "chan"),
        ),
        check_vma=False,
    )
```

time: 75.7 us -> 70.4 us (0.930)
  Pallas kernels: 14.2 us -> 10.1 us
  local copies, waits for them, and re-layouts: 3.15 us -> 1.61 us
  blocking collectives: 14.5 us -> 15.5 us
    pallas_call x11 -> x12, Pallas kernels: 14.2 us -> 10.1 us  [call(): pl.pallas_call(body, out_shape=shapes if len(shapes) > 1 else shapes[0],...]
    all_to_all x2, waiting for transfers between devices: 9.71 us -> 7.84 us  [turned(): return lax.all_to_all(value, 'seq', 0, 0, tiled=True)]
    ppermute x15, waiting for transfers between devices: 3.24 us -> 4.54 us  [swapped(): return lax.ppermute(value, axes, [(at, at ^ flip) for at in range(count)])]
    unnamed x30 -> x24, local copies, waits for them, and re-layouts: 2.61 us -> 1.58 us
    all_to_all x1, blocking collectives: 14.5 us -> 15.5 us  [turned(): return lax.all_to_all(value, 'seq', 0, 0, tiled=True)]
    all_to_all x2, starting transfers between devices: 11.5 us -> 12.3 us  [turned(): return lax.all_to_all(value, 'seq', 0, 0, tiled=True)]
  transfers between devices with their start and end apart: 17 -> 17, of which waited for: 4 -> 5; matrix products, arithmetic and copies ran while one was open for 1% -> 0% of each run, Pallas kernels for 14% -> 12%
where the time goes in v3:
time: 70.4 us; the launch traced here: 69.9 us
  starting transfers between devices  29.4 us (42%)
  blocking collectives  15.5 us (22%)
  waiting for transfers between devices  12.4 us (18%)
  Pallas kernels  10.1 us (14%)
  local copies, waits for them, and re-layouts  1.61 us (2%)
  between operations  0.81 us (1%)
    ppermute x15, starting transfers between devices, swapped(): return lax.ppermute(value, axes, [(at, at ^ flip) for at in range(count)])  17.1 us
    all_to_all x1, blocking collectives, turned(): return lax.all_to_all(value, 'seq', 0, 0, tiled=True)  15.5 us
    all_to_all x2, starting transfers between devices, turned(): return lax.all_to_all(value, 'seq', 0, 0, tiled=True)  12.3 us
    pallas_call x12, Pallas kernels, call(): pl.pallas_call(body, out_shape=shapes if len(shapes) > 1 else shapes[0],...  10.1 us
    all_to_all x2, waiting for transfers between devices, turned(): return lax.all_to_all(value, 'seq', 0, 0, tiled=True)  7.84 us
    ppermute x15, waiting for transfers between devices, swapped(): return lax.ppermute(value, axes, [(at, at ^ flip) for at in range(count)])  4.54 us
    unnamed x24, local copies, waits for them, and re-layouts  1.58 us
  transfers between devices with their start and end apart: 17, of which 5 were waited for; matrix products, arithmetic and copies ran while one was open for 0% of the time, Pallas kernels for 12%

profile of v3, /device:TPU:0, one launch (start us, length us, event | category | flops | bytes accessed | tf_op | source)
XLA Modules:
  0.0 69.9 jit_solution(7988151405684367874)
XLA Ops:
  0.6 1.7 %collective-permute-start = (f32[64,1024]{1,0:T(8,128)}, f32[64,1024]{1,0:T(8,128)S(1)}, u32[]{:S(2)}, u32[]{:S(2)}) collective-permute-start(f32[64,1024]{1,0:T(8,128)} %bitcast.14), channel_id=1, source_target_pairs={{0,2},{1,3},{2,0},{3,1},{4,6},{5,7},{6,4},{7,5},{8,10},{9,11},{10,... | collective-permute-start | bytes 786440 | tf_op jit(solution)/shard_map/ppermute | solution.py:312
  2.4 0.9 %copy-done.6 = f32[1,64,1024]{2,1,0:T(8,128)S(1)} copy-done((f32[1,64,1024]{2,1,0:T(8,128)S(1)}, f32[1,64,1024]{2,1,0:T(8,128)}, u32[]{:S(2)}) %copy-start.6) | copy-done | bytes 262168
  3.3 0.8 %blocks_kernel.1.refs_7_ = f32[512,128]{1,0:T(8,128)} custom-call(f32[64,1024]{1,0:T(8,128)S(1)} %bitcast.18), custom_call_target="tpu_custom_call" | custom-call | tf_op jit(solution)/shard_map/blocks_kernel/pallas_call | solution.py:298
  4.1 8.0 %all-to-all-start = ((f32[16,32,128]{2,1,0:T(8,128)}), f32[16,32,128]{2,1,0:T(8,128)S(1)}, u32[]{:S(2)}, u32[]{:S(2)}) async-start(f32[16,32,128]{2,1,0:T(8,128)} %bitcast.4), calls=%async_computation | async-start | bytes 524288 | tf_op jit(solution)/shard_map/all_to_all | solution.py:316
  12.1 0.5 collective-permute-start.1
  12.7 0.1 pad_add_fusion.refs_0_
  12.8 0.6 copy-done.10
  13.4 1.4 %spectrum_kernel.1 = (f32[512,256]{1,0:T(8,128)S(1)}, f32[16,128]{1,0:T(8,128)S(1)}) custom-call(s32[2]{0:T(128)S(1)} %pad_add_fusion.refs_0_, f32[3,64]{1,0:T(4,128)S(1)} %copy-done.10, f32[4]{0:T(128)S(1)} %copy-done.11, f32[4,16384]{1,0:T(4,128)S(1)} %copy-done.8, bf16[256,384]{1,0:T(8,128)(2,1)S(1)} %copy-done.3, bf16[768,256]{1,0:T(8,128)(2,1)S(1)} %copy-done, ...), custom_call_target="tpu_custom_call" | custom-call | tf_op jit(solution)/shard_map/spectrum_kernel/pallas_call | solution.py:298
  14.8 1.4 %collective-permute-done.1.refs_2_ = f32[64,128]{1,0:T(8,128)S(1)} collective-permute-done((f32[64,128]{1,0:T(8,128)S(1)}, f32[64,128]{1,0:T(8,128)S(1)}, u32[]{:S(2)}, u32[]{:S(2)}) %collective-permute-start.1) | collective-permute-done | bytes 32800 | tf_op jit(solution)/shard_map/ppermute | solution.py:312
  16.2 0.7 %weights_kernel.1 = (bf16[128,384]{1,0:T(8,128)(2,1)S(1)}, bf16[128,384]{1,0:T(8,128)(2,1)S(1)}) custom-call(s32[2]{0:T(128)S(1)} %pad_add_fusion.refs_0_, f32[64,256]{1,0:T(8,128)S(1)} %bitcast.23, f32[64,128]{1,0:T(8,128)S(1)} %collective-permute-done.1.refs_2_, bf16[128,768]{1,0:T(8,128)(2,1)S(1)} %copy-done.4, bf16[768,256]{1,0:T(8,128)(2,1)S(1)} %copy-done.1, ...), custom_call_target="tpu_custom_call" | custom-call | tf_op jit(solution)/shard_map/weights_kernel/pallas_call | solution.py:298
  16.9 3.9 %all-to-all-done.refs_3_.refs_1_.refs_2_ = f32[16,32,128]{2,1,0:T(8,128)S(1)} async-done(((f32[16,32,128]{2,1,0:T(8,128)}), f32[16,32,128]{2,1,0:T(8,128)S(1)}, u32[]{:S(2)}, u32[]{:S(2)}) %all-to-all-start) | async-done | bytes 262176 | tf_op jit(solution)/shard_map/all_to_all | solution.py:316
  20.8 0.0 collective-permute-done.refs_1_.refs_3_
  20.8 0.3 grad_act_kernel.1
  21.1 0.1 collective-permute-start.2
  21.2 1.7 %forward_kernel.1 = (f32[512,256]{1,0:T(8,128)S(1)}, f32[4,128,128]{2,1,0:T(8,128)S(1)}, f32[4,128,128]{2,1,0:T(8,128)S(1)}, f32[16,64,128]{2,1,0:T(8,128)S(1)}) custom-call(f32[16,128]{1,0:T(8,128)S(1)} %get-tuple-element.31.refs_0_, f32[16,32,128]{2,1,0:T(8,128)S(1)} %all-to-all-done.refs_3_.refs_1_.refs_2_, ...), custom_call_target="tpu_custom_call" | custom-call | tf_op jit(solution)/shard_map/forward_kernel/pallas_call | solution.py:298
  22.9 0.0 collective-permute-done.2.refs_2_
  22.9 0.1 join_kernel.1
  23.0 15.5 %all_to_all.15.refs_1_ = f32[16,64,128]{2,1,0:T(8,128)S(1)} all-to-all(f32[16,64,128]{2,1,0:T(8,128)S(1)} %join_kernel.1), channel_id=1, replica_groups=mesh['dp'=2,'seq'=16,'chan'=4] {'seq'}, dimensions={0} | all-to-all | bytes 1048576 | tf_op jit(solution)/shard_map/all_to_all | solution.py:316
  38.5 0.1 collective-permute-start.3
  38.6 0.0 copy-start.7
  38.6 0.4 slope_kernel.1
  39.0 1.1 %collective-permute-done.3.refs_1_ = f32[512,128]{1,0:T(8,128)S(1)} collective-permute-done((f32[512,128]{1,0:T(8,128)S(1)}, f32[512,128]{1,0:T(8,128)S(1)}, u32[]{:S(2)}, u32[]{:S(2)}) %collective-permute-start.3) | collective-permute-done | bytes 262176 | tf_op jit(solution)/shard_map/ppermute | solution.py:312
  40.1 0.6 tail_kernel.1
  40.7 3.0 %collective-permute-start.6 = (f32[72,128]{1,0:T(8,128)S(1)}, f32[72,128]{1,0:T(8,128)S(1)}, u32[]{:S(2)}, u32[]{:S(2)}) collective-permute-start(f32[72,128]{1,0:T(8,128)S(1)} %get-tuple-element.43.refs_8_.refs_0_), channel_id=1, source_target_pairs={{0,64},{1,65},{2,66},{3,67},{64,0},{65,1},{66,2},{67,3},{4,68},{5,... | collective-permute-start | bytes 110600 | tf_op jit(solution)/shard_map/ppermute | solution.py:312
  43.7 0.2 collective-permute-start.8
  43.9 0.4 collective-permute-start.7
  44.3 2.5 %backward_kernel.1 = (f32[16,32,128]{2,1,0:T(8,128)}, f32[4,16384]{1,0:T(4,128)S(1)}) custom-call(f32[4,128,128]{2,1,0:T(8,128)S(1)} %get-tuple-element.39.refs_0_, f32[512,256]{1,0:T(8,128)S(1)} %get-tuple-element.40.refs_1_, f32[512,256]{1,0:T(8,128)S(1)} %get-tuple-element.32.refs_5_.refs_2_, bf16[256,384]{1,0:T(8,128)(2,1)S(1)} %copy-done.3, ...), custom_call_target="tpu_custom_call" | custom-call | tf_op jit(solution)/shard_map/backward_kernel/pallas_call | solution.py:298
  46.8 2.0 %collective-permute-done.8.refs_3_ = f32[64,128]{1,0:T(8,128)S(1)} collective-permute-done((f32[64,128]{1,0:T(8,128)S(1)}, f32[64,128]{1,0:T(8,128)S(1)}, u32[]{:S(2)}, u32[]{:S(2)}) %collective-permute-start.8) | collective-permute-done | bytes 32800 | tf_op jit(solution)/shard_map/ppermute | solution.py:312
  48.8 0.0 collective-permute-done.7.refs_2_
  48.8 0.0 collective-permute-done.6.refs_1_
  48.8 0.9 %collective-permute-start.11 = (f32[136,128]{1,0:T(8,128)S(1)}, f32[136,128]{1,0:T(8,128)S(1)}, u32[]{:S(2)}, u32[]{:S(2)}) collective-permute-start(f32[136,128]{1,0:T(8,128)S(1)} %merge_kernel.1), channel_id=1, source_target_pairs={{0,32},{4,36},{8,40},{12,44},{16,48},{20,52},{24,56},{28,60},{32,0... | collective-permute-start | bytes 208904 | tf_op jit(solution)/shard_map/ppermute | solution.py:312
  49.8 1.2 %collective-permute-start.10 = (f32[136,128]{1,0:T(8,128)S(1)}, f32[136,128]{1,0:T(8,128)S(1)}, u32[]{:S(2)}, u32[]{:S(2)}) collective-permute-start(f32[136,128]{1,0:T(8,128)S(1)} %merge_kernel.1), channel_id=1, source_target_pairs={{0,48},{4,52},{8,56},{12,60},{16,32},{20,36},{24,40},{28,44},{32,1... | collective-permute-start | bytes 208904 | tf_op jit(solution)/shard_map/ppermute | solution.py:312
  51.0 1.4 %collective-permute-start.9 = (f32[136,128]{1,0:T(8,128)S(1)}, f32[136,128]{1,0:T(8,128)S(1)}, u32[]{:S(2)}, u32[]{:S(2)}) collective-permute-start(f32[136,128]{1,0:T(8,128)S(1)} %merge_kernel.1), channel_id=1, source_target_pairs={{0,16},{4,20},{8,24},{12,28},{16,0},{20,4},{24,8},{28,12},{32,48},... | collective-permute-start | bytes 208904 | tf_op jit(solution)/shard_map/ppermute | solution.py:312
  52.4 2.1 %collective-permute-start.5 = (f32[4,16384]{1,0:T(4,128)S(1)}, f32[4,16384]{1,0:T(4,128)S(1)}, u32[]{:S(2)}, u32[]{:S(2)}) collective-permute-start(f32[4,16384]{1,0:T(4,128)S(1)} %get-tuple-element.47.refs_4_), channel_id=1, source_target_pairs={{0,64},{64,0},{1,65},{65,1},{2,66},{66,2},{3,67},{67,3},{4,68},{68... | collective-permute-start | bytes 786440 | tf_op jit(solution)/shard_map/ppermute | solution.py:312
  54.5 4.3 %all-to-all-start.2 = ((f32[16,32,128]{2,1,0:T(8,128)}), f32[16,32,128]{2,1,0:T(8,128)S(1)}, u32[]{:S(2)}, u32[]{:S(2)}) async-start(f32[16,32,128]{2,1,0:T(8,128)} %get-tuple-element.44), calls=%async_computation.2 | async-start | bytes 524288 | tf_op jit(solution)/shard_map/all_to_all | solution.py:316
  58.8 0.9 %collective-permute-start.4 = (f32[64,1024]{1,0:T(8,128)S(1)}, f32[64,1024]{1,0:T(8,128)S(1)}, u32[]{:S(2)}, u32[]{:S(2)}) collective-permute-start(f32[64,1024]{1,0:T(8,128)S(1)} %get-tuple-element.46), channel_id=1, source_target_pairs={{0,2},{1,3},{2,0},{3,1},{4,6},{5,7},{6,4},{7,5},{8,10},{9,11},{10,... | collective-permute-start | bytes 786440 | tf_op jit(solution)/shard_map/ppermute | solution.py:312
  59.7 0.0 collective-permute-done.11
  59.7 0.0 collective-permute-done.10
  59.7 0.0 collective-permute-done.9
  59.7 3.4 %collective-permute-start.14 = (f32[136,128]{1,0:T(8,128)S(1)}, f32[136,128]{1,0:T(8,128)S(1)}, u32[]{:S(2)}, u32[]{:S(2)}) collective-permute-start(f32[136,128]{1,0:T(8,128)S(1)} %add_add_fusion.refs_1_), channel_id=1, source_target_pairs={{0,8},{4,12},{8,0},{12,4},{16,24},{20,28},{24,16},{28,20},{32,40},... | collective-permute-start | bytes 208904 | tf_op jit(solution)/shard_map/ppermute | solution.py:312
  63.1 1.2 %collective-permute-start.13 = (f32[136,128]{1,0:T(8,128)S(1)}, f32[136,128]{1,0:T(8,128)S(1)}, u32[]{:S(2)}, u32[]{:S(2)}) collective-permute-start(f32[136,128]{1,0:T(8,128)S(1)} %add_add_fusion.refs_1_), channel_id=1, source_target_pairs={{0,12},{4,8},{8,4},{12,0},{16,28},{20,24},{24,20},{28,16},{32,44},... | collective-permute-start | bytes 208904 | tf_op jit(solution)/shard_map/ppermute | solution.py:312
  64.3 0.0 collective-permute-start.12
  64.3 3.9 %all-to-all-done.2 = f32[16,32,128]{2,1,0:T(8,128)S(1)} async-done(((f32[16,32,128]{2,1,0:T(8,128)}), f32[16,32,128]{2,1,0:T(8,128)S(1)}, u32[]{:S(2)}, u32[]{:S(2)}) %all-to-all-start.2) | async-done | bytes 262176 | tf_op jit(solution)/shard_map/all_to_all | solution.py:316
  68.2 0.0 collective-permute-done.4.refs_3_
  68.2 0.0 collective-permute-done.5.refs_5_
  68.2 1.0 %finish_kernel.1 = (f32[64,1024]{1,0:T(8,128)}, f32[64,1024]{1,0:T(8,128)}, f32[4,16384]{1,0:T(4,128)}, f32[8,128]{1,0:T(8,128)S(1)}) custom-call(f32[64,1024]{1,0:T(8,128)S(1)} %bitcast.17, f32[512,128]{1,0:T(8,128)S(1)} %bitcast.20, f32[64,1024]{1,0:T(8,128)S(1)} %get-tuple-element.45.refs_2_, f32[64,1024]{1,0:T(8,128)S(1)} %collective-permute-done.4.refs_3_, ...), custom_call_target="tpu_custom_call" | custom-call | tf_op jit(solution)/shard_map/finish_kernel/pallas_call | solution.py:298
  69.2 0.0 collective-permute-done.14.refs_4_
  69.2 0.7 %final_kernel.1 = (f32[64,256]{1,0:T(8,128)}, f32[3,64]{1,0:T(4,128)}, f32[1,4]{1,0:T(1,128)}) custom-call(f32[16,128]{1,0:T(8,128)S(1)} %get-tuple-element.31.refs_0_, f32[136,128]{1,0:T(8,128)S(1)} %add_add_fusion.refs_1_, f32[136,128]{1,0:T(8,128)S(1)} %collective-permute-done.12.refs_2_, f32[136,128]{1,0:T(8,128)S(1)} %collective-permute-done.13.refs_3_, ...), custom_call_target="tpu_custom_call" | custom-call | tf_op jit(solution)/shard_map/final_kernel/pallas_call | solution.py:298
  (27 shorter events, 0.1 us)
Async XLA Ops:
  0.6 20.2 %collective-permute-start = (f32[64,1024]{1,0:T(8,128)}, f32[64,1024]{1,0:T(8,128)S(1)}, u32[]{:S(2)}, u32[]{:S(2)}) collective-permute-start(f32[64,1024]{1,0:T(8,128)} %bitcast.14), channel_id=1, source_target_pairs={{0,2},{1,3},{2,0},{3,1},{4,6},{5,7},{6,4},{7,5},{8,10},{9,11},{10,... | collective-permute-start | bytes 786440 | tf_op jit(solution)/shard_map/ppermute | solution.py:312
  2.4 0.9 %copy-start.6 = (f32[1,64,1024]{2,1,0:T(8,128)S(1)}, f32[1,64,1024]{2,1,0:T(8,128)}, u32[]{:S(2)}) copy-start(f32[1,64,1024]{2,1,0:T(8,128)} %param.11) | copy-start | bytes 786436
  3.3 8.8 %copy-start.9 = (f32[256,64]{0,1:T(8,128)S(1)}, f32[256,64]{0,1:T(8,128)}, u32[]{:S(2)}) copy-start(f32[256,64]{0,1:T(8,128)} %param.16) | copy-start | bytes 196612
  3.3 9.4 %copy-start.5 = (f32[2,128,128]{2,1,0:T(8,128)S(1)}, f32[2,128,128]{2,1,0:T(8,128)}, u32[]{:S(2)}) copy-start(f32[2,128,128]{2,1,0:T(8,128)} %constant.31.clone.refs_6_.refs_7_) | copy-start | bytes 393220
  3.3 9.4 %copy-start.8 = (f32[4,16384]{1,0:T(4,128)S(1)}, f32[4,16384]{1,0:T(4,128)}, u32[]{:S(2)}) copy-start(f32[4,16384]{1,0:T(4,128)} %refs_3_.4) | copy-start | bytes 786436
  4.1 8.7 %copy-start = (bf16[768,256]{1,0:T(8,128)(2,1)S(1)}, bf16[768,256]{1,0:T(8,128)(2,1)}, u32[]{:S(2)}) copy-start(bf16[768,256]{1,0:T(8,128)(2,1)} %constant.28.clone.refs_5_.refs_4_) | copy-start | bytes 1179652
  4.1 8.7 %copy-start.3 = (bf16[256,384]{1,0:T(8,128)(2,1)S(1)}, bf16[256,384]{1,0:T(8,128)(2,1)}, u32[]{:S(2)}) copy-start(bf16[256,384]{1,0:T(8,128)(2,1)} %constant.27.clone.refs_4_.refs_3_) | copy-start | bytes 589828
  4.1 16.7 %all-to-all-start = ((f32[16,32,128]{2,1,0:T(8,128)}), f32[16,32,128]{2,1,0:T(8,128)S(1)}, u32[]{:S(2)}, u32[]{:S(2)}) async-start(f32[16,32,128]{2,1,0:T(8,128)} %bitcast.4), calls=%async_computation | async-start | bytes 524288 | tf_op jit(solution)/shard_map/all_to_all | solution.py:316
  12.1 4.0 %collective-permute-start.1 = (f32[64,128]{1,0:T(8,128)S(1)}, f32[64,128]{1,0:T(8,128)S(1)}, u32[]{:S(2)}, u32[]{:S(2)}) collective-permute-start(f32[64,128]{1,0:T(8,128)S(1)} %dynamic-slice_bitcast_fusion), channel_id=1, source_target_pairs={{0,2},{1,3},{2,0},{3,1},{4,6},{5,7},{6,4},{7,5},{8,10},{9,11},{10,... | collective-permute-start | bytes 98312 | tf_op jit(solution)/shard_map/ppermute | solution.py:312
  12.7 0.7 copy-start.10
  12.7 0.7 copy-start.11
  13.4 2.8 %copy-start.1 = (bf16[768,256]{1,0:T(8,128)(2,1)S(1)}, bf16[768,256]{1,0:T(8,128)(2,1)}, u32[]{:S(2)}) copy-start(bf16[768,256]{1,0:T(8,128)(2,1)} %constant.30.clone.refs_4_.refs_6_) | copy-start | bytes 1179652
  13.4 2.8 %copy-start.4 = (bf16[128,768]{1,0:T(8,128)(2,1)S(1)}, bf16[128,768]{1,0:T(8,128)(2,1)}, u32[]{:S(2)}) copy-start(bf16[128,768]{1,0:T(8,128)(2,1)} %constant.29.clone.refs_3_.refs_5_) | copy-start | bytes 589828
  16.1 4.7 %copy-start.2 = (f32[1,64,1024]{2,1,0:T(8,128)S(1)}, f32[1,64,1024]{2,1,0:T(8,128)}, u32[]{:S(2)}) copy-start(f32[1,64,1024]{2,1,0:T(8,128)} %param.12) | copy-start | bytes 786436
  21.1 1.8 %collective-permute-start.2 = (f32[512,128]{1,0:T(8,128)S(1)}, f32[512,128]{1,0:T(8,128)S(1)}, u32[]{:S(2)}, u32[]{:S(2)}) collective-permute-start(f32[512,128]{1,0:T(8,128)S(1)} %get-tuple-element.36), channel_id=1, source_target_pairs={{0,1},{1,0},{2,3},{3,2},{4,5},{5,4},{6,7},{7,6},{8,9},{9,8},{10,11... | collective-permute-start | bytes 786440 | tf_op jit(solution)/shard_map/ppermute | solution.py:312
  38.5 1.6 %collective-permute-start.3 = (f32[512,128]{1,0:T(8,128)S(1)}, f32[512,128]{1,0:T(8,128)S(1)}, u32[]{:S(2)}, u32[]{:S(2)}) collective-permute-start(f32[512,128]{1,0:T(8,128)S(1)} %bitcast.21), channel_id=1, source_target_pairs={{0,1},{1,0},{2,3},{3,2},{4,5},{5,4},{6,7},{7,6},{8,9},{9,8},{10,11... | collective-permute-start | bytes 786440 | tf_op jit(solution)/shard_map/ppermute | solution.py:312
  38.6 1.5 %copy-start.7 = (f32[1,64,1024]{2,1,0:T(8,128)S(1)}, f32[1,64,1024]{2,1,0:T(8,128)}, u32[]{:S(2)}) copy-start(f32[1,64,1024]{2,1,0:T(8,128)} %param.11) | copy-start | bytes 786436
  40.7 8.1 %collective-permute-start.6 = (f32[72,128]{1,0:T(8,128)S(1)}, f32[72,128]{1,0:T(8,128)S(1)}, u32[]{:S(2)}, u32[]{:S(2)}) collective-permute-start(f32[72,128]{1,0:T(8,128)S(1)} %get-tuple-element.43.refs_8_.refs_0_), channel_id=1, source_target_pairs={{0,64},{1,65},{2,66},{3,67},{64,0},{65,1},{66,2},{67,3},{4,68},{5,... | collective-permute-start | bytes 110600 | tf_op jit(solution)/shard_map/ppermute | solution.py:312
  43.7 5.1 %collective-permute-start.8 = (f32[64,128]{1,0:T(8,128)S(1)}, f32[64,128]{1,0:T(8,128)S(1)}, u32[]{:S(2)}, u32[]{:S(2)}) collective-permute-start(f32[64,128]{1,0:T(8,128)S(1)} %get-tuple-element.51), channel_id=1, source_target_pairs={{0,66},{1,67},{2,64},{3,65},{64,2},{65,3},{66,0},{67,1},{4,70},{5,... | collective-permute-start | bytes 98312 | tf_op jit(solution)/shard_map/ppermute | solution.py:312
  43.9 4.9 %collective-permute-start.7 = (f32[64,128]{1,0:T(8,128)S(1)}, f32[64,128]{1,0:T(8,128)S(1)}, u32[]{:S(2)}, u32[]{:S(2)}) collective-permute-start(f32[64,128]{1,0:T(8,128)S(1)} %get-tuple-element.51), channel_id=1, source_target_pairs={{0,2},{1,3},{2,0},{3,1},{64,66},{65,67},{66,64},{67,65},{4,6},{5,7... | collective-permute-start | bytes 98312 | tf_op jit(solution)/shard_map/ppermute | solution.py:312
  48.8 10.8 %collective-permute-start.11 = (f32[136,128]{1,0:T(8,128)S(1)}, f32[136,128]{1,0:T(8,128)S(1)}, u32[]{:S(2)}, u32[]{:S(2)}) collective-permute-start(f32[136,128]{1,0:T(8,128)S(1)} %merge_kernel.1), channel_id=1, source_target_pairs={{0,32},{4,36},{8,40},{12,44},{16,48},{20,52},{24,56},{28,60},{32,0... | collective-permute-start | bytes 208904 | tf_op jit(solution)/shard_map/ppermute | solution.py:312
  49.8 9.9 %collective-permute-start.10 = (f32[136,128]{1,0:T(8,128)S(1)}, f32[136,128]{1,0:T(8,128)S(1)}, u32[]{:S(2)}, u32[]{:S(2)}) collective-permute-start(f32[136,128]{1,0:T(8,128)S(1)} %merge_kernel.1), channel_id=1, source_target_pairs={{0,48},{4,52},{8,56},{12,60},{16,32},{20,36},{24,40},{28,44},{32,1... | collective-permute-start | bytes 208904 | tf_op jit(solution)/shard_map/ppermute | solution.py:312
  51.0 8.7 %collective-permute-start.9 = (f32[136,128]{1,0:T(8,128)S(1)}, f32[136,128]{1,0:T(8,128)S(1)}, u32[]{:S(2)}, u32[]{:S(2)}) collective-permute-start(f32[136,128]{1,0:T(8,128)S(1)} %merge_kernel.1), channel_id=1, source_target_pairs={{0,16},{4,20},{8,24},{12,28},{16,0},{20,4},{24,8},{28,12},{32,48},... | collective-permute-start | bytes 208904 | tf_op jit(solution)/shard_map/ppermute | solution.py:312
  52.4 15.8 %collective-permute-start.5 = (f32[4,16384]{1,0:T(4,128)S(1)}, f32[4,16384]{1,0:T(4,128)S(1)}, u32[]{:S(2)}, u32[]{:S(2)}) collective-permute-start(f32[4,16384]{1,0:T(4,128)S(1)} %get-tuple-element.47.refs_4_), channel_id=1, source_target_pairs={{0,64},{64,0},{1,65},{65,1},{2,66},{66,2},{3,67},{67,3},{4,68},{68... | collective-permute-start | bytes 786440 | tf_op jit(solution)/shard_map/ppermute | solution.py:312
  54.5 13.7 %all-to-all-start.2 = ((f32[16,32,128]{2,1,0:T(8,128)}), f32[16,32,128]{2,1,0:T(8,128)S(1)}, u32[]{:S(2)}, u32[]{:S(2)}) async-start(f32[16,32,128]{2,1,0:T(8,128)} %get-tuple-element.44), calls=%async_computation.2 | async-start | bytes 524288 | tf_op jit(solution)/shard_map/all_to_all | solution.py:316
  58.8 9.4 %collective-permute-start.4 = (f32[64,1024]{1,0:T(8,128)S(1)}, f32[64,1024]{1,0:T(8,128)S(1)}, u32[]{:S(2)}, u32[]{:S(2)}) collective-permute-start(f32[64,1024]{1,0:T(8,128)S(1)} %get-tuple-element.46), channel_id=1, source_target_pairs={{0,2},{1,3},{2,0},{3,1},{4,6},{5,7},{6,4},{7,5},{8,10},{9,11},{10,... | collective-permute-start | bytes 786440 | tf_op jit(solution)/shard_map/ppermute | solution.py:312
  59.7 9.5 %collective-permute-start.14 = (f32[136,128]{1,0:T(8,128)S(1)}, f32[136,128]{1,0:T(8,128)S(1)}, u32[]{:S(2)}, u32[]{:S(2)}) collective-permute-start(f32[136,128]{1,0:T(8,128)S(1)} %add_add_fusion.refs_1_), channel_id=1, source_target_pairs={{0,8},{4,12},{8,0},{12,4},{16,24},{20,28},{24,16},{28,20},{32,40},... | collective-permute-start | bytes 208904 | tf_op jit(solution)/shard_map/ppermute | solution.py:312
  63.1 6.1 %collective-permute-start.13 = (f32[136,128]{1,0:T(8,128)S(1)}, f32[136,128]{1,0:T(8,128)S(1)}, u32[]{:S(2)}, u32[]{:S(2)}) collective-permute-start(f32[136,128]{1,0:T(8,128)S(1)} %add_add_fusion.refs_1_), channel_id=1, source_target_pairs={{0,12},{4,8},{8,4},{12,0},{16,28},{20,24},{24,20},{28,16},{32,44},... | collective-permute-start | bytes 208904 | tf_op jit(solution)/shard_map/ppermute | solution.py:312
  64.3 4.9 %collective-permute-start.12 = (f32[136,128]{1,0:T(8,128)S(1)}, f32[136,128]{1,0:T(8,128)S(1)}, u32[]{:S(2)}, u32[]{:S(2)}) collective-permute-start(f32[136,128]{1,0:T(8,128)S(1)} %add_add_fusion.refs_1_), channel_id=1, source_target_pairs={{0,4},{4,0},{8,12},{12,8},{16,20},{20,16},{24,28},{28,24},{32,36},... | collective-permute-start | bytes 208904 | tf_op jit(solution)/shard_map/ppermute | solution.py:312

commit v4 on v3

--- a/solution.py
+++ b/solution.py
@@ -135,6 +135,9 @@
     first, chan = 4 * place_at[0], place_at[1]
     result = jnp.where(line == 3, jnp.bitwise_and(chan, 1).astype(F32), 0.0)
     result = jnp.where(line == 4, lax.shift_right_logical(chan, 1).astype(F32), result)
+    for row, bit in ((5, 2), (6, 3), (7, 0), (12, 1)):
+        flag = jnp.bitwise_and(lax.shift_right_logical(place_at[0], bit), 1)
+        result = jnp.where(line == row, flag.astype(F32), result)
     result = jnp.where((line >= 8) & (line < 12) & (lane == first + line - 8), 1.0, result)
     for tap in range(3):
         for at in range(4):
@@ -222,20 +225,17 @@
 
 def backward_kernel(
     grads, spec, kernel_spec, into_rows, into_lanes, back_rows, back_lanes, twist,
-    grad_out, kernel_out, grad_in, rows, sem,
+    grad_in, kernel_out, rows,
 ):
     spectrum = forward([grads[at] for at in range(4)], into_rows, into_lanes, twist)
     result = backward(times_conj(spectrum, kernel_spec[...]), back_rows, back_lanes, twist)
     for at in range(4):
         grad_in[:, at * 8 : (at + 1) * 8, :] = result[at].reshape(16, 8, SIDE)
-    copy = pltpu.make_async_copy(grad_in, grad_out, sem)
-    copy.start()
     result = backward(times_conj(spectrum, spec[...]), back_rows, back_lanes, twist)
     for at in range(4):
         rows[at * SIDE : (at + 1) * SIDE, :] = result[at]
     for at in range(SIDE):
         kernel_out[:, at * SIDE : (at + 1) * SIDE] = rows[pl.ds(at, 4, stride=SIDE), :]
-    copy.wait()
 
 
 def tail_kernel(act, act_near, cot, cot_far, signal, weights, small, mine, theirs, out, out_far):
@@ -255,25 +255,53 @@
     out_far[...] = mixed[64:]
 
 
-def merge_kernel(mine, mine_far, theirs, theirs_far, out):
-    out[:64, :] = mine[:64, :] + mine_far[:64, :]
-    out[64:128, :] = theirs[...] + theirs_far[...]
-    out[128:, :] = mine[64:, :] + mine_far[64:, :]
-
-
-def finish_kernel(cotangent, grad_in, own, near, kernel_own, kernel_near, grad_inputs, outputs, grad_kernel, token):
-    for at in range(8):
-        lanes = slice(at * SIDE, (at + 1) * SIDE)
-        grad_inputs[:, lanes] = cotangent[:, lanes] + grad_in[pl.ds(at, 64, stride=8), :]
+def flag(gains, row, shape):
+    return jnp.broadcast_to(gains[row : row + 1, :], shape) > 0.5
+
+
+def relative(blocks, low, high):
+    blocks = [jnp.where(low, blocks[at ^ 1], blocks[at]) for at in range(4)]
+    return [jnp.where(high, blocks[at ^ 2], blocks[at]) for at in range(4)]
+
+
+def merge_kernel(gains, grad, mine, mine_far, theirs_far, theirs, out0, out1, out2, out3):
+    total = [
+        mine[:64, :] + mine_far[:64, :],
+        theirs[...] + theirs_far[...],
+        mine[64:, :] + mine_far[64:, :],
+    ]
+    shape = (SIDE, SIDE)
+    blocks = [grad[at * 4 : (at + 1) * 4].reshape(SIDE, SIDE) for at in range(4)]
+    blocks = relative(blocks, flag(gains, 5, shape), flag(gains, 6, shape))
+    for out, block in zip((out0, out1, out2, out3), blocks):
+        out[:64, :] = total[0]
+        out[64:128, :] = total[1]
+        out[128:136, :] = total[2]
+        out[136:, :] = block
+
+
+def sum_kernel(gains, in0, in2, in3, in1, out0, out1, out2, out3):
+    whole = in0[:136, :] + in1[:136, :] + in2[:136, :] + in3[:136, :]
+    outs = (out0, out1, out2, out3)
+    for out in outs:
+        out[:136, :] = whole
+    shape = (32, SIDE)
+    low, high = flag(gains, 7, shape), flag(gains, 12, shape)
+    for near, ref in enumerate((in0, in1, in2, in3)):
+        blocks = relative([ref[136 + 32 * at : 168 + 32 * at, :] for at in range(4)], low, high)
+        for out, block in zip(outs, blocks):
+            out[136 + 32 * near : 168 + 32 * near, :] = block
+
+
+def finish_kernel(own, near, kernel_own, kernel_near, outputs, grad_kernel, token):
     outputs[...] = own[...] + near[...]
     grad_kernel[...] = kernel_own[...] + kernel_near[...]
     token[...] = jnp.zeros_like(token)
 
 
-def final_kernel(gains, total0, total1, total2, total3, out, taps, skip):
-    core = jnp.broadcast_to(gains[3:4, :], (64, SIDE)) > 0.5
-    place = jnp.broadcast_to(gains[4:5, :], (64, SIDE)) > 0.5
-    whole = total0[...] + total1[...] + total2[...] + total3[...]
+def final_kernel(gains, cotangent, in0, in2, in3, in1, out, taps, skip, grad_inputs, rows):
+    core, place = flag(gains, 3, (64, SIDE)), flag(gains, 4, (64, SIDE))
+    whole = in0[:136, :] + in1[:136, :] + in2[:136, :] + in3[:136, :]
     near, far = [
         jnp.where(core, pltpu.roll(one, 64, 1), one) for one in (whole[:64], whole[64:128])
     ]
@@ -284,6 +312,17 @@
     line = lax.broadcasted_iota(jnp.int32, (4, SIDE), 0)
     lane = lax.broadcasted_iota(jnp.int32, (4, SIDE), 1)
     skip[...] = jnp.sum(jnp.where(line == lane, own, 0.0), axis=0, keepdims=True)[:, :4]
+    shape = (SIDE, SIDE)
+    by_x = relative([ref[136:, :] for ref in (in0, in1, in2, in3)], flag(gains, 7, shape), flag(gains, 12, shape))
+    shape = (32, SIDE)
+    low, high = flag(gains, 5, shape), flag(gains, 6, shape)
+    for x, column in enumerate(by_x):
+        column = relative([column[32 * at : 32 * at + 32] for at in range(4)], low, high)
+        for z in range(4):
+            rows[(4 * z + x) * 32 : (4 * z + x + 1) * 32, :] = column[z]
+    for at in range(8):
+        lanes = slice(at * SIDE, (at + 1) * SIDE)
+        grad_inputs[:, lanes] = cotangent[:, lanes] + rows[pl.ds(at, 64, stride=8), :]
 
 
 def call(kernel, outs, *args, scalars=0, far=(), far_outs=(), scratch=(), after=(), aliases=()):
@@ -369,22 +408,25 @@
         backward_kernel,
         [(16, 32, SIDE), (4, LENGTH)],
         grads, spec, kernel_spec, into_rows, into_lanes, back_rows, back_lanes, twist,
-        far_outs=(0,), after=[mine], scratch=[(16, 32, SIDE), (512, SIDE), pltpu.SemaphoreType.DMA],
+        after=[mine], scratch=[(512, SIDE)],
     )
     both = ("dp", "chan")
-    total = call(
-        merge_kernel, [(136, SIDE)], mine, swapped(mine, both, 4), swapped(theirs, both, 2), swapped(theirs, both, 6),
-        after=[kernel_local],
-    )
-    grad_in = turned(grad_long).reshape(512, SIDE)
-    grad_inputs, outputs, grad_kernel, token = call(
-        finish_kernel, [(64, 1024), (64, 1024), (4, LENGTH), (8, SIDE)],
-        grad_out, grad_in, out_own, swapped(out_far, "chan", 2), kernel_local, swapped(kernel_local, "dp", 1),
-    )
-    total = total + swapped(total, "seq", 4) + swapped(total, "seq", 12) + swapped(total, "seq", 8)
-    grad_mix, grad_conv, grad_skip = call(
-        final_kernel, [(64, 256), (3, 64), (1, 4)], gains, total, *(swapped(total, "seq", at) for at in (1, 3, 2)),
-        after=[token],
+    far_theirs = [swapped(theirs, both, flip) for flip in (6, 2)]
+    sends = call(
+        merge_kernel, [(264, SIDE)] * 4, gains, grad_long, mine, swapped(mine, both, 4), *far_theirs
+    )
+    sends = call(
+        sum_kernel, [(264, SIDE)] * 4,
+        gains, sends[0], *(swapped(sends[at], "seq", 4 * at) for at in (2, 3, 1)),
+    )
+    outputs, grad_kernel, token = call(
+        finish_kernel, [(64, 1024), (4, LENGTH), (8, SIDE)],
+        out_own, swapped(out_far, "chan", 2), kernel_local, swapped(kernel_local, "dp", 1),
+    )
+    grad_mix, grad_conv, grad_skip, grad_inputs = call(
+        final_kernel, [(64, 256), (3, 64), (1, 4), (64, 1024)],
+        gains, grad_out, sends[0], *(swapped(sends[at], "seq", at) for at in (2, 3, 1)),
+        scratch=[(512, SIDE)], after=[token],
     )
     return (outputs[None], grad_inputs[None], grad_kernel, grad_skip[0], grad_mix.T, grad_conv)
 

time: 70.4 us -> 67.4 us (0.957)
  starting transfers between devices: 29.4 us -> 24.3 us
  waiting for transfers between devices: 12.4 us -> 14.9 us
    ppermute x15, waiting for transfers between devices: 4.54 us -> 11 us  [swapped(): return lax.ppermute(value, axes, [(at, at ^ flip) for at in range(count)])]
    all_to_all x2 -> x1, starting transfers between devices: 12.3 us -> 8.01 us  [turned(): return lax.all_to_all(value, 'seq', 0, 0, tiled=True)]
    all_to_all x2 -> x1, waiting for transfers between devices: 7.84 us -> 3.93 us  [turned(): return lax.all_to_all(value, 'seq', 0, 0, tiled=True)]
    ppermute x15, starting transfers between devices: 17.1 us -> 16.3 us  [swapped(): return lax.ppermute(value, axes, [(at, at ^ flip) for at in range(count)])]
    pallas_call x12 -> x13, Pallas kernels: 10.1 us -> 9.89 us  [call(): pl.pallas_call(body, out_shape=shapes if len(shapes) > 1 else shapes[0],...]
  transfers between devices with their start and end apart: 17 -> 16, of which waited for: 5 -> 10; matrix products, arithmetic and copies ran while one was open for 0% -> 0% of each run, Pallas kernels for 12% -> 12%
where the time goes in v4:
time: 67.4 us; the launch traced here: 67.1 us
  starting transfers between devices  24.3 us (36%)
  blocking collectives  15.5 us (23%)
  waiting for transfers between devices  14.9 us (22%)
  Pallas kernels  9.89 us (15%)
  local copies, waits for them, and re-layouts  1.61 us (2%)
  between operations  0.8 us (1%)
    ppermute x15, starting transfers between devices, swapped(): return lax.ppermute(value, axes, [(at, at ^ flip) for at in range(count)])  16.3 us
    all_to_all x1, blocking collectives, turned(): return lax.all_to_all(value, 'seq', 0, 0, tiled=True)  15.5 us
    ppermute x15, waiting for transfers between devices, swapped(): return lax.ppermute(value, axes, [(at, at ^ flip) for at in range(count)])  11 us
    pallas_call x13, Pallas kernels, call(): pl.pallas_call(body, out_shape=shapes if len(shapes) > 1 else shapes[0],...  9.89 us
    all_to_all x1, starting transfers between devices, turned(): return lax.all_to_all(value, 'seq', 0, 0, tiled=True)  8.01 us
    all_to_all x1, waiting for transfers between devices, turned(): return lax.all_to_all(value, 'seq', 0, 0, tiled=True)  3.93 us
    unnamed x24, local copies, waits for them, and re-layouts  1.58 us
  transfers between devices with their start and end apart: 16, of which 10 were waited for; matrix products, arithmetic and copies ran while one was open for 0% of the time, Pallas kernels for 12%

profile of v4, /device:TPU:0, one launch (start us, length us, event | category | flops | bytes accessed | tf_op | source)
XLA Modules:
  0.0 67.1 jit_solution(6001920690243651639)
XLA Ops:
  0.6 1.7 %collective-permute-start = (f32[64,1024]{1,0:T(8,128)}, f32[64,1024]{1,0:T(8,128)S(1)}, u32[]{:S(2)}, u32[]{:S(2)}) collective-permute-start(f32[64,1024]{1,0:T(8,128)} %bitcast.13), channel_id=1, source_target_pairs={{0,2},{1,3},{2,0},{3,1},{4,6},{5,7},{6,4},{7,5},{8,10},{9,11},{10,... | collective-permute-start | bytes 786440 | tf_op jit(solution)/shard_map/ppermute | solution.py:351
  2.4 0.9 %copy-done.6 = f32[1,64,1024]{2,1,0:T(8,128)S(1)} copy-done((f32[1,64,1024]{2,1,0:T(8,128)S(1)}, f32[1,64,1024]{2,1,0:T(8,128)}, u32[]{:S(2)}) %copy-start.6) | copy-done | bytes 262168
  3.3 0.8 %blocks_kernel.1.refs_7_ = f32[512,128]{1,0:T(8,128)} custom-call(f32[64,1024]{1,0:T(8,128)S(1)} %bitcast.17), custom_call_target="tpu_custom_call" | custom-call | tf_op jit(solution)/shard_map/blocks_kernel/pallas_call | solution.py:337
  4.1 8.0 %all-to-all-start = ((f32[16,32,128]{2,1,0:T(8,128)}), f32[16,32,128]{2,1,0:T(8,128)S(1)}, u32[]{:S(2)}, u32[]{:S(2)}) async-start(f32[16,32,128]{2,1,0:T(8,128)} %bitcast.3), calls=%async_computation | async-start | bytes 524288 | tf_op jit(solution)/shard_map/all_to_all | solution.py:355
  12.1 0.5 collective-permute-start.1
  12.7 0.1 pad_add_fusion.refs_0_
  12.8 0.6 copy-done.10
  13.4 1.4 %spectrum_kernel.1 = (f32[512,256]{1,0:T(8,128)S(1)}, f32[16,128]{1,0:T(8,128)S(1)}) custom-call(s32[2]{0:T(128)S(1)} %pad_add_fusion.refs_0_, f32[3,64]{1,0:T(4,128)S(1)} %copy-done.10, f32[4]{0:T(128)S(1)} %copy-done.11, f32[4,16384]{1,0:T(4,128)S(1)} %copy-done.8, bf16[256,384]{1,0:T(8,128)(2,1)S(1)} %copy-done.3, bf16[768,256]{1,0:T(8,128)(2,1)S(1)} %copy-done, ...), custom_call_target="tpu_custom_call" | custom-call | tf_op jit(solution)/shard_map/spectrum_kernel/pallas_call | solution.py:337
  14.8 1.4 %collective-permute-done.1.refs_2_ = f32[64,128]{1,0:T(8,128)S(1)} collective-permute-done((f32[64,128]{1,0:T(8,128)S(1)}, f32[64,128]{1,0:T(8,128)S(1)}, u32[]{:S(2)}, u32[]{:S(2)}) %collective-permute-start.1) | collective-permute-done | bytes 32800 | tf_op jit(solution)/shard_map/ppermute | solution.py:351
  16.2 0.7 %weights_kernel.1 = (bf16[128,384]{1,0:T(8,128)(2,1)S(1)}, bf16[128,384]{1,0:T(8,128)(2,1)S(1)}) custom-call(s32[2]{0:T(128)S(1)} %pad_add_fusion.refs_0_, f32[64,256]{1,0:T(8,128)S(1)} %bitcast.21, f32[64,128]{1,0:T(8,128)S(1)} %collective-permute-done.1.refs_2_, bf16[128,768]{1,0:T(8,128)(2,1)S(1)} %copy-done.4, bf16[768,256]{1,0:T(8,128)(2,1)S(1)} %copy-done.1, ...), custom_call_target="tpu_custom_call" | custom-call | tf_op jit(solution)/shard_map/weights_kernel/pallas_call | solution.py:337
  16.9 3.9 %all-to-all-done.refs_3_.refs_1_.refs_2_ = f32[16,32,128]{2,1,0:T(8,128)S(1)} async-done(((f32[16,32,128]{2,1,0:T(8,128)}), f32[16,32,128]{2,1,0:T(8,128)S(1)}, u32[]{:S(2)}, u32[]{:S(2)}) %all-to-all-start) | async-done | bytes 262176 | tf_op jit(solution)/shard_map/all_to_all | solution.py:355
  20.8 0.0 collective-permute-done.refs_1_.refs_3_
  20.8 0.3 grad_act_kernel.1
  21.1 0.1 collective-permute-start.2
  21.2 1.7 %forward_kernel.1 = (f32[512,256]{1,0:T(8,128)S(1)}, f32[4,128,128]{2,1,0:T(8,128)S(1)}, f32[4,128,128]{2,1,0:T(8,128)S(1)}, f32[16,64,128]{2,1,0:T(8,128)S(1)}) custom-call(f32[16,128]{1,0:T(8,128)S(1)} %get-tuple-element.39.refs_0_, f32[16,32,128]{2,1,0:T(8,128)S(1)} %all-to-all-done.refs_3_.refs_1_.refs_2_, ...), custom_call_target="tpu_custom_call" | custom-call | tf_op jit(solution)/shard_map/forward_kernel/pallas_call | solution.py:337
  22.9 0.0 collective-permute-done.2.refs_2_
  23.0 0.1 join_kernel.1
  23.0 15.5 %all_to_all.10.refs_1_ = f32[16,64,128]{2,1,0:T(8,128)S(1)} all-to-all(f32[16,64,128]{2,1,0:T(8,128)S(1)} %join_kernel.1), channel_id=1, replica_groups=mesh['dp'=2,'seq'=16,'chan'=4] {'seq'}, dimensions={0} | all-to-all | bytes 1048576 | tf_op jit(solution)/shard_map/all_to_all | solution.py:355
  38.5 0.1 collective-permute-start.3
  38.6 0.0 copy-start.7
  38.6 0.4 slope_kernel.1
  39.0 1.1 %collective-permute-done.3.refs_1_ = f32[512,128]{1,0:T(8,128)S(1)} collective-permute-done((f32[512,128]{1,0:T(8,128)S(1)}, f32[512,128]{1,0:T(8,128)S(1)}, u32[]{:S(2)}, u32[]{:S(2)}) %collective-permute-start.3) | collective-permute-done | bytes 262176 | tf_op jit(solution)/shard_map/ppermute | solution.py:351
  40.1 0.6 tail_kernel.1
  40.7 3.0 %collective-permute-start.6 = (f32[72,128]{1,0:T(8,128)S(1)}, f32[72,128]{1,0:T(8,128)S(1)}, u32[]{:S(2)}, u32[]{:S(2)}) collective-permute-start(f32[72,128]{1,0:T(8,128)S(1)} %get-tuple-element.53.refs_8_.refs_2_), channel_id=1, source_target_pairs={{0,64},{1,65},{2,66},{3,67},{64,0},{65,1},{66,2},{67,3},{4,68},{5,... | collective-permute-start | bytes 110600 | tf_op jit(solution)/shard_map/ppermute | solution.py:351
  43.7 0.1 collective-permute-start.8
  43.8 1.1 %collective-permute-start.7 = (f32[64,128]{1,0:T(8,128)S(1)}, f32[64,128]{1,0:T(8,128)S(1)}, u32[]{:S(2)}, u32[]{:S(2)}) collective-permute-start(f32[64,128]{1,0:T(8,128)S(1)} %get-tuple-element.57), channel_id=1, source_target_pairs={{0,66},{1,67},{2,64},{3,65},{64,2},{65,3},{66,0},{67,1},{4,70},{5,... | collective-permute-start | bytes 98312 | tf_op jit(solution)/shard_map/ppermute | solution.py:351
  44.9 2.2 %backward_kernel.1 = (f32[16,32,128]{2,1,0:T(8,128)S(1)}, f32[4,16384]{1,0:T(4,128)S(1)}) custom-call(f32[4,128,128]{2,1,0:T(8,128)S(1)} %get-tuple-element.51.refs_0_, f32[512,256]{1,0:T(8,128)S(1)} %get-tuple-element.52.refs_1_, f32[512,256]{1,0:T(8,128)S(1)} %get-tuple-element.40.refs_5_.refs_2_, bf16[256,384]{1,0:T(8,128)(2,1)S(1)} %copy-done.3, ...), custom_call_target="tpu_custom_call" | custom-call | tf_op jit(solution)/shard_map/backward_kernel/pallas_call | solution.py:337
  47.1 0.5 collective-permute-done.8.refs_5_
  47.6 1.4 %collective-permute-done.7.refs_4_ = f32[64,128]{1,0:T(8,128)S(1)} collective-permute-done((f32[64,128]{1,0:T(8,128)S(1)}, f32[64,128]{1,0:T(8,128)S(1)}, u32[]{:S(2)}, u32[]{:S(2)}) %collective-permute-start.7) | collective-permute-done | bytes 32800 | tf_op jit(solution)/shard_map/ppermute | solution.py:351
  49.0 0.0 collective-permute-done.6.refs_3_
  49.0 0.9 %collective-permute-start.9 = (f32[264,128]{1,0:T(8,128)S(1)}, f32[264,128]{1,0:T(8,128)S(1)}, u32[]{:S(2)}, u32[]{:S(2)}) collective-permute-start(f32[264,128]{1,0:T(8,128)S(1)} %get-tuple-element.59), channel_id=1, source_target_pairs={{0,32},{4,36},{8,40},{12,44},{16,48},{20,52},{24,56},{28,60},{32,0... | collective-permute-start | bytes 405512 | tf_op jit(solution)/shard_map/ppermute | solution.py:351
  50.0 1.2 %collective-permute-start.10 = (f32[264,128]{1,0:T(8,128)S(1)}, f32[264,128]{1,0:T(8,128)S(1)}, u32[]{:S(2)}, u32[]{:S(2)}) collective-permute-start(f32[264,128]{1,0:T(8,128)S(1)} %get-tuple-element.60), channel_id=1, source_target_pairs={{0,48},{4,52},{8,56},{12,60},{16,32},{20,36},{24,40},{28,44},{32,1... | collective-permute-start | bytes 405512 | tf_op jit(solution)/shard_map/ppermute | solution.py:351
  51.2 1.4 %collective-permute-start.11 = (f32[264,128]{1,0:T(8,128)S(1)}, f32[264,128]{1,0:T(8,128)S(1)}, u32[]{:S(2)}, u32[]{:S(2)}) collective-permute-start(f32[264,128]{1,0:T(8,128)S(1)} %get-tuple-element.61), channel_id=1, source_target_pairs={{0,16},{4,20},{8,24},{12,28},{16,0},{20,4},{24,8},{28,12},{32,48},... | collective-permute-start | bytes 405512 | tf_op jit(solution)/shard_map/ppermute | solution.py:351
  52.6 0.7 %collective-permute-start.4 = (f32[64,1024]{1,0:T(8,128)S(1)}, f32[64,1024]{1,0:T(8,128)S(1)}, u32[]{:S(2)}, u32[]{:S(2)}) collective-permute-start(f32[64,1024]{1,0:T(8,128)S(1)} %get-tuple-element.50), channel_id=1, source_target_pairs={{0,2},{1,3},{2,0},{3,1},{4,6},{5,7},{6,4},{7,5},{8,10},{9,11},{10,... | collective-permute-start | bytes 786440 | tf_op jit(solution)/shard_map/ppermute | solution.py:351
  53.3 1.8 %collective-permute-start.5 = (f32[4,16384]{1,0:T(4,128)S(1)}, f32[4,16384]{1,0:T(4,128)S(1)}, u32[]{:S(2)}, u32[]{:S(2)}) collective-permute-start(f32[4,16384]{1,0:T(4,128)S(1)} %get-tuple-element.54.refs_2_), channel_id=1, source_target_pairs={{0,64},{64,0},{1,65},{65,1},{2,66},{66,2},{3,67},{67,3},{4,68},{68... | collective-permute-start | bytes 786440 | tf_op jit(solution)/shard_map/ppermute | solution.py:351
  55.1 1.1 %collective-permute-done.9.refs_2_ = f32[264,128]{1,0:T(8,128)S(1)} collective-permute-done((f32[264,128]{1,0:T(8,128)S(1)}, f32[264,128]{1,0:T(8,128)S(1)}, u32[]{:S(2)}, u32[]{:S(2)}) %collective-permute-start.9) | collective-permute-done | bytes 135200 | tf_op jit(solution)/shard_map/ppermute | solution.py:351
  56.2 1.4 %collective-permute-done.10.refs_3_ = f32[264,128]{1,0:T(8,128)S(1)} collective-permute-done((f32[264,128]{1,0:T(8,128)S(1)}, f32[264,128]{1,0:T(8,128)S(1)}, u32[]{:S(2)}, u32[]{:S(2)}) %collective-permute-start.10) | collective-permute-done | bytes 135200 | tf_op jit(solution)/shard_map/ppermute | solution.py:351
  57.6 0.0 collective-permute-done.11.refs_4_
  57.6 1.0 %collective-permute-start.12 = (f32[264,128]{1,0:T(8,128)S(1)}, f32[264,128]{1,0:T(8,128)S(1)}, u32[]{:S(2)}, u32[]{:S(2)}) collective-permute-start(f32[264,128]{1,0:T(8,128)S(1)} %get-tuple-element.63), channel_id=1, source_target_pairs={{0,8},{4,12},{8,0},{12,4},{16,24},{20,28},{24,16},{28,20},{32,40},... | collective-permute-start | bytes 405512 | tf_op jit(solution)/shard_map/ppermute | solution.py:351
  58.6 2.3 %collective-permute-start.13 = (f32[264,128]{1,0:T(8,128)S(1)}, f32[264,128]{1,0:T(8,128)S(1)}, u32[]{:S(2)}, u32[]{:S(2)}) collective-permute-start(f32[264,128]{1,0:T(8,128)S(1)} %get-tuple-element.64), channel_id=1, source_target_pairs={{0,12},{4,8},{8,4},{12,0},{16,28},{20,24},{24,20},{28,16},{32,44},... | collective-permute-start | bytes 405512 | tf_op jit(solution)/shard_map/ppermute | solution.py:351
  60.9 0.3 collective-permute-start.14
  61.2 0.2 collective-permute-done.4.refs_1_
  61.3 3.4 %collective-permute-done.5.refs_3_ = f32[4,16384]{1,0:T(4,128)S(1)} collective-permute-done((f32[4,16384]{1,0:T(4,128)S(1)}, f32[4,16384]{1,0:T(4,128)S(1)}, u32[]{:S(2)}, u32[]{:S(2)}) %collective-permute-start.5) | collective-permute-done | bytes 262176 | tf_op jit(solution)/shard_map/ppermute | solution.py:351
  64.8 0.8 %finish_kernel.1 = (f32[64,1024]{1,0:T(8,128)}, f32[4,16384]{1,0:T(4,128)}, f32[8,128]{1,0:T(8,128)S(1)}) custom-call(f32[64,1024]{1,0:T(8,128)S(1)} %get-tuple-element.49.refs_0_, f32[64,1024]{1,0:T(8,128)S(1)} %collective-permute-done.4.refs_1_, f32[4,16384]{1,0:T(4,128)S(1)} %get-tuple-element.54.refs_2_, f32[4,16384]{1,0:T(4,128)S(1)} %collective-permute-done.5.refs_3_), custom_call_target="tpu_custom_call" | custom-call | tf_op jit(solution)/shard_map/finish_kernel/pallas_call | solution.py:337
  65.6 0.0 collective-permute-done.12.refs_3_
  65.6 0.6 collective-permute-done.13.refs_4_
  66.2 0.0 collective-permute-done.14.refs_5_
  66.2 0.9 %final_kernel.1 = (f32[64,256]{1,0:T(8,128)}, f32[3,64]{1,0:T(4,128)}, f32[1,4]{1,0:T(1,128)}, f32[64,1024]{1,0:T(8,128)}) custom-call(f32[16,128]{1,0:T(8,128)S(1)} %get-tuple-element.39.refs_0_, f32[64,1024]{1,0:T(8,128)S(1)} %bitcast.16, f32[264,128]{1,0:T(8,128)S(1)} %get-tuple-element.62.refs_2_, f32[264,128]{1,0:T(8,128)S(1)} %collective-permute-done.12.refs_3_, ...), custom_call_target="tpu_custom_call" | custom-call | tf_op jit(solution)/shard_map/final_kernel/pallas_call | solution.py:337
  (25 shorter events, 0.2 us)
Async XLA Ops:
  0.6 20.2 %collective-permute-start = (f32[64,1024]{1,0:T(8,128)}, f32[64,1024]{1,0:T(8,128)S(1)}, u32[]{:S(2)}, u32[]{:S(2)}) collective-permute-start(f32[64,1024]{1,0:T(8,128)} %bitcast.13), channel_id=1, source_target_pairs={{0,2},{1,3},{2,0},{3,1},{4,6},{5,7},{6,4},{7,5},{8,10},{9,11},{10,... | collective-permute-start | bytes 786440 | tf_op jit(solution)/shard_map/ppermute | solution.py:351
  2.4 0.9 %copy-start.6 = (f32[1,64,1024]{2,1,0:T(8,128)S(1)}, f32[1,64,1024]{2,1,0:T(8,128)}, u32[]{:S(2)}) copy-start(f32[1,64,1024]{2,1,0:T(8,128)} %param.11) | copy-start | bytes 786436
  3.3 8.8 %copy-start.9 = (f32[256,64]{0,1:T(8,128)S(1)}, f32[256,64]{0,1:T(8,128)}, u32[]{:S(2)}) copy-start(f32[256,64]{0,1:T(8,128)} %param.16) | copy-start | bytes 196612
  3.3 9.4 %copy-start.5 = (f32[2,128,128]{2,1,0:T(8,128)S(1)}, f32[2,128,128]{2,1,0:T(8,128)}, u32[]{:S(2)}) copy-start(f32[2,128,128]{2,1,0:T(8,128)} %constant.31.clone.refs_6_.refs_7_) | copy-start | bytes 393220
  3.3 9.4 %copy-start.8 = (f32[4,16384]{1,0:T(4,128)S(1)}, f32[4,16384]{1,0:T(4,128)}, u32[]{:S(2)}) copy-start(f32[4,16384]{1,0:T(4,128)} %refs_3_.4) | copy-start | bytes 786436
  4.1 8.7 %copy-start = (bf16[768,256]{1,0:T(8,128)(2,1)S(1)}, bf16[768,256]{1,0:T(8,128)(2,1)}, u32[]{:S(2)}) copy-start(bf16[768,256]{1,0:T(8,128)(2,1)} %constant.28.clone.refs_5_.refs_4_) | copy-start | bytes 1179652
  4.1 8.7 %copy-start.3 = (bf16[256,384]{1,0:T(8,128)(2,1)S(1)}, bf16[256,384]{1,0:T(8,128)(2,1)}, u32[]{:S(2)}) copy-start(bf16[256,384]{1,0:T(8,128)(2,1)} %constant.27.clone.refs_4_.refs_3_) | copy-start | bytes 589828
  4.1 16.7 %all-to-all-start = ((f32[16,32,128]{2,1,0:T(8,128)}), f32[16,32,128]{2,1,0:T(8,128)S(1)}, u32[]{:S(2)}, u32[]{:S(2)}) async-start(f32[16,32,128]{2,1,0:T(8,128)} %bitcast.3), calls=%async_computation | async-start | bytes 524288 | tf_op jit(solution)/shard_map/all_to_all | solution.py:355
  12.1 4.0 %collective-permute-start.1 = (f32[64,128]{1,0:T(8,128)S(1)}, f32[64,128]{1,0:T(8,128)S(1)}, u32[]{:S(2)}, u32[]{:S(2)}) collective-permute-start(f32[64,128]{1,0:T(8,128)S(1)} %dynamic-slice_bitcast_fusion), channel_id=1, source_target_pairs={{0,2},{1,3},{2,0},{3,1},{4,6},{5,7},{6,4},{7,5},{8,10},{9,11},{10,... | collective-permute-start | bytes 98312 | tf_op jit(solution)/shard_map/ppermute | solution.py:351
  12.7 0.7 %copy-start.10 = (f32[3,64]{1,0:T(4,128)S(1)}, f32[3,64]{1,0:T(4,128)}, u32[]{:S(2)}) copy-start(f32[3,64]{1,0:T(4,128)} %refs_1_.1) | copy-start | bytes 2308
  12.7 0.7 %copy-start.11 = (f32[4]{0:T(128)S(1)}, f32[4]{0:T(128)}, u32[]{:S(2)}) copy-start(f32[4]{0:T(128)} %refs_2_.1) | copy-start | bytes 52
  13.4 2.8 %copy-start.1 = (bf16[768,256]{1,0:T(8,128)(2,1)S(1)}, bf16[768,256]{1,0:T(8,128)(2,1)}, u32[]{:S(2)}) copy-start(bf16[768,256]{1,0:T(8,128)(2,1)} %constant.30.clone.refs_4_.refs_6_) | copy-start | bytes 1179652
  13.4 2.8 %copy-start.4 = (bf16[128,768]{1,0:T(8,128)(2,1)S(1)}, bf16[128,768]{1,0:T(8,128)(2,1)}, u32[]{:S(2)}) copy-start(bf16[128,768]{1,0:T(8,128)(2,1)} %constant.29.clone.refs_3_.refs_5_) | copy-start | bytes 589828
  16.1 4.7 %copy-start.2 = (f32[1,64,1024]{2,1,0:T(8,128)S(1)}, f32[1,64,1024]{2,1,0:T(8,128)}, u32[]{:S(2)}) copy-start(f32[1,64,1024]{2,1,0:T(8,128)} %param.12) | copy-start | bytes 786436
  21.1 1.8 %collective-permute-start.2 = (f32[512,128]{1,0:T(8,128)S(1)}, f32[512,128]{1,0:T(8,128)S(1)}, u32[]{:S(2)}, u32[]{:S(2)}) collective-permute-start(f32[512,128]{1,0:T(8,128)S(1)} %get-tuple-element.44), channel_id=1, source_target_pairs={{0,1},{1,0},{2,3},{3,2},{4,5},{5,4},{6,7},{7,6},{8,9},{9,8},{10,11... | collective-permute-start | bytes 786440 | tf_op jit(solution)/shard_map/ppermute | solution.py:351
  38.5 1.6 %collective-permute-start.3 = (f32[512,128]{1,0:T(8,128)S(1)}, f32[512,128]{1,0:T(8,128)S(1)}, u32[]{:S(2)}, u32[]{:S(2)}) collective-permute-start(f32[512,128]{1,0:T(8,128)S(1)} %bitcast.19), channel_id=1, source_target_pairs={{0,1},{1,0},{2,3},{3,2},{4,5},{5,4},{6,7},{7,6},{8,9},{9,8},{10,11... | collective-permute-start | bytes 786440 | tf_op jit(solution)/shard_map/ppermute | solution.py:351
  38.6 1.5 %copy-start.7 = (f32[1,64,1024]{2,1,0:T(8,128)S(1)}, f32[1,64,1024]{2,1,0:T(8,128)}, u32[]{:S(2)}) copy-start(f32[1,64,1024]{2,1,0:T(8,128)} %param.11) | copy-start | bytes 786436
  40.7 8.2 %collective-permute-start.6 = (f32[72,128]{1,0:T(8,128)S(1)}, f32[72,128]{1,0:T(8,128)S(1)}, u32[]{:S(2)}, u32[]{:S(2)}) collective-permute-start(f32[72,128]{1,0:T(8,128)S(1)} %get-tuple-element.53.refs_8_.refs_2_), channel_id=1, source_target_pairs={{0,64},{1,65},{2,66},{3,67},{64,0},{65,1},{66,2},{67,3},{4,68},{5,... | collective-permute-start | bytes 110600 | tf_op jit(solution)/shard_map/ppermute | solution.py:351
  43.7 3.9 %collective-permute-start.8 = (f32[64,128]{1,0:T(8,128)S(1)}, f32[64,128]{1,0:T(8,128)S(1)}, u32[]{:S(2)}, u32[]{:S(2)}) collective-permute-start(f32[64,128]{1,0:T(8,128)S(1)} %get-tuple-element.57), channel_id=1, source_target_pairs={{0,2},{1,3},{2,0},{3,1},{64,66},{65,67},{66,64},{67,65},{4,6},{5,7... | collective-permute-start | bytes 98312 | tf_op jit(solution)/shard_map/ppermute | solution.py:351
  43.8 5.1 %collective-permute-start.7 = (f32[64,128]{1,0:T(8,128)S(1)}, f32[64,128]{1,0:T(8,128)S(1)}, u32[]{:S(2)}, u32[]{:S(2)}) collective-permute-start(f32[64,128]{1,0:T(8,128)S(1)} %get-tuple-element.57), channel_id=1, source_target_pairs={{0,66},{1,67},{2,64},{3,65},{64,2},{65,3},{66,0},{67,1},{4,70},{5,... | collective-permute-start | bytes 98312 | tf_op jit(solution)/shard_map/ppermute | solution.py:351
  49.0 7.2 %collective-permute-start.9 = (f32[264,128]{1,0:T(8,128)S(1)}, f32[264,128]{1,0:T(8,128)S(1)}, u32[]{:S(2)}, u32[]{:S(2)}) collective-permute-start(f32[264,128]{1,0:T(8,128)S(1)} %get-tuple-element.59), channel_id=1, source_target_pairs={{0,32},{4,36},{8,40},{12,44},{16,48},{20,52},{24,56},{28,60},{32,0... | collective-permute-start | bytes 405512 | tf_op jit(solution)/shard_map/ppermute | solution.py:351
  50.0 7.6 %collective-permute-start.10 = (f32[264,128]{1,0:T(8,128)S(1)}, f32[264,128]{1,0:T(8,128)S(1)}, u32[]{:S(2)}, u32[]{:S(2)}) collective-permute-start(f32[264,128]{1,0:T(8,128)S(1)} %get-tuple-element.60), channel_id=1, source_target_pairs={{0,48},{4,52},{8,56},{12,60},{16,32},{20,36},{24,40},{28,44},{32,1... | collective-permute-start | bytes 405512 | tf_op jit(solution)/shard_map/ppermute | solution.py:351
  51.2 6.4 %collective-permute-start.11 = (f32[264,128]{1,0:T(8,128)S(1)}, f32[264,128]{1,0:T(8,128)S(1)}, u32[]{:S(2)}, u32[]{:S(2)}) collective-permute-start(f32[264,128]{1,0:T(8,128)S(1)} %get-tuple-element.61), channel_id=1, source_target_pairs={{0,16},{4,20},{8,24},{12,28},{16,0},{20,4},{24,8},{28,12},{32,48},... | collective-permute-start | bytes 405512 | tf_op jit(solution)/shard_map/ppermute | solution.py:351
  52.6 8.7 %collective-permute-start.4 = (f32[64,1024]{1,0:T(8,128)S(1)}, f32[64,1024]{1,0:T(8,128)S(1)}, u32[]{:S(2)}, u32[]{:S(2)}) collective-permute-start(f32[64,1024]{1,0:T(8,128)S(1)} %get-tuple-element.50), channel_id=1, source_target_pairs={{0,2},{1,3},{2,0},{3,1},{4,6},{5,7},{6,4},{7,5},{8,10},{9,11},{10,... | collective-permute-start | bytes 786440 | tf_op jit(solution)/shard_map/ppermute | solution.py:351
  53.3 11.5 %collective-permute-start.5 = (f32[4,16384]{1,0:T(4,128)S(1)}, f32[4,16384]{1,0:T(4,128)S(1)}, u32[]{:S(2)}, u32[]{:S(2)}) collective-permute-start(f32[4,16384]{1,0:T(4,128)S(1)} %get-tuple-element.54.refs_2_), channel_id=1, source_target_pairs={{0,64},{64,0},{1,65},{65,1},{2,66},{66,2},{3,67},{67,3},{4,68},{68... | collective-permute-start | bytes 786440 | tf_op jit(solution)/shard_map/ppermute | solution.py:351
  57.6 8.0 %collective-permute-start.12 = (f32[264,128]{1,0:T(8,128)S(1)}, f32[264,128]{1,0:T(8,128)S(1)}, u32[]{:S(2)}, u32[]{:S(2)}) collective-permute-start(f32[264,128]{1,0:T(8,128)S(1)} %get-tuple-element.63), channel_id=1, source_target_pairs={{0,8},{4,12},{8,0},{12,4},{16,24},{20,28},{24,16},{28,20},{32,40},... | collective-permute-start | bytes 405512 | tf_op jit(solution)/shard_map/ppermute | solution.py:351
  58.6 7.6 %collective-permute-start.13 = (f32[264,128]{1,0:T(8,128)S(1)}, f32[264,128]{1,0:T(8,128)S(1)}, u32[]{:S(2)}, u32[]{:S(2)}) collective-permute-start(f32[264,128]{1,0:T(8,128)S(1)} %get-tuple-element.64), channel_id=1, source_target_pairs={{0,12},{4,8},{8,4},{12,0},{16,28},{20,24},{24,20},{28,16},{32,44},... | collective-permute-start | bytes 405512 | tf_op jit(solution)/shard_map/ppermute | solution.py:351
  60.9 5.3 %collective-permute-start.14 = (f32[264,128]{1,0:T(8,128)S(1)}, f32[264,128]{1,0:T(8,128)S(1)}, u32[]{:S(2)}, u32[]{:S(2)}) collective-permute-start(f32[264,128]{1,0:T(8,128)S(1)} %get-tuple-element.65), channel_id=1, source_target_pairs={{0,4},{4,0},{8,12},{12,8},{16,20},{20,16},{24,28},{28,24},{32,36},... | collective-permute-start | bytes 405512 | tf_op jit(solution)/shard_map/ppermute | solution.py:351

commit v5 on v4

--- a/solution.py
+++ b/solution.py
@@ -135,9 +135,11 @@
     first, chan = 4 * place_at[0], place_at[1]
     result = jnp.where(line == 3, jnp.bitwise_and(chan, 1).astype(F32), 0.0)
     result = jnp.where(line == 4, lax.shift_right_logical(chan, 1).astype(F32), result)
+    turn = 2 * jnp.bitwise_and(chan, 1)
     for row, bit in ((5, 2), (6, 3), (7, 0), (12, 1)):
-        flag = jnp.bitwise_and(lax.shift_right_logical(place_at[0], bit), 1)
-        result = jnp.where(line == row, flag.astype(F32), result)
+        bit = bit + turn if bit < 2 else bit - turn
+        one = jnp.bitwise_and(lax.shift_right_logical(place_at[0], bit), 1)
+        result = jnp.where(line == row, one.astype(F32), result)
     result = jnp.where((line >= 8) & (line < 12) & (lane == first + line - 8), 1.0, result)
     for tap in range(3):
         for at in range(4):
@@ -264,6 +266,10 @@
     return [jnp.where(high, blocks[at ^ 2], blocks[at]) for at in range(4)]
 
 
+def by_core(grid, swap):
+    return [[jnp.where(swap, grid[b][a], grid[a][b]) if a != b else grid[a][a] for b in range(4)] for a in range(4)]
+
+
 def merge_kernel(gains, grad, mine, mine_far, theirs_far, theirs, out0, out1, out2, out3):
     total = [
         mine[:64, :] + mine_far[:64, :],
@@ -271,8 +277,8 @@
         mine[64:, :] + mine_far[64:, :],
     ]
     shape = (SIDE, SIDE)
-    blocks = [grad[at * 4 : (at + 1) * 4].reshape(SIDE, SIDE) for at in range(4)]
-    blocks = relative(blocks, flag(gains, 5, shape), flag(gains, 6, shape))
+    grid = by_core([[grad[4 * a + b] for b in range(4)] for a in range(4)], flag(gains, 3, (32, SIDE)))
+    blocks = relative([jnp.concatenate(row, axis=0) for row in grid], flag(gains, 5, shape), flag(gains, 6, shape))
     for out, block in zip((out0, out1, out2, out3), blocks):
         out[:64, :] = total[0]
         out[64:128, :] = total[1]
@@ -293,13 +299,16 @@
             out[136 + 32 * near : 168 + 32 * near, :] = block
 
 
-def finish_kernel(own, near, kernel_own, kernel_near, outputs, grad_kernel, token):
+def outputs_kernel(own, near, outputs, token):
     outputs[...] = own[...] + near[...]
-    grad_kernel[...] = kernel_own[...] + kernel_near[...]
     token[...] = jnp.zeros_like(token)
 
 
-def final_kernel(gains, cotangent, in0, in2, in3, in1, out, taps, skip, grad_inputs, rows):
+def finish_kernel(own, near, grad_kernel):
+    grad_kernel[...] = own[...] + near[...]
+
+
+def final_kernel(gains, cotangent, in0, in2, in3, in1, out, taps, skip, grad_inputs, token, rows):
     core, place = flag(gains, 3, (64, SIDE)), flag(gains, 4, (64, SIDE))
     whole = in0[:136, :] + in1[:136, :] + in2[:136, :] + in3[:136, :]
     near, far = [
@@ -307,19 +316,21 @@
     ]
     out[:, :SIDE] = jnp.where(place, far, near)
     out[:, SIDE:] = jnp.where(place, near, far)
+    token[...] = jnp.zeros_like(token)
     taps[...] = whole[128:131, :64]
     own = jnp.sum(whole[131:132] * gains[8:12, :], axis=1, keepdims=True)
     line = lax.broadcasted_iota(jnp.int32, (4, SIDE), 0)
     lane = lax.broadcasted_iota(jnp.int32, (4, SIDE), 1)
     skip[...] = jnp.sum(jnp.where(line == lane, own, 0.0), axis=0, keepdims=True)[:, :4]
     shape = (SIDE, SIDE)
-    by_x = relative([ref[136:, :] for ref in (in0, in1, in2, in3)], flag(gains, 7, shape), flag(gains, 12, shape))
+    columns = relative([ref[136:, :] for ref in (in0, in1, in2, in3)], flag(gains, 7, shape), flag(gains, 12, shape))
     shape = (32, SIDE)
     low, high = flag(gains, 5, shape), flag(gains, 6, shape)
-    for x, column in enumerate(by_x):
-        column = relative([column[32 * at : 32 * at + 32] for at in range(4)], low, high)
-        for z in range(4):
-            rows[(4 * z + x) * 32 : (4 * z + x + 1) * 32, :] = column[z]
+    columns = [relative([column[32 * at : 32 * at + 32] for at in range(4)], low, high) for column in columns]
+    grid = by_core([[columns[b][a] for b in range(4)] for a in range(4)], flag(gains, 3, shape))
+    for z in range(4):
+        for x in range(4):
+            rows[(4 * z + x) * 32 : (4 * z + x + 1) * 32, :] = grid[z][x]
     for at in range(8):
         lanes = slice(at * SIDE, (at + 1) * SIDE)
         grad_inputs[:, lanes] = cotangent[:, lanes] + rows[pl.ds(at, 64, stride=8), :]
@@ -343,12 +354,22 @@
         compiler_params=pltpu.CompilerParams(vmem_limit_bytes=20 * 1024 * 1024),
         input_output_aliases=dict(aliases),
         name=kernel.__name__,
+        cost_estimate=pl.CostEstimate(flops=20000000000, bytes_accessed=0, transcendentals=0) if kernel is forward_kernel else None,
     )(*args, *after)
 
 
 def swapped(value, axes, flip):
     count = lax.axis_size(axes)
     return lax.ppermute(value, axes, [(at, at ^ flip) for at in range(count)])
+
+
+def crossed(value, flip, second):
+    pairs = []
+    for seq in range(16):
+        for chan in range(4):
+            there = seq ^ (flip if (chan + second) % 2 else 4 * flip)
+            pairs.append((4 * seq + chan, 4 * there + chan))
+    return lax.ppermute(value, ("seq", "chan"), pairs)
 
 
 def turned(value):
@@ -377,10 +398,10 @@
     )
     weights_into, weights_back = call(
         weights_kernel, [jax.ShapeDtypeStruct((SIDE, 3 * SIDE), BF16)] * 2, place_at, mix, mix_far,
-        back_rows, back_lanes, scalars=1, after=[kernel_spec],
+        back_rows, back_lanes, scalars=1,
     )
     grad_own, grad_other = call(
-        grad_act_kernel, [(512, SIDE)] * 2, grad_out, cot_far, weights_into, after=[signal_in]
+        grad_act_kernel, [(512, SIDE)] * 2, grad_out, cot_far, weights_into
     )
     grad_near = swapped(grad_other, "chan", 1)
     spec, long_conv, slopes, act = call(
@@ -417,16 +438,18 @@
     )
     sends = call(
         sum_kernel, [(264, SIDE)] * 4,
-        gains, sends[0], *(swapped(sends[at], "seq", 4 * at) for at in (2, 3, 1)),
-    )
-    outputs, grad_kernel, token = call(
-        finish_kernel, [(64, 1024), (4, LENGTH), (8, SIDE)],
-        out_own, swapped(out_far, "chan", 2), kernel_local, swapped(kernel_local, "dp", 1),
-    )
-    grad_mix, grad_conv, grad_skip, grad_inputs = call(
-        final_kernel, [(64, 256), (3, 64), (1, 4), (64, 1024)],
-        gains, grad_out, sends[0], *(swapped(sends[at], "seq", at) for at in (2, 3, 1)),
+        gains, sends[0], *(crossed(sends[at], at, 0) for at in (2, 3, 1)),
+    )
+    outputs, token = call(
+        outputs_kernel, [(64, 1024), (8, SIDE)], out_own, swapped(out_far, "chan", 2)
+    )
+    grad_mix, grad_conv, grad_skip, grad_inputs, token = call(
+        final_kernel, [(64, 256), (3, 64), (1, 4), (64, 1024), (8, SIDE)],
+        gains, grad_out, sends[0], *(crossed(sends[at], at, 1) for at in (2, 3, 1)),
         scratch=[(512, SIDE)], after=[token],
+    )
+    grad_kernel = call(
+        finish_kernel, [(4, LENGTH)], kernel_local, swapped(kernel_local, "dp", 1)
     )
     return (outputs[None], grad_inputs[None], grad_kernel, grad_skip[0], grad_mix.T, grad_conv)
 

time: 67.4 us -> 66.6 us (0.988)
  waiting for transfers between devices: 14.9 us -> 13.5 us
    ppermute x15 -> x9, starting transfers between devices: 16.3 us -> 8.52 us  [swapped(): return lax.ppermute(value, axes, [(at, at ^ flip) for at in range(count)])]
    ppermute x0 -> x6, starting transfers between devices: none -> 7.14 us  [crossed(): return lax.ppermute(value, ('seq', 'chan'), pairs)]
    ppermute x15 -> x9, waiting for transfers between devices: 11 us -> 7.16 us  [swapped(): return lax.ppermute(value, axes, [(at, at ^ flip) for at in range(count)])]
    ppermute x0 -> x6, waiting for transfers between devices: none -> 3.07 us  [crossed(): return lax.ppermute(value, ('seq', 'chan'), pairs)]
    pallas_call x13 -> x14, Pallas kernels: 9.89 us -> 10.5 us  [call(): pl.pallas_call(body, out_shape=shapes if len(shapes) > 1 else shapes[0],...]
  transfers between devices with their start and end apart: 16 -> 16, of which waited for: 10 -> 11; matrix products, arithmetic and copies ran while one was open for 0% -> 0% of each run, Pallas kernels for 12% -> 14%
where the time goes in v5:
time: 66.6 us; the launch traced here: 66.3 us
  starting transfers between devices  23.7 us (36%)
  blocking collectives  15.9 us (24%)
  waiting for transfers between devices  13.5 us (20%)
  Pallas kernels  10.5 us (16%)
  local copies, waits for them, and re-layouts  1.83 us (3%)
  between operations  0.81 us (1%)
    all_to_all x1, blocking collectives, turned(): return lax.all_to_all(value, 'seq', 0, 0, tiled=True)  15.9 us
    pallas_call x14, Pallas kernels, call(): pl.pallas_call(body, out_shape=shapes if len(shapes) > 1 else shapes[0],...  10.5 us
    ppermute x9, starting transfers between devices, swapped(): return lax.ppermute(value, axes, [(at, at ^ flip) for at in range(count)])  8.52 us
    all_to_all x1, starting transfers between devices, turned(): return lax.all_to_all(value, 'seq', 0, 0, tiled=True)  8.01 us
    ppermute x9, waiting for transfers between devices, swapped(): return lax.ppermute(value, axes, [(at, at ^ flip) for at in range(count)])  7.16 us
    ppermute x6, starting transfers between devices, crossed(): return lax.ppermute(value, ('seq', 'chan'), pairs)  7.14 us
    all_to_all x1, waiting for transfers between devices, turned(): return lax.all_to_all(value, 'seq', 0, 0, tiled=True)  3.28 us
    ppermute x6, waiting for transfers between devices, crossed(): return lax.ppermute(value, ('seq', 'chan'), pairs)  3.07 us
  transfers between devices with their start and end apart: 16, of which 11 were waited for; matrix products, arithmetic and copies ran while one was open for 0% of the time, Pallas kernels for 14%

profile of v5, /device:TPU:0, one launch (start us, length us, event | category | flops | bytes accessed | tf_op | source)
XLA Modules:
  0.0 66.3 jit_solution(5575633471132924601)
XLA Ops:
  0.6 1.7 %collective-permute-start = (f32[64,1024]{1,0:T(8,128)}, f32[64,1024]{1,0:T(8,128)S(1)}, u32[]{:S(2)}, u32[]{:S(2)}) collective-permute-start(f32[64,1024]{1,0:T(8,128)} %bitcast.13), channel_id=1, source_target_pairs={{0,2},{1,3},{2,0},{3,1},{4,6},{5,7},{6,4},{7,5},{8,10},{9,11},{10,... | collective-permute-start | bytes 786440 | tf_op jit(solution)/shard_map/ppermute | solution.py:363
  2.4 0.9 %copy-done.3 = f32[1,64,1024]{2,1,0:T(8,128)S(1)} copy-done((f32[1,64,1024]{2,1,0:T(8,128)S(1)}, f32[1,64,1024]{2,1,0:T(8,128)}, u32[]{:S(2)}) %copy-start.3) | copy-done | bytes 262168
  3.3 0.8 %blocks_kernel.1.refs_7_ = f32[512,128]{1,0:T(8,128)} custom-call(f32[64,1024]{1,0:T(8,128)S(1)} %bitcast.17), custom_call_target="tpu_custom_call" | custom-call | tf_op jit(solution)/shard_map/blocks_kernel/pallas_call | solution.py:348
  4.1 8.0 %all-to-all-start = ((f32[16,32,128]{2,1,0:T(8,128)}), f32[16,32,128]{2,1,0:T(8,128)S(1)}, u32[]{:S(2)}, u32[]{:S(2)}) async-start(f32[16,32,128]{2,1,0:T(8,128)} %bitcast.3), calls=%async_computation | async-start | bytes 524288 | tf_op jit(solution)/shard_map/all_to_all | solution.py:376
  12.1 0.5 collective-permute-start.1
  12.7 0.1 pad_add_fusion.refs_0_
  12.8 0.6 copy-done.10
  13.4 1.4 %spectrum_kernel.1 = (f32[512,256]{1,0:T(8,128)S(1)}, f32[16,128]{1,0:T(8,128)S(1)}) custom-call(s32[2]{0:T(128)S(1)} %pad_add_fusion.refs_0_, f32[3,64]{1,0:T(4,128)S(1)} %copy-done.10, f32[4]{0:T(128)S(1)} %copy-done.11, f32[4,16384]{1,0:T(4,128)S(1)} %copy-done.8, bf16[256,384]{1,0:T(8,128)(2,1)S(1)} %copy-done.6, bf16[768,256]{1,0:T(8,128)(2,1)S(1)} %copy-done.2, ...), custom_call_target="tpu_custom_call" | custom-call | tf_op jit(solution)/shard_map/spectrum_kernel/pallas_call | solution.py:348
  14.8 1.4 %collective-permute-done.1.refs_2_ = f32[64,128]{1,0:T(8,128)S(1)} collective-permute-done((f32[64,128]{1,0:T(8,128)S(1)}, f32[64,128]{1,0:T(8,128)S(1)}, u32[]{:S(2)}, u32[]{:S(2)}) %collective-permute-start.1) | collective-permute-done | bytes 32800 | tf_op jit(solution)/shard_map/ppermute | solution.py:363
  16.2 0.7 %weights_kernel.1 = (bf16[128,384]{1,0:T(8,128)(2,1)S(1)}, bf16[128,384]{1,0:T(8,128)(2,1)S(1)}) custom-call(s32[2]{0:T(128)S(1)} %pad_add_fusion.refs_0_, f32[64,256]{1,0:T(8,128)S(1)} %bitcast.21, f32[64,128]{1,0:T(8,128)S(1)} %collective-permute-done.1.refs_2_, bf16[128,768]{1,0:T(8,128)(2,1)S(1)} %copy-done.5, bf16[768,256]{1,0:T(8,128)(2,1)S(1)} %copy-done.1), custom_call_target="tpu_custom_call" | custom-call | tf_op jit(solution)/shard_map/weights_kernel/pallas_call | solution.py:348
  16.9 0.0 collective-permute-done.refs_1_.refs_3_
  16.9 0.2 copy-done
  17.1 0.3 grad_act_kernel.1
  17.4 0.1 collective-permute-start.2
  17.5 3.3 %all-to-all-done.refs_1_.refs_2_ = f32[16,32,128]{2,1,0:T(8,128)S(1)} async-done(((f32[16,32,128]{2,1,0:T(8,128)}), f32[16,32,128]{2,1,0:T(8,128)S(1)}, u32[]{:S(2)}, u32[]{:S(2)}) %all-to-all-start) | async-done | bytes 262176 | tf_op jit(solution)/shard_map/all_to_all | solution.py:376
  20.8 1.7 %forward_kernel.1 = (f32[512,256]{1,0:T(8,128)S(1)}, f32[4,128,128]{2,1,0:T(8,128)S(1)}, f32[4,128,128]{2,1,0:T(8,128)S(1)}, f32[16,64,128]{2,1,0:T(8,128)S(1)}) custom-call(f32[16,128]{1,0:T(8,128)S(1)} %get-tuple-element.38.refs_0_, f32[16,32,128]{2,1,0:T(8,128)S(1)} %all-to-all-done.refs_1_.refs_2_, f32[512,256]{1,0:T(8,128)S(1)} %get-tuple-element.39.refs_2_, ...), custom_call_target="tpu_custom_call" | custom-call | flops 20000000000 | tf_op jit(solution)/shard_map/forward_kernel/pallas_call | solution.py:348
  22.5 0.1 join_kernel.1
  22.6 15.9 %all_to_all.10.refs_1_ = f32[16,64,128]{2,1,0:T(8,128)S(1)} all-to-all(f32[16,64,128]{2,1,0:T(8,128)S(1)} %join_kernel.1), channel_id=1, replica_groups=mesh['dp'=2,'seq'=16,'chan'=4] {'seq'}, dimensions={0} | all-to-all | bytes 1048576 | tf_op jit(solution)/shard_map/all_to_all | solution.py:376
  38.5 0.1 collective-permute-start.3
  38.6 0.0 copy-start.4
  38.6 0.4 slope_kernel.1
  39.0 1.1 %collective-permute-done.3.refs_1_ = f32[512,128]{1,0:T(8,128)S(1)} collective-permute-done((f32[512,128]{1,0:T(8,128)S(1)}, f32[512,128]{1,0:T(8,128)S(1)}, u32[]{:S(2)}, u32[]{:S(2)}) %collective-permute-start.3) | collective-permute-done | bytes 262176 | tf_op jit(solution)/shard_map/ppermute | solution.py:363
  40.1 0.6 tail_kernel.1
  40.7 3.0 %collective-permute-start.5 = (f32[72,128]{1,0:T(8,128)S(1)}, f32[72,128]{1,0:T(8,128)S(1)}, u32[]{:S(2)}, u32[]{:S(2)}) collective-permute-start(f32[72,128]{1,0:T(8,128)S(1)} %get-tuple-element.53.refs_8_.refs_2_), channel_id=1, source_target_pairs={{0,64},{1,65},{2,66},{3,67},{64,0},{65,1},{66,2},{67,3},{4,68},{5,... | collective-permute-start | bytes 110600 | tf_op jit(solution)/shard_map/ppermute | solution.py:363
  43.7 0.1 collective-permute-start.7
  43.8 1.1 %collective-permute-start.6 = (f32[64,128]{1,0:T(8,128)S(1)}, f32[64,128]{1,0:T(8,128)S(1)}, u32[]{:S(2)}, u32[]{:S(2)}) collective-permute-start(f32[64,128]{1,0:T(8,128)S(1)} %get-tuple-element.55), channel_id=1, source_target_pairs={{0,66},{1,67},{2,64},{3,65},{64,2},{65,3},{66,0},{67,1},{4,70},{5,... | collective-permute-start | bytes 98312 | tf_op jit(solution)/shard_map/ppermute | solution.py:363
  44.9 2.2 %backward_kernel.1 = (f32[16,32,128]{2,1,0:T(8,128)S(1)}, f32[4,16384]{1,0:T(4,128)S(1)}) custom-call(f32[4,128,128]{2,1,0:T(8,128)S(1)} %get-tuple-element.51.refs_0_, f32[512,256]{1,0:T(8,128)S(1)} %get-tuple-element.52.refs_1_, f32[512,256]{1,0:T(8,128)S(1)} %get-tuple-element.39.refs_2_, bf16[256,384]{1,0:T(8,128)(2,1)S(1)} %copy-done.6, ...), custom_call_target="tpu_custom_call" | custom-call | tf_op jit(solution)/shard_map/backward_kernel/pallas_call | solution.py:348
  47.1 0.5 collective-permute-done.7.refs_5_
  47.6 1.4 %collective-permute-done.6.refs_4_ = f32[64,128]{1,0:T(8,128)S(1)} collective-permute-done((f32[64,128]{1,0:T(8,128)S(1)}, f32[64,128]{1,0:T(8,128)S(1)}, u32[]{:S(2)}, u32[]{:S(2)}) %collective-permute-start.6) | collective-permute-done | bytes 32800 | tf_op jit(solution)/shard_map/ppermute | solution.py:363
  49.0 0.1 merge_kernel.1
  49.0 0.9 %collective-permute-start.8 = (f32[264,128]{1,0:T(8,128)S(1)}, f32[264,128]{1,0:T(8,128)S(1)}, u32[]{:S(2)}, u32[]{:S(2)}) collective-permute-start(f32[264,128]{1,0:T(8,128)S(1)} %get-tuple-element.57), channel_id=1, source_target_pairs={{0,32},{1,9},{2,34},{3,11},{4,36},{5,13},{6,38},{7,15},{8,40},{9,1... | collective-permute-start | bytes 405512 | tf_op jit(solution)/shard_map/ppermute | solution.py:372
  50.0 1.2 %collective-permute-start.9 = (f32[264,128]{1,0:T(8,128)S(1)}, f32[264,128]{1,0:T(8,128)S(1)}, u32[]{:S(2)}, u32[]{:S(2)}) collective-permute-start(f32[264,128]{1,0:T(8,128)S(1)} %get-tuple-element.58), channel_id=1, source_target_pairs={{0,48},{1,13},{2,50},{3,15},{4,52},{5,9},{6,54},{7,11},{8,56},{9,5... | collective-permute-start | bytes 405512 | tf_op jit(solution)/shard_map/ppermute | solution.py:372
  51.2 1.4 %collective-permute-start.10 = (f32[264,128]{1,0:T(8,128)S(1)}, f32[264,128]{1,0:T(8,128)S(1)}, u32[]{:S(2)}, u32[]{:S(2)}) collective-permute-start(f32[264,128]{1,0:T(8,128)S(1)} %get-tuple-element.59), channel_id=1, source_target_pairs={{0,16},{1,5},{2,18},{3,7},{4,20},{5,1},{6,22},{7,3},{8,24},{9,13},... | collective-permute-start | bytes 405512 | tf_op jit(solution)/shard_map/ppermute | solution.py:372
  52.6 1.0 %collective-permute-start.14 = (f32[4,16384]{1,0:T(4,128)S(1)}, f32[4,16384]{1,0:T(4,128)S(1)}, u32[]{:S(2)}, u32[]{:S(2)}) collective-permute-start(f32[4,16384]{1,0:T(4,128)S(1)} %get-tuple-element.66.refs_0_), channel_id=1, source_target_pairs={{0,64},{64,0},{1,65},{65,1},{2,66},{66,2},{3,67},{67,3},{4,68},{68... | collective-permute-start | bytes 786440 | tf_op jit(solution)/shard_map/ppermute | solution.py:363
  53.6 0.9 %collective-permute-start.4 = (f32[64,1024]{1,0:T(8,128)S(1)}, f32[64,1024]{1,0:T(8,128)S(1)}, u32[]{:S(2)}, u32[]{:S(2)}) collective-permute-start(f32[64,1024]{1,0:T(8,128)S(1)} %get-tuple-element.49), channel_id=1, source_target_pairs={{0,2},{1,3},{2,0},{3,1},{4,6},{5,7},{6,4},{7,5},{8,10},{9,11},{10,... | collective-permute-start | bytes 786440 | tf_op jit(solution)/shard_map/ppermute | solution.py:363
  54.5 1.2 %collective-permute-done.8.refs_2_ = f32[264,128]{1,0:T(8,128)S(1)} collective-permute-done((f32[264,128]{1,0:T(8,128)S(1)}, f32[264,128]{1,0:T(8,128)S(1)}, u32[]{:S(2)}, u32[]{:S(2)}) %collective-permute-start.8) | collective-permute-done | bytes 135200 | tf_op jit(solution)/shard_map/ppermute | solution.py:372
  55.7 1.4 %collective-permute-done.9.refs_3_ = f32[264,128]{1,0:T(8,128)S(1)} collective-permute-done((f32[264,128]{1,0:T(8,128)S(1)}, f32[264,128]{1,0:T(8,128)S(1)}, u32[]{:S(2)}, u32[]{:S(2)}) %collective-permute-start.9) | collective-permute-done | bytes 135200 | tf_op jit(solution)/shard_map/ppermute | solution.py:372
  57.1 0.0 collective-permute-done.10.refs_4_
  57.1 1.2 %collective-permute-start.11 = (f32[264,128]{1,0:T(8,128)S(1)}, f32[264,128]{1,0:T(8,128)S(1)}, u32[]{:S(2)}, u32[]{:S(2)}) collective-permute-start(f32[264,128]{1,0:T(8,128)S(1)} %get-tuple-element.61), channel_id=1, source_target_pairs={{0,8},{1,33},{2,10},{3,35},{4,12},{5,37},{6,14},{7,39},{8,0},{9,41... | collective-permute-start | bytes 405512 | tf_op jit(solution)/shard_map/ppermute | solution.py:372
  58.3 2.1 %collective-permute-start.12 = (f32[264,128]{1,0:T(8,128)S(1)}, f32[264,128]{1,0:T(8,128)S(1)}, u32[]{:S(2)}, u32[]{:S(2)}) collective-permute-start(f32[264,128]{1,0:T(8,128)S(1)} %get-tuple-element.62), channel_id=1, source_target_pairs={{0,12},{1,49},{2,14},{3,51},{4,8},{5,53},{6,10},{7,55},{8,4},{9,57... | collective-permute-start | bytes 405512 | tf_op jit(solution)/shard_map/ppermute | solution.py:372
  60.4 0.3 collective-permute-start.13
  60.7 2.2 %collective-permute-done.14.refs_1_ = f32[4,16384]{1,0:T(4,128)S(1)} collective-permute-done((f32[4,16384]{1,0:T(4,128)S(1)}, f32[4,16384]{1,0:T(4,128)S(1)}, u32[]{:S(2)}, u32[]{:S(2)}) %collective-permute-start.14) | collective-permute-done | bytes 262176 | tf_op jit(solution)/shard_map/ppermute | solution.py:363
  62.9 0.7 %finish_kernel.1 = f32[4,16384]{1,0:T(4,128)} custom-call(f32[4,16384]{1,0:T(4,128)S(1)} %get-tuple-element.66.refs_0_, f32[4,16384]{1,0:T(4,128)S(1)} %collective-permute-done.14.refs_1_), custom_call_target="tpu_custom_call" | custom-call | tf_op jit(solution)/shard_map/finish_kernel/pallas_call | solution.py:348
  63.6 0.6 collective-permute-done.4.refs_1_
  64.2 0.7 %outputs_kernel.1 = (f32[64,1024]{1,0:T(8,128)}, f32[8,128]{1,0:T(8,128)S(1)}) custom-call(f32[64,1024]{1,0:T(8,128)S(1)} %get-tuple-element.48.refs_0_, f32[64,1024]{1,0:T(8,128)S(1)} %collective-permute-done.4.refs_1_), custom_call_target="tpu_custom_call" | custom-call | tf_op jit(solution)/shard_map/outputs_kernel/pallas_call | solution.py:348
  64.9 0.2 collective-permute-done.12.refs_4_
  65.2 0.3 collective-permute-done.13.refs_5_
  65.5 0.9 %final_kernel.1 = (f32[64,256]{1,0:T(8,128)}, f32[3,64]{1,0:T(4,128)}, f32[1,4]{1,0:T(1,128)}, f32[64,1024]{1,0:T(8,128)}, f32[8,128]{1,0:T(8,128)}) custom-call(f32[16,128]{1,0:T(8,128)S(1)} %get-tuple-element.38.refs_0_, f32[64,1024]{1,0:T(8,128)S(1)} %bitcast.16, f32[264,128]{1,0:T(8,128)S(1)} %get-tuple-element.60.refs_2_, ...), custom_call_target="tpu_custom_call" | custom-call | tf_op jit(solution)/shard_map/final_kernel/pallas_call | solution.py:348
  (26 shorter events, 0.1 us)
Async XLA Ops:
  0.6 16.2 %collective-permute-start = (f32[64,1024]{1,0:T(8,128)}, f32[64,1024]{1,0:T(8,128)S(1)}, u32[]{:S(2)}, u32[]{:S(2)}) collective-permute-start(f32[64,1024]{1,0:T(8,128)} %bitcast.13), channel_id=1, source_target_pairs={{0,2},{1,3},{2,0},{3,1},{4,6},{5,7},{6,4},{7,5},{8,10},{9,11},{10,... | collective-permute-start | bytes 786440 | tf_op jit(solution)/shard_map/ppermute | solution.py:363
  2.4 0.9 %copy-start.3 = (f32[1,64,1024]{2,1,0:T(8,128)S(1)}, f32[1,64,1024]{2,1,0:T(8,128)}, u32[]{:S(2)}) copy-start(f32[1,64,1024]{2,1,0:T(8,128)} %param.11) | copy-start | bytes 786436
  3.3 8.8 %copy-start.9 = (f32[256,64]{0,1:T(8,128)S(1)}, f32[256,64]{0,1:T(8,128)}, u32[]{:S(2)}) copy-start(f32[256,64]{0,1:T(8,128)} %param.16) | copy-start | bytes 196612
  3.3 9.4 %copy-start.7 = (f32[2,128,128]{2,1,0:T(8,128)S(1)}, f32[2,128,128]{2,1,0:T(8,128)}, u32[]{:S(2)}) copy-start(f32[2,128,128]{2,1,0:T(8,128)} %constant.31.clone.refs_6_.refs_7_) | copy-start | bytes 393220
  3.3 9.4 %copy-start.8 = (f32[4,16384]{1,0:T(4,128)S(1)}, f32[4,16384]{1,0:T(4,128)}, u32[]{:S(2)}) copy-start(f32[4,16384]{1,0:T(4,128)} %refs_3_.4) | copy-start | bytes 786436
  4.1 8.7 %copy-start.2 = (bf16[768,256]{1,0:T(8,128)(2,1)S(1)}, bf16[768,256]{1,0:T(8,128)(2,1)}, u32[]{:S(2)}) copy-start(bf16[768,256]{1,0:T(8,128)(2,1)} %constant.28.clone.refs_5_.refs_4_) | copy-start | bytes 1179652
  4.1 8.7 %copy-start.6 = (bf16[256,384]{1,0:T(8,128)(2,1)S(1)}, bf16[256,384]{1,0:T(8,128)(2,1)}, u32[]{:S(2)}) copy-start(bf16[256,384]{1,0:T(8,128)(2,1)} %constant.27.clone.refs_4_.refs_3_) | copy-start | bytes 589828
  4.1 16.7 %all-to-all-start = ((f32[16,32,128]{2,1,0:T(8,128)}), f32[16,32,128]{2,1,0:T(8,128)S(1)}, u32[]{:S(2)}, u32[]{:S(2)}) async-start(f32[16,32,128]{2,1,0:T(8,128)} %bitcast.3), calls=%async_computation | async-start | bytes 524288 | tf_op jit(solution)/shard_map/all_to_all | solution.py:376
  12.1 4.0 %collective-permute-start.1 = (f32[64,128]{1,0:T(8,128)S(1)}, f32[64,128]{1,0:T(8,128)S(1)}, u32[]{:S(2)}, u32[]{:S(2)}) collective-permute-start(f32[64,128]{1,0:T(8,128)S(1)} %dynamic-slice_bitcast_fusion), channel_id=1, source_target_pairs={{0,2},{1,3},{2,0},{3,1},{4,6},{5,7},{6,4},{7,5},{8,10},{9,11},{10,... | collective-permute-start | bytes 98312 | tf_op jit(solution)/shard_map/ppermute | solution.py:363
  12.7 0.7 %copy-start.10 = (f32[3,64]{1,0:T(4,128)S(1)}, f32[3,64]{1,0:T(4,128)}, u32[]{:S(2)}) copy-start(f32[3,64]{1,0:T(4,128)} %refs_1_.1) | copy-start | bytes 2308
  12.7 0.7 %copy-start.11 = (f32[4]{0:T(128)S(1)}, f32[4]{0:T(128)}, u32[]{:S(2)}) copy-start(f32[4]{0:T(128)} %refs_2_.1) | copy-start | bytes 52
  13.4 2.8 %copy-start.1 = (bf16[768,256]{1,0:T(8,128)(2,1)S(1)}, bf16[768,256]{1,0:T(8,128)(2,1)}, u32[]{:S(2)}) copy-start(bf16[768,256]{1,0:T(8,128)(2,1)} %constant.30.clone.refs_4_.refs_6_) | copy-start | bytes 1179652
  13.4 2.8 %copy-start.5 = (bf16[128,768]{1,0:T(8,128)(2,1)S(1)}, bf16[128,768]{1,0:T(8,128)(2,1)}, u32[]{:S(2)}) copy-start(bf16[128,768]{1,0:T(8,128)(2,1)} %constant.29.clone.refs_3_.refs_5_) | copy-start | bytes 589828
  16.1 1.0 %copy-start = (f32[1,64,1024]{2,1,0:T(8,128)S(1)}, f32[1,64,1024]{2,1,0:T(8,128)}, u32[]{:S(2)}) copy-start(f32[1,64,1024]{2,1,0:T(8,128)} %param.12) | copy-start | bytes 786436
  17.4 5.1 %collective-permute-start.2 = (f32[512,128]{1,0:T(8,128)S(1)}, f32[512,128]{1,0:T(8,128)S(1)}, u32[]{:S(2)}, u32[]{:S(2)}) collective-permute-start(f32[512,128]{1,0:T(8,128)S(1)} %get-tuple-element.43), channel_id=1, source_target_pairs={{0,1},{1,0},{2,3},{3,2},{4,5},{5,4},{6,7},{7,6},{8,9},{9,8},{10,11... | collective-permute-start | bytes 786440 | tf_op jit(solution)/shard_map/ppermute | solution.py:363
  38.5 1.6 %collective-permute-start.3 = (f32[512,128]{1,0:T(8,128)S(1)}, f32[512,128]{1,0:T(8,128)S(1)}, u32[]{:S(2)}, u32[]{:S(2)}) collective-permute-start(f32[512,128]{1,0:T(8,128)S(1)} %bitcast.19), channel_id=1, source_target_pairs={{0,1},{1,0},{2,3},{3,2},{4,5},{5,4},{6,7},{7,6},{8,9},{9,8},{10,11... | collective-permute-start | bytes 786440 | tf_op jit(solution)/shard_map/ppermute | solution.py:363
  38.6 1.5 %copy-start.4 = (f32[1,64,1024]{2,1,0:T(8,128)S(1)}, f32[1,64,1024]{2,1,0:T(8,128)}, u32[]{:S(2)}) copy-start(f32[1,64,1024]{2,1,0:T(8,128)} %param.11) | copy-start | bytes 786436
  40.7 8.2 %collective-permute-start.5 = (f32[72,128]{1,0:T(8,128)S(1)}, f32[72,128]{1,0:T(8,128)S(1)}, u32[]{:S(2)}, u32[]{:S(2)}) collective-permute-start(f32[72,128]{1,0:T(8,128)S(1)} %get-tuple-element.53.refs_8_.refs_2_), channel_id=1, source_target_pairs={{0,64},{1,65},{2,66},{3,67},{64,0},{65,1},{66,2},{67,3},{4,68},{5,... | collective-permute-start | bytes 110600 | tf_op jit(solution)/shard_map/ppermute | solution.py:363
  43.7 3.9 %collective-permute-start.7 = (f32[64,128]{1,0:T(8,128)S(1)}, f32[64,128]{1,0:T(8,128)S(1)}, u32[]{:S(2)}, u32[]{:S(2)}) collective-permute-start(f32[64,128]{1,0:T(8,128)S(1)} %get-tuple-element.55), channel_id=1, source_target_pairs={{0,2},{1,3},{2,0},{3,1},{64,66},{65,67},{66,64},{67,65},{4,6},{5,7... | collective-permute-start | bytes 98312 | tf_op jit(solution)/shard_map/ppermute | solution.py:363
  43.8 5.1 %collective-permute-start.6 = (f32[64,128]{1,0:T(8,128)S(1)}, f32[64,128]{1,0:T(8,128)S(1)}, u32[]{:S(2)}, u32[]{:S(2)}) collective-permute-start(f32[64,128]{1,0:T(8,128)S(1)} %get-tuple-element.55), channel_id=1, source_target_pairs={{0,66},{1,67},{2,64},{3,65},{64,2},{65,3},{66,0},{67,1},{4,70},{5,... | collective-permute-start | bytes 98312 | tf_op jit(solution)/shard_map/ppermute | solution.py:363
  49.0 6.7 %collective-permute-start.8 = (f32[264,128]{1,0:T(8,128)S(1)}, f32[264,128]{1,0:T(8,128)S(1)}, u32[]{:S(2)}, u32[]{:S(2)}) collective-permute-start(f32[264,128]{1,0:T(8,128)S(1)} %get-tuple-element.57), channel_id=1, source_target_pairs={{0,32},{1,9},{2,34},{3,11},{4,36},{5,13},{6,38},{7,15},{8,40},{9,1... | collective-permute-start | bytes 405512 | tf_op jit(solution)/shard_map/ppermute | solution.py:372
  50.0 7.1 %collective-permute-start.9 = (f32[264,128]{1,0:T(8,128)S(1)}, f32[264,128]{1,0:T(8,128)S(1)}, u32[]{:S(2)}, u32[]{:S(2)}) collective-permute-start(f32[264,128]{1,0:T(8,128)S(1)} %get-tuple-element.58), channel_id=1, source_target_pairs={{0,48},{1,13},{2,50},{3,15},{4,52},{5,9},{6,54},{7,11},{8,56},{9,5... | collective-permute-start | bytes 405512 | tf_op jit(solution)/shard_map/ppermute | solution.py:372
  51.2 5.9 %collective-permute-start.10 = (f32[264,128]{1,0:T(8,128)S(1)}, f32[264,128]{1,0:T(8,128)S(1)}, u32[]{:S(2)}, u32[]{:S(2)}) collective-permute-start(f32[264,128]{1,0:T(8,128)S(1)} %get-tuple-element.59), channel_id=1, source_target_pairs={{0,16},{1,5},{2,18},{3,7},{4,20},{5,1},{6,22},{7,3},{8,24},{9,13},... | collective-permute-start | bytes 405512 | tf_op jit(solution)/shard_map/ppermute | solution.py:372
  52.6 10.3 %collective-permute-start.14 = (f32[4,16384]{1,0:T(4,128)S(1)}, f32[4,16384]{1,0:T(4,128)S(1)}, u32[]{:S(2)}, u32[]{:S(2)}) collective-permute-start(f32[4,16384]{1,0:T(4,128)S(1)} %get-tuple-element.66.refs_0_), channel_id=1, source_target_pairs={{0,64},{64,0},{1,65},{65,1},{2,66},{66,2},{3,67},{67,3},{4,68},{68... | collective-permute-start | bytes 786440 | tf_op jit(solution)/shard_map/ppermute | solution.py:363
  53.6 10.6 %collective-permute-start.4 = (f32[64,1024]{1,0:T(8,128)S(1)}, f32[64,1024]{1,0:T(8,128)S(1)}, u32[]{:S(2)}, u32[]{:S(2)}) collective-permute-start(f32[64,1024]{1,0:T(8,128)S(1)} %get-tuple-element.49), channel_id=1, source_target_pairs={{0,2},{1,3},{2,0},{3,1},{4,6},{5,7},{6,4},{7,5},{8,10},{9,11},{10,... | collective-permute-start | bytes 786440 | tf_op jit(solution)/shard_map/ppermute | solution.py:363
  57.1 7.8 %collective-permute-start.11 = (f32[264,128]{1,0:T(8,128)S(1)}, f32[264,128]{1,0:T(8,128)S(1)}, u32[]{:S(2)}, u32[]{:S(2)}) collective-permute-start(f32[264,128]{1,0:T(8,128)S(1)} %get-tuple-element.61), channel_id=1, source_target_pairs={{0,8},{1,33},{2,10},{3,35},{4,12},{5,37},{6,14},{7,39},{8,0},{9,41... | collective-permute-start | bytes 405512 | tf_op jit(solution)/shard_map/ppermute | solution.py:372
  58.3 6.8 %collective-permute-start.12 = (f32[264,128]{1,0:T(8,128)S(1)}, f32[264,128]{1,0:T(8,128)S(1)}, u32[]{:S(2)}, u32[]{:S(2)}) collective-permute-start(f32[264,128]{1,0:T(8,128)S(1)} %get-tuple-element.62), channel_id=1, source_target_pairs={{0,12},{1,49},{2,14},{3,51},{4,8},{5,53},{6,10},{7,55},{8,4},{9,57... | collective-permute-start | bytes 405512 | tf_op jit(solution)/shard_map/ppermute | solution.py:372
  60.4 5.0 %collective-permute-start.13 = (f32[264,128]{1,0:T(8,128)S(1)}, f32[264,128]{1,0:T(8,128)S(1)}, u32[]{:S(2)}, u32[]{:S(2)}) collective-permute-start(f32[264,128]{1,0:T(8,128)S(1)} %get-tuple-element.63), channel_id=1, source_target_pairs={{0,4},{1,17},{2,6},{3,19},{4,0},{5,21},{6,2},{7,23},{8,12},{9,25},... | collective-permute-start | bytes 405512 | tf_op jit(solution)/shard_map/ppermute | solution.py:372

commit v6 on v5

--- a/solution.py
+++ b/solution.py
@@ -213,23 +213,27 @@
     copy.wait()
 
 
-def slope_kernel(gains, grad_act, signal, long_conv, slopes, grads, small):
+def slope_kernel(
+    gains, grad_act, signal, long_conv, slopes, into_rows, into_lanes, twist, grad_spec, small,
+):
     small[...] = jnp.zeros_like(small)
+    grads = []
     for index in range(4):
         taps = gains_of(gains, index)
         grad = channel(grad_act, 4 + index) * slopes[index]
         later = [advanced(grad, 2), advanced(grad, 1), grad]
-        grads[index] = taps[0] * later[0] + taps[1] * later[1] + taps[2] * later[2]
+        grads.append(taps[0] * later[0] + taps[1] * later[1] + taps[2] * later[2])
         pairs = [one * long_conv[index] for one in later] + [grads[index] * channel(signal, index)]
         sums = jnp.concatenate([jnp.sum(one, axis=0, keepdims=True) for one in pairs], axis=0)
         small[:4, :] = small[:4, :] + jnp.sum(sums, axis=1, keepdims=True) * gains[8 + index : 9 + index, :]
+    grad_spec[...] = forward(grads, into_rows, into_lanes, twist)
 
 
 def backward_kernel(
-    grads, spec, kernel_spec, into_rows, into_lanes, back_rows, back_lanes, twist,
+    grad_spec, spec, kernel_spec, back_rows, back_lanes, twist,
     grad_in, kernel_out, rows,
 ):
-    spectrum = forward([grads[at] for at in range(4)], into_rows, into_lanes, twist)
+    spectrum = grad_spec[...]
     result = backward(times_conj(spectrum, kernel_spec[...]), back_rows, back_lanes, twist)
     for at in range(4):
         grad_in[:, at * 8 : (at + 1) * 8, :] = result[at].reshape(16, 8, SIDE)
@@ -417,8 +421,8 @@
     act_in = turned(act)
     act_own = act_in[:, :32].reshape(512, SIDE)
     act_near = swapped(act_own, "chan", 1)
-    grads, small = call(
-        slope_kernel, [(4, SIDE, SIDE), (8, SIDE)], gains, act_in, signal_in, long_conv, slopes
+    grad_spec, small = call(
+        slope_kernel, [(512, 256), (8, SIDE)], gains, act_in, signal_in, long_conv, slopes, into_rows, into_lanes, twist
     )
     mine, theirs, out_own, out_far = call(
         tail_kernel,
@@ -428,7 +432,7 @@
     grad_long, kernel_local = call(
         backward_kernel,
         [(16, 32, SIDE), (4, LENGTH)],
-        grads, spec, kernel_spec, into_rows, into_lanes, back_rows, back_lanes, twist,
+        grad_spec, spec, kernel_spec, back_rows, back_lanes, twist,
         after=[mine], scratch=[(512, SIDE)],
     )
     both = ("dp", "chan")

time: 66.6 us -> 66.6 us (level)
  no operation moved by 1% of the time
where the time goes in v6:
time: 66.6 us; the launch traced here: 66.3 us
  starting transfers between devices  23.7 us (36%)
  blocking collectives  15.9 us (24%)
  waiting for transfers between devices  13.5 us (20%)
  Pallas kernels  10.5 us (16%)
  local copies, waits for them, and re-layouts  1.83 us (3%)
  between operations  0.81 us (1%)
    all_to_all x1, blocking collectives, turned(): return lax.all_to_all(value, 'seq', 0, 0, tiled=True)  15.9 us
    pallas_call x14, Pallas kernels, call(): pl.pallas_call(body, out_shape=shapes if len(shapes) > 1 else shapes[0],...  10.5 us
    ppermute x9, starting transfers between devices, swapped(): return lax.ppermute(value, axes, [(at, at ^ flip) for at in range(count)])  8.52 us
    all_to_all x1, starting transfers between devices, turned(): return lax.all_to_all(value, 'seq', 0, 0, tiled=True)  8.01 us
    ppermute x6, starting transfers between devices, crossed(): return lax.ppermute(value, ('seq', 'chan'), pairs)  7.14 us
    ppermute x9, waiting for transfers between devices, swapped(): return lax.ppermute(value, axes, [(at, at ^ flip) for at in range(count)])  7.04 us
    all_to_all x1, waiting for transfers between devices, turned(): return lax.all_to_all(value, 'seq', 0, 0, tiled=True)  3.28 us
    ppermute x6, waiting for transfers between devices, crossed(): return lax.ppermute(value, ('seq', 'chan'), pairs)  3.19 us
  transfers between devices with their start and end apart: 16, of which 11 were waited for; matrix products, arithmetic and copies ran while one was open for 0% of the time, Pallas kernels for 14%

profile of v6, /device:TPU:0, one launch (start us, length us, event | category | flops | bytes accessed | tf_op | source)
XLA Modules:
  0.0 66.3 jit_solution(1071461250030587982)
XLA Ops:
  0.6 1.7 %collective-permute-start = (f32[64,1024]{1,0:T(8,128)}, f32[64,1024]{1,0:T(8,128)S(1)}, u32[]{:S(2)}, u32[]{:S(2)}) collective-permute-start(f32[64,1024]{1,0:T(8,128)} %bitcast.13), channel_id=1, source_target_pairs={{0,2},{1,3},{2,0},{3,1},{4,6},{5,7},{6,4},{7,5},{8,10},{9,11},{10,... | collective-permute-start | bytes 786440 | tf_op jit(solution)/shard_map/ppermute | solution.py:367
  2.4 0.9 %copy-done.4 = f32[1,64,1024]{2,1,0:T(8,128)S(1)} copy-done((f32[1,64,1024]{2,1,0:T(8,128)S(1)}, f32[1,64,1024]{2,1,0:T(8,128)}, u32[]{:S(2)}) %copy-start.4) | copy-done | bytes 262168
  3.3 0.8 %blocks_kernel.1.refs_7_ = f32[512,128]{1,0:T(8,128)} custom-call(f32[64,1024]{1,0:T(8,128)S(1)} %bitcast.17), custom_call_target="tpu_custom_call" | custom-call | tf_op jit(solution)/shard_map/blocks_kernel/pallas_call | solution.py:352
  4.1 8.0 %all-to-all-start = ((f32[16,32,128]{2,1,0:T(8,128)}), f32[16,32,128]{2,1,0:T(8,128)S(1)}, u32[]{:S(2)}, u32[]{:S(2)}) async-start(f32[16,32,128]{2,1,0:T(8,128)} %bitcast.3), calls=%async_computation | async-start | bytes 524288 | tf_op jit(solution)/shard_map/all_to_all | solution.py:380
  12.1 0.5 collective-permute-start.1
  12.7 0.1 pad_add_fusion.refs_0_
  12.8 0.6 copy-done.10
  13.4 1.4 %spectrum_kernel.1 = (f32[512,256]{1,0:T(8,128)S(1)}, f32[16,128]{1,0:T(8,128)S(1)}) custom-call(s32[2]{0:T(128)S(1)} %pad_add_fusion.refs_0_, f32[3,64]{1,0:T(4,128)S(1)} %copy-done.10, f32[4]{0:T(128)S(1)} %copy-done.11, f32[4,16384]{1,0:T(4,128)S(1)} %copy-done.8, bf16[256,384]{1,0:T(8,128)(2,1)S(1)} %copy-done.7, bf16[768,256]{1,0:T(8,128)(2,1)S(1)} %copy-done.2, ...), custom_call_target="tpu_custom_call" | custom-call | tf_op jit(solution)/shard_map/spectrum_kernel/pallas_call | solution.py:352
  14.8 1.4 %collective-permute-done.1.refs_2_ = f32[64,128]{1,0:T(8,128)S(1)} collective-permute-done((f32[64,128]{1,0:T(8,128)S(1)}, f32[64,128]{1,0:T(8,128)S(1)}, u32[]{:S(2)}, u32[]{:S(2)}) %collective-permute-start.1) | collective-permute-done | bytes 32800 | tf_op jit(solution)/shard_map/ppermute | solution.py:367
  16.2 0.7 %weights_kernel.1 = (bf16[128,384]{1,0:T(8,128)(2,1)S(1)}, bf16[128,384]{1,0:T(8,128)(2,1)S(1)}) custom-call(s32[2]{0:T(128)S(1)} %pad_add_fusion.refs_0_, f32[64,256]{1,0:T(8,128)S(1)} %bitcast.21, f32[64,128]{1,0:T(8,128)S(1)} %collective-permute-done.1.refs_2_, bf16[128,768]{1,0:T(8,128)(2,1)S(1)} %copy-done.6, bf16[768,256]{1,0:T(8,128)(2,1)S(1)} %copy-done.1), custom_call_target="tpu_custom_call" | custom-call | tf_op jit(solution)/shard_map/weights_kernel/pallas_call | solution.py:352
  16.9 0.0 collective-permute-done.refs_1_.refs_3_
  16.9 0.2 copy-done
  17.1 0.3 grad_act_kernel.1
  17.4 0.1 collective-permute-start.2
  17.5 3.3 %all-to-all-done.refs_1_.refs_2_ = f32[16,32,128]{2,1,0:T(8,128)S(1)} async-done(((f32[16,32,128]{2,1,0:T(8,128)}), f32[16,32,128]{2,1,0:T(8,128)S(1)}, u32[]{:S(2)}, u32[]{:S(2)}) %all-to-all-start) | async-done | bytes 262176 | tf_op jit(solution)/shard_map/all_to_all | solution.py:380
  20.8 1.7 %forward_kernel.1 = (f32[512,256]{1,0:T(8,128)S(1)}, f32[4,128,128]{2,1,0:T(8,128)S(1)}, f32[4,128,128]{2,1,0:T(8,128)S(1)}, f32[16,64,128]{2,1,0:T(8,128)S(1)}) custom-call(f32[16,128]{1,0:T(8,128)S(1)} %get-tuple-element.38.refs_0_, f32[16,32,128]{2,1,0:T(8,128)S(1)} %all-to-all-done.refs_1_.refs_2_, f32[512,256]{1,0:T(8,128)S(1)} %get-tuple-element.39.refs_2_, ...), custom_call_target="tpu_custom_call" | custom-call | flops 20000000000 | tf_op jit(solution)/shard_map/forward_kernel/pallas_call | solution.py:352
  22.5 0.1 join_kernel.1
  22.6 15.9 %all_to_all.10.refs_1_ = f32[16,64,128]{2,1,0:T(8,128)S(1)} all-to-all(f32[16,64,128]{2,1,0:T(8,128)S(1)} %join_kernel.1), channel_id=1, replica_groups=mesh['dp'=2,'seq'=16,'chan'=4] {'seq'}, dimensions={0} | all-to-all | bytes 1048576 | tf_op jit(solution)/shard_map/all_to_all | solution.py:380
  38.5 0.1 collective-permute-start.3
  38.6 0.0 copy-start.5
  38.6 0.9 %slope_kernel.1 = (f32[512,256]{1,0:T(8,128)S(1)}, f32[8,128]{1,0:T(8,128)S(1)}) custom-call(f32[16,128]{1,0:T(8,128)S(1)} %get-tuple-element.38.refs_0_, f32[16,64,128]{2,1,0:T(8,128)S(1)} %all_to_all.10.refs_1_, f32[16,32,128]{2,1,0:T(8,128)S(1)} %all-to-all-done.refs_1_.refs_2_, f32[4,128,128]{2,1,0:T(8,128)S(1)} %get-tuple-element.45.refs_3_, ...), custom_call_target="tpu_custom_call" | custom-call | tf_op jit(solution)/shard_map/slope_kernel/pallas_call | solution.py:352
  39.5 0.6 collective-permute-done.3.refs_1_
  40.1 0.6 tail_kernel.1
  40.7 3.0 %collective-permute-start.5 = (f32[72,128]{1,0:T(8,128)S(1)}, f32[72,128]{1,0:T(8,128)S(1)}, u32[]{:S(2)}, u32[]{:S(2)}) collective-permute-start(f32[72,128]{1,0:T(8,128)S(1)} %get-tuple-element.53.refs_6_.refs_2_), channel_id=1, source_target_pairs={{0,64},{1,65},{2,66},{3,67},{64,0},{65,1},{66,2},{67,3},{4,68},{5,... | collective-permute-start | bytes 110600 | tf_op jit(solution)/shard_map/ppermute | solution.py:367
  43.7 0.1 collective-permute-start.7
  43.8 1.1 %collective-permute-start.6 = (f32[64,128]{1,0:T(8,128)S(1)}, f32[64,128]{1,0:T(8,128)S(1)}, u32[]{:S(2)}, u32[]{:S(2)}) collective-permute-start(f32[64,128]{1,0:T(8,128)S(1)} %get-tuple-element.55), channel_id=1, source_target_pairs={{0,66},{1,67},{2,64},{3,65},{64,2},{65,3},{66,0},{67,1},{4,70},{5,... | collective-permute-start | bytes 98312 | tf_op jit(solution)/shard_map/ppermute | solution.py:367
  44.9 1.7 %backward_kernel.1 = (f32[16,32,128]{2,1,0:T(8,128)S(1)}, f32[4,16384]{1,0:T(4,128)S(1)}) custom-call(f32[512,256]{1,0:T(8,128)S(1)} %get-tuple-element.51.refs_0_, f32[512,256]{1,0:T(8,128)S(1)} %get-tuple-element.52.refs_1_, f32[512,256]{1,0:T(8,128)S(1)} %get-tuple-element.39.refs_2_, bf16[128,768]{1,0:T(8,128)(2,1)S(1)} %copy-done.6, ...), custom_call_target="tpu_custom_call" | custom-call | tf_op jit(solution)/shard_map/backward_kernel/pallas_call | solution.py:352
  46.6 1.1 %collective-permute-done.7.refs_5_ = f32[64,128]{1,0:T(8,128)S(1)} collective-permute-done((f32[64,128]{1,0:T(8,128)S(1)}, f32[64,128]{1,0:T(8,128)S(1)}, u32[]{:S(2)}, u32[]{:S(2)}) %collective-permute-start.7) | collective-permute-done | bytes 32800 | tf_op jit(solution)/shard_map/ppermute | solution.py:367
  47.6 1.4 %collective-permute-done.6.refs_4_ = f32[64,128]{1,0:T(8,128)S(1)} collective-permute-done((f32[64,128]{1,0:T(8,128)S(1)}, f32[64,128]{1,0:T(8,128)S(1)}, u32[]{:S(2)}, u32[]{:S(2)}) %collective-permute-start.6) | collective-permute-done | bytes 32800 | tf_op jit(solution)/shard_map/ppermute | solution.py:367
  49.0 0.0 collective-permute-done.5.refs_3_
  49.0 0.1 merge_kernel.1
  49.0 0.9 %collective-permute-start.8 = (f32[264,128]{1,0:T(8,128)S(1)}, f32[264,128]{1,0:T(8,128)S(1)}, u32[]{:S(2)}, u32[]{:S(2)}) collective-permute-start(f32[264,128]{1,0:T(8,128)S(1)} %get-tuple-element.57), channel_id=1, source_target_pairs={{0,32},{1,9},{2,34},{3,11},{4,36},{5,13},{6,38},{7,15},{8,40},{9,1... | collective-permute-start | bytes 405512 | tf_op jit(solution)/shard_map/ppermute | solution.py:376
  50.0 1.2 %collective-permute-start.9 = (f32[264,128]{1,0:T(8,128)S(1)}, f32[264,128]{1,0:T(8,128)S(1)}, u32[]{:S(2)}, u32[]{:S(2)}) collective-permute-start(f32[264,128]{1,0:T(8,128)S(1)} %get-tuple-element.58), channel_id=1, source_target_pairs={{0,48},{1,13},{2,50},{3,15},{4,52},{5,9},{6,54},{7,11},{8,56},{9,5... | collective-permute-start | bytes 405512 | tf_op jit(solution)/shard_map/ppermute | solution.py:376
  51.2 1.4 %collective-permute-start.10 = (f32[264,128]{1,0:T(8,128)S(1)}, f32[264,128]{1,0:T(8,128)S(1)}, u32[]{:S(2)}, u32[]{:S(2)}) collective-permute-start(f32[264,128]{1,0:T(8,128)S(1)} %get-tuple-element.59), channel_id=1, source_target_pairs={{0,16},{1,5},{2,18},{3,7},{4,20},{5,1},{6,22},{7,3},{8,24},{9,13},... | collective-permute-start | bytes 405512 | tf_op jit(solution)/shard_map/ppermute | solution.py:376
  52.6 0.7 %collective-permute-start.14 = (f32[4,16384]{1,0:T(4,128)S(1)}, f32[4,16384]{1,0:T(4,128)S(1)}, u32[]{:S(2)}, u32[]{:S(2)}) collective-permute-start(f32[4,16384]{1,0:T(4,128)S(1)} %get-tuple-element.66.refs_0_), channel_id=1, source_target_pairs={{0,64},{64,0},{1,65},{65,1},{2,66},{66,2},{3,67},{67,3},{4,68},{68... | collective-permute-start | bytes 786440 | tf_op jit(solution)/shard_map/ppermute | solution.py:367
  53.3 1.2 %collective-permute-start.4 = (f32[64,1024]{1,0:T(8,128)S(1)}, f32[64,1024]{1,0:T(8,128)S(1)}, u32[]{:S(2)}, u32[]{:S(2)}) collective-permute-start(f32[64,1024]{1,0:T(8,128)S(1)} %get-tuple-element.49), channel_id=1, source_target_pairs={{0,2},{1,3},{2,0},{3,1},{4,6},{5,7},{6,4},{7,5},{8,10},{9,11},{10,... | collective-permute-start | bytes 786440 | tf_op jit(solution)/shard_map/ppermute | solution.py:367
  54.5 1.2 %collective-permute-done.8.refs_2_ = f32[264,128]{1,0:T(8,128)S(1)} collective-permute-done((f32[264,128]{1,0:T(8,128)S(1)}, f32[264,128]{1,0:T(8,128)S(1)}, u32[]{:S(2)}, u32[]{:S(2)}) %collective-permute-start.8) | collective-permute-done | bytes 135200 | tf_op jit(solution)/shard_map/ppermute | solution.py:376
  55.7 1.4 %collective-permute-done.9.refs_3_ = f32[264,128]{1,0:T(8,128)S(1)} collective-permute-done((f32[264,128]{1,0:T(8,128)S(1)}, f32[264,128]{1,0:T(8,128)S(1)}, u32[]{:S(2)}, u32[]{:S(2)}) %collective-permute-start.9) | collective-permute-done | bytes 135200 | tf_op jit(solution)/shard_map/ppermute | solution.py:376
  57.1 1.2 %collective-permute-start.11 = (f32[264,128]{1,0:T(8,128)S(1)}, f32[264,128]{1,0:T(8,128)S(1)}, u32[]{:S(2)}, u32[]{:S(2)}) collective-permute-start(f32[264,128]{1,0:T(8,128)S(1)} %get-tuple-element.61), channel_id=1, source_target_pairs={{0,8},{1,33},{2,10},{3,35},{4,12},{5,37},{6,14},{7,39},{8,0},{9,41... | collective-permute-start | bytes 405512 | tf_op jit(solution)/shard_map/ppermute | solution.py:376
  58.3 2.1 %collective-permute-start.12 = (f32[264,128]{1,0:T(8,128)S(1)}, f32[264,128]{1,0:T(8,128)S(1)}, u32[]{:S(2)}, u32[]{:S(2)}) collective-permute-start(f32[264,128]{1,0:T(8,128)S(1)} %get-tuple-element.62), channel_id=1, source_target_pairs={{0,12},{1,49},{2,14},{3,51},{4,8},{5,53},{6,10},{7,55},{8,4},{9,57... | collective-permute-start | bytes 405512 | tf_op jit(solution)/shard_map/ppermute | solution.py:376
  60.4 0.3 collective-permute-start.13
  60.7 2.2 %collective-permute-done.14.refs_1_ = f32[4,16384]{1,0:T(4,128)S(1)} collective-permute-done((f32[4,16384]{1,0:T(4,128)S(1)}, f32[4,16384]{1,0:T(4,128)S(1)}, u32[]{:S(2)}, u32[]{:S(2)}) %collective-permute-start.14) | collective-permute-done | bytes 262176 | tf_op jit(solution)/shard_map/ppermute | solution.py:367
  62.9 0.7 %finish_kernel.1 = f32[4,16384]{1,0:T(4,128)} custom-call(f32[4,16384]{1,0:T(4,128)S(1)} %get-tuple-element.66.refs_0_, f32[4,16384]{1,0:T(4,128)S(1)} %collective-permute-done.14.refs_1_), custom_call_target="tpu_custom_call" | custom-call | tf_op jit(solution)/shard_map/finish_kernel/pallas_call | solution.py:352
  63.6 0.5 collective-permute-done.4.refs_1_
  64.1 0.7 %outputs_kernel.1 = (f32[64,1024]{1,0:T(8,128)}, f32[8,128]{1,0:T(8,128)S(1)}) custom-call(f32[64,1024]{1,0:T(8,128)S(1)} %get-tuple-element.48.refs_0_, f32[64,1024]{1,0:T(8,128)S(1)} %collective-permute-done.4.refs_1_), custom_call_target="tpu_custom_call" | custom-call | tf_op jit(solution)/shard_map/outputs_kernel/pallas_call | solution.py:352
  64.8 0.3 collective-permute-done.12.refs_4_
  65.2 0.3 collective-permute-done.13.refs_5_
  65.4 0.9 %final_kernel.1 = (f32[64,256]{1,0:T(8,128)}, f32[3,64]{1,0:T(4,128)}, f32[1,4]{1,0:T(1,128)}, f32[64,1024]{1,0:T(8,128)}, f32[8,128]{1,0:T(8,128)}) custom-call(f32[16,128]{1,0:T(8,128)S(1)} %get-tuple-element.38.refs_0_, f32[64,1024]{1,0:T(8,128)S(1)} %bitcast.16, f32[264,128]{1,0:T(8,128)S(1)} %get-tuple-element.60.refs_2_, ...), custom_call_target="tpu_custom_call" | custom-call | tf_op jit(solution)/shard_map/final_kernel/pallas_call | solution.py:352
  (26 shorter events, 0.1 us)
Async XLA Ops:
  0.6 16.2 %collective-permute-start = (f32[64,1024]{1,0:T(8,128)}, f32[64,1024]{1,0:T(8,128)S(1)}, u32[]{:S(2)}, u32[]{:S(2)}) collective-permute-start(f32[64,1024]{1,0:T(8,128)} %bitcast.13), channel_id=1, source_target_pairs={{0,2},{1,3},{2,0},{3,1},{4,6},{5,7},{6,4},{7,5},{8,10},{9,11},{10,... | collective-permute-start | bytes 786440 | tf_op jit(solution)/shard_map/ppermute | solution.py:367
  2.4 0.9 %copy-start.4 = (f32[1,64,1024]{2,1,0:T(8,128)S(1)}, f32[1,64,1024]{2,1,0:T(8,128)}, u32[]{:S(2)}) copy-start(f32[1,64,1024]{2,1,0:T(8,128)} %param.11) | copy-start | bytes 786436
  3.3 8.8 %copy-start.9 = (f32[256,64]{0,1:T(8,128)S(1)}, f32[256,64]{0,1:T(8,128)}, u32[]{:S(2)}) copy-start(f32[256,64]{0,1:T(8,128)} %param.16) | copy-start | bytes 196612
  3.3 9.4 %copy-start.7 = (bf16[256,384]{1,0:T(8,128)(2,1)S(1)}, bf16[256,384]{1,0:T(8,128)(2,1)}, u32[]{:S(2)}) copy-start(bf16[256,384]{1,0:T(8,128)(2,1)} %constant.27.clone.refs_4_.refs_3_.refs_5_) | copy-start | bytes 589828
  3.3 9.4 %copy-start.8 = (f32[4,16384]{1,0:T(4,128)S(1)}, f32[4,16384]{1,0:T(4,128)}, u32[]{:S(2)}) copy-start(f32[4,16384]{1,0:T(4,128)} %refs_3_.4) | copy-start | bytes 786436
  4.1 8.7 %copy-start.2 = (bf16[768,256]{1,0:T(8,128)(2,1)S(1)}, bf16[768,256]{1,0:T(8,128)(2,1)}, u32[]{:S(2)}) copy-start(bf16[768,256]{1,0:T(8,128)(2,1)} %constant.28.clone.refs_5_.refs_4_.refs_6_) | copy-start | bytes 1179652
  4.1 8.7 %copy-start.3 = (f32[2,128,128]{2,1,0:T(8,128)S(1)}, f32[2,128,128]{2,1,0:T(8,128)}, u32[]{:S(2)}) copy-start(f32[2,128,128]{2,1,0:T(8,128)} %constant.31.clone.refs_6_.refs_7_.refs_5_) | copy-start | bytes 393220
  4.1 16.7 %all-to-all-start = ((f32[16,32,128]{2,1,0:T(8,128)}), f32[16,32,128]{2,1,0:T(8,128)S(1)}, u32[]{:S(2)}, u32[]{:S(2)}) async-start(f32[16,32,128]{2,1,0:T(8,128)} %bitcast.3), calls=%async_computation | async-start | bytes 524288 | tf_op jit(solution)/shard_map/all_to_all | solution.py:380
  12.1 4.0 %collective-permute-start.1 = (f32[64,128]{1,0:T(8,128)S(1)}, f32[64,128]{1,0:T(8,128)S(1)}, u32[]{:S(2)}, u32[]{:S(2)}) collective-permute-start(f32[64,128]{1,0:T(8,128)S(1)} %dynamic-slice_bitcast_fusion), channel_id=1, source_target_pairs={{0,2},{1,3},{2,0},{3,1},{4,6},{5,7},{6,4},{7,5},{8,10},{9,11},{10,... | collective-permute-start | bytes 98312 | tf_op jit(solution)/shard_map/ppermute | solution.py:367
  12.7 0.7 %copy-start.10 = (f32[3,64]{1,0:T(4,128)S(1)}, f32[3,64]{1,0:T(4,128)}, u32[]{:S(2)}) copy-start(f32[3,64]{1,0:T(4,128)} %refs_1_.1) | copy-start | bytes 2308
  12.7 0.7 %copy-start.11 = (f32[4]{0:T(128)S(1)}, f32[4]{0:T(128)}, u32[]{:S(2)}) copy-start(f32[4]{0:T(128)} %refs_2_.1) | copy-start | bytes 52
  13.4 2.8 %copy-start.1 = (bf16[768,256]{1,0:T(8,128)(2,1)S(1)}, bf16[768,256]{1,0:T(8,128)(2,1)}, u32[]{:S(2)}) copy-start(bf16[768,256]{1,0:T(8,128)(2,1)} %constant.30.clone.refs_4_.refs_6_) | copy-start | bytes 1179652
  13.4 2.8 %copy-start.6 = (bf16[128,768]{1,0:T(8,128)(2,1)S(1)}, bf16[128,768]{1,0:T(8,128)(2,1)}, u32[]{:S(2)}) copy-start(bf16[128,768]{1,0:T(8,128)(2,1)} %constant.29.clone.refs_3_.refs_5_) | copy-start | bytes 589828
  16.1 1.0 %copy-start = (f32[1,64,1024]{2,1,0:T(8,128)S(1)}, f32[1,64,1024]{2,1,0:T(8,128)}, u32[]{:S(2)}) copy-start(f32[1,64,1024]{2,1,0:T(8,128)} %param.12) | copy-start | bytes 786436
  17.4 5.1 %collective-permute-start.2 = (f32[512,128]{1,0:T(8,128)S(1)}, f32[512,128]{1,0:T(8,128)S(1)}, u32[]{:S(2)}, u32[]{:S(2)}) collective-permute-start(f32[512,128]{1,0:T(8,128)S(1)} %get-tuple-element.43), channel_id=1, source_target_pairs={{0,1},{1,0},{2,3},{3,2},{4,5},{5,4},{6,7},{7,6},{8,9},{9,8},{10,11... | collective-permute-start | bytes 786440 | tf_op jit(solution)/shard_map/ppermute | solution.py:367
  38.5 1.6 %collective-permute-start.3 = (f32[512,128]{1,0:T(8,128)S(1)}, f32[512,128]{1,0:T(8,128)S(1)}, u32[]{:S(2)}, u32[]{:S(2)}) collective-permute-start(f32[512,128]{1,0:T(8,128)S(1)} %bitcast.19), channel_id=1, source_target_pairs={{0,1},{1,0},{2,3},{3,2},{4,5},{5,4},{6,7},{7,6},{8,9},{9,8},{10,11... | collective-permute-start | bytes 786440 | tf_op jit(solution)/shard_map/ppermute | solution.py:367
  38.6 1.5 %copy-start.5 = (f32[1,64,1024]{2,1,0:T(8,128)S(1)}, f32[1,64,1024]{2,1,0:T(8,128)}, u32[]{:S(2)}) copy-start(f32[1,64,1024]{2,1,0:T(8,128)} %param.11) | copy-start | bytes 786436
  40.7 8.2 %collective-permute-start.5 = (f32[72,128]{1,0:T(8,128)S(1)}, f32[72,128]{1,0:T(8,128)S(1)}, u32[]{:S(2)}, u32[]{:S(2)}) collective-permute-start(f32[72,128]{1,0:T(8,128)S(1)} %get-tuple-element.53.refs_6_.refs_2_), channel_id=1, source_target_pairs={{0,64},{1,65},{2,66},{3,67},{64,0},{65,1},{66,2},{67,3},{4,68},{5,... | collective-permute-start | bytes 110600 | tf_op jit(solution)/shard_map/ppermute | solution.py:367
  43.7 3.9 %collective-permute-start.7 = (f32[64,128]{1,0:T(8,128)S(1)}, f32[64,128]{1,0:T(8,128)S(1)}, u32[]{:S(2)}, u32[]{:S(2)}) collective-permute-start(f32[64,128]{1,0:T(8,128)S(1)} %get-tuple-element.55), channel_id=1, source_target_pairs={{0,2},{1,3},{2,0},{3,1},{64,66},{65,67},{66,64},{67,65},{4,6},{5,7... | collective-permute-start | bytes 98312 | tf_op jit(solution)/shard_map/ppermute | solution.py:367
  43.8 5.1 %collective-permute-start.6 = (f32[64,128]{1,0:T(8,128)S(1)}, f32[64,128]{1,0:T(8,128)S(1)}, u32[]{:S(2)}, u32[]{:S(2)}) collective-permute-start(f32[64,128]{1,0:T(8,128)S(1)} %get-tuple-element.55), channel_id=1, source_target_pairs={{0,66},{1,67},{2,64},{3,65},{64,2},{65,3},{66,0},{67,1},{4,70},{5,... | collective-permute-start | bytes 98312 | tf_op jit(solution)/shard_map/ppermute | solution.py:367
  49.0 6.7 %collective-permute-start.8 = (f32[264,128]{1,0:T(8,128)S(1)}, f32[264,128]{1,0:T(8,128)S(1)}, u32[]{:S(2)}, u32[]{:S(2)}) collective-permute-start(f32[264,128]{1,0:T(8,128)S(1)} %get-tuple-element.57), channel_id=1, source_target_pairs={{0,32},{1,9},{2,34},{3,11},{4,36},{5,13},{6,38},{7,15},{8,40},{9,1... | collective-permute-start | bytes 405512 | tf_op jit(solution)/shard_map/ppermute | solution.py:376
  50.0 7.1 %collective-permute-start.9 = (f32[264,128]{1,0:T(8,128)S(1)}, f32[264,128]{1,0:T(8,128)S(1)}, u32[]{:S(2)}, u32[]{:S(2)}) collective-permute-start(f32[264,128]{1,0:T(8,128)S(1)} %get-tuple-element.58), channel_id=1, source_target_pairs={{0,48},{1,13},{2,50},{3,15},{4,52},{5,9},{6,54},{7,11},{8,56},{9,5... | collective-permute-start | bytes 405512 | tf_op jit(solution)/shard_map/ppermute | solution.py:376
  51.2 5.9 %collective-permute-start.10 = (f32[264,128]{1,0:T(8,128)S(1)}, f32[264,128]{1,0:T(8,128)S(1)}, u32[]{:S(2)}, u32[]{:S(2)}) collective-permute-start(f32[264,128]{1,0:T(8,128)S(1)} %get-tuple-element.59), channel_id=1, source_target_pairs={{0,16},{1,5},{2,18},{3,7},{4,20},{5,1},{6,22},{7,3},{8,24},{9,13},... | collective-permute-start | bytes 405512 | tf_op jit(solution)/shard_map/ppermute | solution.py:376
  52.6 10.3 %collective-permute-start.14 = (f32[4,16384]{1,0:T(4,128)S(1)}, f32[4,16384]{1,0:T(4,128)S(1)}, u32[]{:S(2)}, u32[]{:S(2)}) collective-permute-start(f32[4,16384]{1,0:T(4,128)S(1)} %get-tuple-element.66.refs_0_), channel_id=1, source_target_pairs={{0,64},{64,0},{1,65},{65,1},{2,66},{66,2},{3,67},{67,3},{4,68},{68... | collective-permute-start | bytes 786440 | tf_op jit(solution)/shard_map/ppermute | solution.py:367
  53.3 10.8 %collective-permute-start.4 = (f32[64,1024]{1,0:T(8,128)S(1)}, f32[64,1024]{1,0:T(8,128)S(1)}, u32[]{:S(2)}, u32[]{:S(2)}) collective-permute-start(f32[64,1024]{1,0:T(8,128)S(1)} %get-tuple-element.49), channel_id=1, source_target_pairs={{0,2},{1,3},{2,0},{3,1},{4,6},{5,7},{6,4},{7,5},{8,10},{9,11},{10,... | collective-permute-start | bytes 786440 | tf_op jit(solution)/shard_map/ppermute | solution.py:367
  57.1 7.7 %collective-permute-start.11 = (f32[264,128]{1,0:T(8,128)S(1)}, f32[264,128]{1,0:T(8,128)S(1)}, u32[]{:S(2)}, u32[]{:S(2)}) collective-permute-start(f32[264,128]{1,0:T(8,128)S(1)} %get-tuple-element.61), channel_id=1, source_target_pairs={{0,8},{1,33},{2,10},{3,35},{4,12},{5,37},{6,14},{7,39},{8,0},{9,41... | collective-permute-start | bytes 405512 | tf_op jit(solution)/shard_map/ppermute | solution.py:376
  58.3 6.8 %collective-permute-start.12 = (f32[264,128]{1,0:T(8,128)S(1)}, f32[264,128]{1,0:T(8,128)S(1)}, u32[]{:S(2)}, u32[]{:S(2)}) collective-permute-start(f32[264,128]{1,0:T(8,128)S(1)} %get-tuple-element.62), channel_id=1, source_target_pairs={{0,12},{1,49},{2,14},{3,51},{4,8},{5,53},{6,10},{7,55},{8,4},{9,57... | collective-permute-start | bytes 405512 | tf_op jit(solution)/shard_map/ppermute | solution.py:376
  60.4 5.0 %collective-permute-start.13 = (f32[264,128]{1,0:T(8,128)S(1)}, f32[264,128]{1,0:T(8,128)S(1)}, u32[]{:S(2)}, u32[]{:S(2)}) collective-permute-start(f32[264,128]{1,0:T(8,128)S(1)} %get-tuple-element.63), channel_id=1, source_target_pairs={{0,4},{1,17},{2,6},{3,19},{4,0},{5,21},{6,2},{7,23},{8,12},{9,25},... | collective-permute-start | bytes 405512 | tf_op jit(solution)/shard_map/ppermute | solution.py:376

commit v7 on v6

--- a/solution.py
+++ b/solution.py
@@ -150,7 +150,7 @@
 def weights_kernel(place_at, mix, mix_far, _rows, _lanes, into, back):
     chan = place_at[1]
     start = pl.multiple_of(128 * lax.shift_right_logical(chan, 1), 128)
-    both = jnp.concatenate([mix[:, pl.ds(start, 128)], mix_far[...]], axis=0)
+    both = jnp.concatenate([mix[:, pl.ds(start, 128)], mix_far[:, pl.ds(start, 128)]], axis=0)
     both = pltpu.roll(both, 64 * jnp.bitwise_and(chan, 1), 1)
     high, low = parts(both)
     back[...] = jnp.concatenate([high, low, high], axis=1)
@@ -358,7 +358,7 @@
         compiler_params=pltpu.CompilerParams(vmem_limit_bytes=20 * 1024 * 1024),
         input_output_aliases=dict(aliases),
         name=kernel.__name__,
-        cost_estimate=pl.CostEstimate(flops=20000000000, bytes_accessed=0, transcendentals=0) if kernel is forward_kernel else None,
+        cost_estimate=pl.CostEstimate(flops=20000000000, bytes_accessed=0, transcendentals=0) if kernel in (forward_kernel, grad_act_kernel) else None,
     )(*args, *after)
 
 
@@ -389,8 +389,7 @@
     mix = mix_weight.T
 
     cot_far = swapped(grad_out, "chan", 2)
-    far = jnp.bitwise_xor(lax.shift_right_logical(chan, 1), 1)
-    mix_far = swapped(lax.dynamic_slice(mix, (0, 128 * far), (64, 128)), "chan", 2)
+    mix_far = swapped(mix, "chan", 2)
     signal_blocks = call(
         blocks_kernel, [(512, SIDE)], signal
     )

time: 66.6 us -> 66 us (level)
  blocking collectives: 15.9 us -> 14 us
  waiting for transfers between devices: 13.5 us -> 15.4 us
    all_to_all x1, waiting for transfers between devices: 3.28 us -> 5.19 us  [turned(): return lax.all_to_all(value, 'seq', 0, 0, tiled=True)]
    all_to_all x1, blocking collectives: 15.9 us -> 14 us  [turned(): return lax.all_to_all(value, 'seq', 0, 0, tiled=True)]
  transfers between devices with their start and end apart: 16 -> 16, of which waited for: 11 -> 10; matrix products, arithmetic and copies ran while one was open for 0% -> 0% of each run, Pallas kernels for 14% -> 14%
where the time goes in v7:
time: 66 us; the launch traced here: 65.7 us
  starting transfers between devices  23.1 us (35%)
  waiting for transfers between devices  15.4 us (23%)
  blocking collectives  14 us (21%)
  Pallas kernels  10.5 us (16%)
  local copies, waits for them, and re-layouts  1.76 us (3%)
  between operations  0.85 us (1%)
    all_to_all x1, blocking collectives, turned(): return lax.all_to_all(value, 'seq', 0, 0, tiled=True)  14 us
    pallas_call x14, Pallas kernels, call(): pl.pallas_call(body, out_shape=shapes if len(shapes) > 1 else shapes[0],...  10.5 us
    all_to_all x1, starting transfers between devices, turned(): return lax.all_to_all(value, 'seq', 0, 0, tiled=True)  8.09 us
    ppermute x9, starting transfers between devices, swapped(): return lax.ppermute(value, axes, [(at, at ^ flip) for at in range(count)])  7.86 us
    ppermute x6, starting transfers between devices, crossed(): return lax.ppermute(value, ('seq', 'chan'), pairs)  7.14 us
    ppermute x9, waiting for transfers between devices, swapped(): return lax.ppermute(value, axes, [(at, at ^ flip) for at in range(count)])  6.45 us
    all_to_all x1, waiting for transfers between devices, turned(): return lax.all_to_all(value, 'seq', 0, 0, tiled=True)  5.19 us
    ppermute x6, waiting for transfers between devices, crossed(): return lax.ppermute(value, ('seq', 'chan'), pairs)  3.75 us
  transfers between devices with their start and end apart: 16, of which 10 were waited for; matrix products, arithmetic and copies ran while one was open for 0% of the time, Pallas kernels for 14%

profile of v7, /device:TPU:0, one launch (start us, length us, event | category | flops | bytes accessed | tf_op | source)
XLA Modules:
  0.0 65.7 jit_solution(16205735487935989771)
XLA Ops:
  0.6 1.7 %collective-permute-start = (f32[64,1024]{1,0:T(8,128)}, f32[64,1024]{1,0:T(8,128)S(1)}, u32[]{:S(2)}, u32[]{:S(2)}) collective-permute-start(f32[64,1024]{1,0:T(8,128)} %bitcast.11), channel_id=1, source_target_pairs={{0,2},{1,3},{2,0},{3,1},{4,6},{5,7},{6,4},{7,5},{8,10},{9,11},{10,... | collective-permute-start | bytes 786440 | tf_op jit(solution)/shard_map/ppermute | solution.py:367
  2.4 0.4 collective-permute-start.1
  2.7 0.9 %copy-done.4 = f32[1,64,1024]{2,1,0:T(8,128)S(1)} copy-done((f32[1,64,1024]{2,1,0:T(8,128)S(1)}, f32[1,64,1024]{2,1,0:T(8,128)}, u32[]{:S(2)}) %copy-start.4) | copy-done | bytes 262168
  3.7 0.8 %blocks_kernel.1.refs_7_ = f32[512,128]{1,0:T(8,128)} custom-call(f32[64,1024]{1,0:T(8,128)S(1)} %bitcast.15), custom_call_target="tpu_custom_call" | custom-call | tf_op jit(solution)/shard_map/blocks_kernel/pallas_call | solution.py:352
  4.5 8.1 %all-to-all-start = ((f32[16,32,128]{2,1,0:T(8,128)}), f32[16,32,128]{2,1,0:T(8,128)S(1)}, u32[]{:S(2)}, u32[]{:S(2)}) async-start(f32[16,32,128]{2,1,0:T(8,128)} %bitcast.3), calls=%async_computation | async-start | bytes 524288 | tf_op jit(solution)/shard_map/all_to_all | solution.py:380
  12.6 0.0 copy-start.10
  12.6 0.0 copy-start.11
  12.6 0.1 pad_add_fusion.refs_0_
  12.7 0.6 copy-done.10
  13.3 1.4 %spectrum_kernel.1 = (f32[512,256]{1,0:T(8,128)S(1)}, f32[16,128]{1,0:T(8,128)S(1)}) custom-call(s32[2]{0:T(128)S(1)} %pad_add_fusion.refs_0_, f32[3,64]{1,0:T(4,128)S(1)} %copy-done.10, f32[4]{0:T(128)S(1)} %copy-done.11, f32[4,16384]{1,0:T(4,128)S(1)} %copy-done.8, bf16[256,384]{1,0:T(8,128)(2,1)S(1)} %copy-done.7, bf16[768,256]{1,0:T(8,128)(2,1)S(1)} %copy-done.1, ...), custom_call_target="tpu_custom_call" | custom-call | tf_op jit(solution)/shard_map/spectrum_kernel/pallas_call | solution.py:352
  14.7 0.0 copy-start.3
  14.7 0.7 %weights_kernel.1 = (bf16[128,384]{1,0:T(8,128)(2,1)S(1)}, bf16[128,384]{1,0:T(8,128)(2,1)S(1)}) custom-call(s32[2]{0:T(128)S(1)} %pad_add_fusion.refs_0_, f32[64,256]{1,0:T(8,128)S(1)} %bitcast.20, f32[64,256]{1,0:T(8,128)S(1)} %collective-permute-done.1.refs_2_, bf16[128,768]{1,0:T(8,128)(2,1)S(1)} %copy-done.6, bf16[768,256]{1,0:T(8,128)(2,1)S(1)} %copy-done), custom_call_target="tpu_custom_call" | custom-call | tf_op jit(solution)/shard_map/weights_kernel/pallas_call | solution.py:352
  15.5 0.2 copy-done.3
  15.6 0.3 grad_act_kernel.1
  16.0 0.1 collective-permute-start.2
  16.1 5.2 %all-to-all-done.refs_1_.refs_2_ = f32[16,32,128]{2,1,0:T(8,128)S(1)} async-done(((f32[16,32,128]{2,1,0:T(8,128)}), f32[16,32,128]{2,1,0:T(8,128)S(1)}, u32[]{:S(2)}, u32[]{:S(2)}) %all-to-all-start) | async-done | bytes 262176 | tf_op jit(solution)/shard_map/all_to_all | solution.py:380
  21.2 1.7 %forward_kernel.1 = (f32[512,256]{1,0:T(8,128)S(1)}, f32[4,128,128]{2,1,0:T(8,128)S(1)}, f32[4,128,128]{2,1,0:T(8,128)S(1)}, f32[16,64,128]{2,1,0:T(8,128)S(1)}) custom-call(f32[16,128]{1,0:T(8,128)S(1)} %get-tuple-element.38.refs_0_, f32[16,32,128]{2,1,0:T(8,128)S(1)} %all-to-all-done.refs_1_.refs_2_, f32[512,256]{1,0:T(8,128)S(1)} %get-tuple-element.39.refs_2_, ...), custom_call_target="tpu_custom_call" | custom-call | flops 20000000000 | tf_op jit(solution)/shard_map/forward_kernel/pallas_call | solution.py:352
  23.0 0.1 join_kernel.1
  23.0 14.0 %all_to_all.10.refs_1_ = f32[16,64,128]{2,1,0:T(8,128)S(1)} all-to-all(f32[16,64,128]{2,1,0:T(8,128)S(1)} %join_kernel.1), channel_id=1, replica_groups=mesh['dp'=2,'seq'=16,'chan'=4] {'seq'}, dimensions={0} | all-to-all | bytes 1048576 | tf_op jit(solution)/shard_map/all_to_all | solution.py:380
  37.1 0.1 collective-permute-start.3
  37.2 0.0 copy-start.5
  37.2 0.9 %slope_kernel.1 = (f32[512,256]{1,0:T(8,128)S(1)}, f32[8,128]{1,0:T(8,128)S(1)}) custom-call(f32[16,128]{1,0:T(8,128)S(1)} %get-tuple-element.38.refs_0_, f32[16,64,128]{2,1,0:T(8,128)S(1)} %all_to_all.10.refs_1_, f32[16,32,128]{2,1,0:T(8,128)S(1)} %all-to-all-done.refs_1_.refs_2_, f32[4,128,128]{2,1,0:T(8,128)S(1)} %get-tuple-element.45.refs_3_, ...), custom_call_target="tpu_custom_call" | custom-call | tf_op jit(solution)/shard_map/slope_kernel/pallas_call | solution.py:352
  38.1 0.6 collective-permute-done.3.refs_1_
  38.7 0.6 tail_kernel.1
  39.3 3.3 %collective-permute-start.5 = (f32[72,128]{1,0:T(8,128)S(1)}, f32[72,128]{1,0:T(8,128)S(1)}, u32[]{:S(2)}, u32[]{:S(2)}) collective-permute-start(f32[72,128]{1,0:T(8,128)S(1)} %get-tuple-element.53.refs_6_.refs_2_), channel_id=1, source_target_pairs={{0,64},{1,65},{2,66},{3,67},{64,0},{65,1},{66,2},{67,3},{4,68},{5,... | collective-permute-start | bytes 110600 | tf_op jit(solution)/shard_map/ppermute | solution.py:367
  42.5 0.7 %collective-permute-start.7 = (f32[64,128]{1,0:T(8,128)S(1)}, f32[64,128]{1,0:T(8,128)S(1)}, u32[]{:S(2)}, u32[]{:S(2)}) collective-permute-start(f32[64,128]{1,0:T(8,128)S(1)} %get-tuple-element.55), channel_id=1, source_target_pairs={{0,2},{1,3},{2,0},{3,1},{64,66},{65,67},{66,64},{67,65},{4,6},{5,7... | collective-permute-start | bytes 98312 | tf_op jit(solution)/shard_map/ppermute | solution.py:367
  43.2 0.4 collective-permute-start.6
  43.6 1.7 %backward_kernel.1 = (f32[16,32,128]{2,1,0:T(8,128)S(1)}, f32[4,16384]{1,0:T(4,128)S(1)}) custom-call(f32[512,256]{1,0:T(8,128)S(1)} %get-tuple-element.51.refs_0_, f32[512,256]{1,0:T(8,128)S(1)} %get-tuple-element.52.refs_1_, f32[512,256]{1,0:T(8,128)S(1)} %get-tuple-element.39.refs_2_, bf16[128,768]{1,0:T(8,128)(2,1)S(1)} %copy-done.6, ...), custom_call_target="tpu_custom_call" | custom-call | tf_op jit(solution)/shard_map/backward_kernel/pallas_call | solution.py:352
  45.3 1.2 %collective-permute-done.7.refs_5_ = f32[64,128]{1,0:T(8,128)S(1)} collective-permute-done((f32[64,128]{1,0:T(8,128)S(1)}, f32[64,128]{1,0:T(8,128)S(1)}, u32[]{:S(2)}, u32[]{:S(2)}) %collective-permute-start.7) | collective-permute-done | bytes 32800 | tf_op jit(solution)/shard_map/ppermute | solution.py:367
  46.4 1.9 %collective-permute-done.6.refs_4_ = f32[64,128]{1,0:T(8,128)S(1)} collective-permute-done((f32[64,128]{1,0:T(8,128)S(1)}, f32[64,128]{1,0:T(8,128)S(1)}, u32[]{:S(2)}, u32[]{:S(2)}) %collective-permute-start.6) | collective-permute-done | bytes 32800 | tf_op jit(solution)/shard_map/ppermute | solution.py:367
  48.3 0.1 merge_kernel.1
  48.4 0.9 %collective-permute-start.8 = (f32[264,128]{1,0:T(8,128)S(1)}, f32[264,128]{1,0:T(8,128)S(1)}, u32[]{:S(2)}, u32[]{:S(2)}) collective-permute-start(f32[264,128]{1,0:T(8,128)S(1)} %get-tuple-element.57), channel_id=1, source_target_pairs={{0,32},{1,9},{2,34},{3,11},{4,36},{5,13},{6,38},{7,15},{8,40},{9,1... | collective-permute-start | bytes 405512 | tf_op jit(solution)/shard_map/ppermute | solution.py:376
  49.3 1.3 %collective-permute-start.9 = (f32[264,128]{1,0:T(8,128)S(1)}, f32[264,128]{1,0:T(8,128)S(1)}, u32[]{:S(2)}, u32[]{:S(2)}) collective-permute-start(f32[264,128]{1,0:T(8,128)S(1)} %get-tuple-element.58), channel_id=1, source_target_pairs={{0,48},{1,13},{2,50},{3,15},{4,52},{5,9},{6,54},{7,11},{8,56},{9,5... | collective-permute-start | bytes 405512 | tf_op jit(solution)/shard_map/ppermute | solution.py:376
  50.6 1.3 %collective-permute-start.10 = (f32[264,128]{1,0:T(8,128)S(1)}, f32[264,128]{1,0:T(8,128)S(1)}, u32[]{:S(2)}, u32[]{:S(2)}) collective-permute-start(f32[264,128]{1,0:T(8,128)S(1)} %get-tuple-element.59), channel_id=1, source_target_pairs={{0,16},{1,5},{2,18},{3,7},{4,20},{5,1},{6,22},{7,3},{8,24},{9,13},... | collective-permute-start | bytes 405512 | tf_op jit(solution)/shard_map/ppermute | solution.py:376
  52.0 0.6 collective-permute-start.14
  52.6 0.6 collective-permute-start.4
  53.2 1.9 %collective-permute-done.8.refs_2_ = f32[264,128]{1,0:T(8,128)S(1)} collective-permute-done((f32[264,128]{1,0:T(8,128)S(1)}, f32[264,128]{1,0:T(8,128)S(1)}, u32[]{:S(2)}, u32[]{:S(2)}) %collective-permute-start.8) | collective-permute-done | bytes 135200 | tf_op jit(solution)/shard_map/ppermute | solution.py:376
  55.1 1.4 %collective-permute-done.9.refs_3_ = f32[264,128]{1,0:T(8,128)S(1)} collective-permute-done((f32[264,128]{1,0:T(8,128)S(1)}, f32[264,128]{1,0:T(8,128)S(1)}, u32[]{:S(2)}, u32[]{:S(2)}) %collective-permute-start.9) | collective-permute-done | bytes 135200 | tf_op jit(solution)/shard_map/ppermute | solution.py:376
  56.5 1.3 %collective-permute-start.11 = (f32[264,128]{1,0:T(8,128)S(1)}, f32[264,128]{1,0:T(8,128)S(1)}, u32[]{:S(2)}, u32[]{:S(2)}) collective-permute-start(f32[264,128]{1,0:T(8,128)S(1)} %get-tuple-element.61), channel_id=1, source_target_pairs={{0,8},{1,33},{2,10},{3,35},{4,12},{5,37},{6,14},{7,39},{8,0},{9,41... | collective-permute-start | bytes 405512 | tf_op jit(solution)/shard_map/ppermute | solution.py:376
  57.8 2.1 %collective-permute-start.12 = (f32[264,128]{1,0:T(8,128)S(1)}, f32[264,128]{1,0:T(8,128)S(1)}, u32[]{:S(2)}, u32[]{:S(2)}) collective-permute-start(f32[264,128]{1,0:T(8,128)S(1)} %get-tuple-element.62), channel_id=1, source_target_pairs={{0,12},{1,49},{2,14},{3,51},{4,8},{5,53},{6,10},{7,55},{8,4},{9,57... | collective-permute-start | bytes 405512 | tf_op jit(solution)/shard_map/ppermute | solution.py:376
  59.8 0.3 collective-permute-start.13
  60.1 2.0 %collective-permute-done.14.refs_1_ = f32[4,16384]{1,0:T(4,128)S(1)} collective-permute-done((f32[4,16384]{1,0:T(4,128)S(1)}, f32[4,16384]{1,0:T(4,128)S(1)}, u32[]{:S(2)}, u32[]{:S(2)}) %collective-permute-start.14) | collective-permute-done | bytes 262176 | tf_op jit(solution)/shard_map/ppermute | solution.py:367
  62.1 0.7 %finish_kernel.1 = f32[4,16384]{1,0:T(4,128)} custom-call(f32[4,16384]{1,0:T(4,128)S(1)} %get-tuple-element.66.refs_0_, f32[4,16384]{1,0:T(4,128)S(1)} %collective-permute-done.14.refs_1_), custom_call_target="tpu_custom_call" | custom-call | tf_op jit(solution)/shard_map/finish_kernel/pallas_call | solution.py:352
  62.8 0.7 %collective-permute-done.4.refs_1_ = f32[64,1024]{1,0:T(8,128)S(1)} collective-permute-done((f32[64,1024]{1,0:T(8,128)S(1)}, f32[64,1024]{1,0:T(8,128)S(1)}, u32[]{:S(2)}, u32[]{:S(2)}) %collective-permute-start.4) | collective-permute-done | bytes 262176 | tf_op jit(solution)/shard_map/ppermute | solution.py:367
  63.6 0.7 %outputs_kernel.1 = (f32[64,1024]{1,0:T(8,128)}, f32[8,128]{1,0:T(8,128)S(1)}) custom-call(f32[64,1024]{1,0:T(8,128)S(1)} %get-tuple-element.48.refs_0_, f32[64,1024]{1,0:T(8,128)S(1)} %collective-permute-done.4.refs_1_), custom_call_target="tpu_custom_call" | custom-call | tf_op jit(solution)/shard_map/outputs_kernel/pallas_call | solution.py:352
  64.3 0.2 collective-permute-done.12.refs_4_
  64.5 0.3 collective-permute-done.13.refs_5_
  64.8 0.9 %final_kernel.1 = (f32[64,256]{1,0:T(8,128)}, f32[3,64]{1,0:T(4,128)}, f32[1,4]{1,0:T(1,128)}, f32[64,1024]{1,0:T(8,128)}, f32[8,128]{1,0:T(8,128)}) custom-call(f32[16,128]{1,0:T(8,128)S(1)} %get-tuple-element.38.refs_0_, f32[64,1024]{1,0:T(8,128)S(1)} %bitcast.14, f32[264,128]{1,0:T(8,128)S(1)} %get-tuple-element.60.refs_2_, ...), custom_call_target="tpu_custom_call" | custom-call | tf_op jit(solution)/shard_map/final_kernel/pallas_call | solution.py:352
  (25 shorter events, 0.1 us)
Async XLA Ops:
  0.6 14.8 %collective-permute-start = (f32[64,1024]{1,0:T(8,128)}, f32[64,1024]{1,0:T(8,128)S(1)}, u32[]{:S(2)}, u32[]{:S(2)}) collective-permute-start(f32[64,1024]{1,0:T(8,128)} %bitcast.11), channel_id=1, source_target_pairs={{0,2},{1,3},{2,0},{3,1},{4,6},{5,7},{6,4},{7,5},{8,10},{9,11},{10,... | collective-permute-start | bytes 786440 | tf_op jit(solution)/shard_map/ppermute | solution.py:367
  2.4 12.3 %collective-permute-start.1 = (f32[64,256]{1,0:T(8,128)}, f32[64,256]{1,0:T(8,128)S(1)}, u32[]{:S(2)}, u32[]{:S(2)}) collective-permute-start(f32[64,256]{1,0:T(8,128)} %bitcast.19), channel_id=1, source_target_pairs={{0,2},{1,3},{2,0},{3,1},{4,6},{5,7},{6,4},{7,5},{8,10},{9,11},{10,... | collective-permute-start | bytes 196616 | tf_op jit(solution)/shard_map/ppermute | solution.py:367
  2.7 0.9 %copy-start.4 = (f32[1,64,1024]{2,1,0:T(8,128)S(1)}, f32[1,64,1024]{2,1,0:T(8,128)}, u32[]{:S(2)}) copy-start(f32[1,64,1024]{2,1,0:T(8,128)} %param.11) | copy-start | bytes 786436
  3.7 9.0 %copy-start.7 = (bf16[256,384]{1,0:T(8,128)(2,1)S(1)}, bf16[256,384]{1,0:T(8,128)(2,1)}, u32[]{:S(2)}) copy-start(bf16[256,384]{1,0:T(8,128)(2,1)} %constant.19.clone.refs_4_.refs_3_.refs_5_) | copy-start | bytes 589828
  3.7 9.0 %copy-start.8 = (f32[4,16384]{1,0:T(4,128)S(1)}, f32[4,16384]{1,0:T(4,128)}, u32[]{:S(2)}) copy-start(f32[4,16384]{1,0:T(4,128)} %refs_3_.4) | copy-start | bytes 786436
  4.5 8.2 %copy-start.1 = (bf16[768,256]{1,0:T(8,128)(2,1)S(1)}, bf16[768,256]{1,0:T(8,128)(2,1)}, u32[]{:S(2)}) copy-start(bf16[768,256]{1,0:T(8,128)(2,1)} %constant.20.clone.refs_5_.refs_4_.refs_6_) | copy-start | bytes 1179652
  4.5 8.2 %copy-start.2 = (f32[2,128,128]{2,1,0:T(8,128)S(1)}, f32[2,128,128]{2,1,0:T(8,128)}, u32[]{:S(2)}) copy-start(f32[2,128,128]{2,1,0:T(8,128)} %constant.23.clone.refs_6_.refs_7_.refs_5_) | copy-start | bytes 393220
  4.5 16.8 %all-to-all-start = ((f32[16,32,128]{2,1,0:T(8,128)}), f32[16,32,128]{2,1,0:T(8,128)S(1)}, u32[]{:S(2)}, u32[]{:S(2)}) async-start(f32[16,32,128]{2,1,0:T(8,128)} %bitcast.3), calls=%async_computation | async-start | bytes 524288 | tf_op jit(solution)/shard_map/all_to_all | solution.py:380
  12.6 0.7 %copy-start.10 = (f32[3,64]{1,0:T(4,128)S(1)}, f32[3,64]{1,0:T(4,128)}, u32[]{:S(2)}) copy-start(f32[3,64]{1,0:T(4,128)} %refs_1_.1) | copy-start | bytes 2308
  12.6 0.7 %copy-start.11 = (f32[4]{0:T(128)S(1)}, f32[4]{0:T(128)}, u32[]{:S(2)}) copy-start(f32[4]{0:T(128)} %refs_2_.1) | copy-start | bytes 52
  13.3 1.5 %copy-start = (bf16[768,256]{1,0:T(8,128)(2,1)S(1)}, bf16[768,256]{1,0:T(8,128)(2,1)}, u32[]{:S(2)}) copy-start(bf16[768,256]{1,0:T(8,128)(2,1)} %constant.22.clone.refs_4_.refs_6_) | copy-start | bytes 1179652
  13.3 1.5 %copy-start.6 = (bf16[128,768]{1,0:T(8,128)(2,1)S(1)}, bf16[128,768]{1,0:T(8,128)(2,1)}, u32[]{:S(2)}) copy-start(bf16[128,768]{1,0:T(8,128)(2,1)} %constant.21.clone.refs_3_.refs_5_) | copy-start | bytes 589828
  13.3 1.5 %copy-start.9 = (f32[256,64]{0,1:T(8,128)S(1)}, f32[256,64]{0,1:T(8,128)}, u32[]{:S(2)}) copy-start(f32[256,64]{0,1:T(8,128)} %param.16) | copy-start | bytes 196612
  14.7 1.0 %copy-start.3 = (f32[1,64,1024]{2,1,0:T(8,128)S(1)}, f32[1,64,1024]{2,1,0:T(8,128)}, u32[]{:S(2)}) copy-start(f32[1,64,1024]{2,1,0:T(8,128)} %param.12) | copy-start | bytes 786436
  16.0 7.0 %collective-permute-start.2 = (f32[512,128]{1,0:T(8,128)S(1)}, f32[512,128]{1,0:T(8,128)S(1)}, u32[]{:S(2)}, u32[]{:S(2)}) collective-permute-start(f32[512,128]{1,0:T(8,128)S(1)} %get-tuple-element.43), channel_id=1, source_target_pairs={{0,1},{1,0},{2,3},{3,2},{4,5},{5,4},{6,7},{7,6},{8,9},{9,8},{10,11... | collective-permute-start | bytes 786440 | tf_op jit(solution)/shard_map/ppermute | solution.py:367
  37.1 1.6 %collective-permute-start.3 = (f32[512,128]{1,0:T(8,128)S(1)}, f32[512,128]{1,0:T(8,128)S(1)}, u32[]{:S(2)}, u32[]{:S(2)}) collective-permute-start(f32[512,128]{1,0:T(8,128)S(1)} %bitcast.17), channel_id=1, source_target_pairs={{0,1},{1,0},{2,3},{3,2},{4,5},{5,4},{6,7},{7,6},{8,9},{9,8},{10,11... | collective-permute-start | bytes 786440 | tf_op jit(solution)/shard_map/ppermute | solution.py:367
  37.2 1.5 %copy-start.5 = (f32[1,64,1024]{2,1,0:T(8,128)S(1)}, f32[1,64,1024]{2,1,0:T(8,128)}, u32[]{:S(2)}) copy-start(f32[1,64,1024]{2,1,0:T(8,128)} %param.11) | copy-start | bytes 786436
  39.3 9.1 %collective-permute-start.5 = (f32[72,128]{1,0:T(8,128)S(1)}, f32[72,128]{1,0:T(8,128)S(1)}, u32[]{:S(2)}, u32[]{:S(2)}) collective-permute-start(f32[72,128]{1,0:T(8,128)S(1)} %get-tuple-element.53.refs_6_.refs_2_), channel_id=1, source_target_pairs={{0,64},{1,65},{2,66},{3,67},{64,0},{65,1},{66,2},{67,3},{4,68},{5,... | collective-permute-start | bytes 110600 | tf_op jit(solution)/shard_map/ppermute | solution.py:367
  42.5 3.9 %collective-permute-start.7 = (f32[64,128]{1,0:T(8,128)S(1)}, f32[64,128]{1,0:T(8,128)S(1)}, u32[]{:S(2)}, u32[]{:S(2)}) collective-permute-start(f32[64,128]{1,0:T(8,128)S(1)} %get-tuple-element.55), channel_id=1, source_target_pairs={{0,2},{1,3},{2,0},{3,1},{64,66},{65,67},{66,64},{67,65},{4,6},{5,7... | collective-permute-start | bytes 98312 | tf_op jit(solution)/shard_map/ppermute | solution.py:367
  43.2 5.1 %collective-permute-start.6 = (f32[64,128]{1,0:T(8,128)S(1)}, f32[64,128]{1,0:T(8,128)S(1)}, u32[]{:S(2)}, u32[]{:S(2)}) collective-permute-start(f32[64,128]{1,0:T(8,128)S(1)} %get-tuple-element.55), channel_id=1, source_target_pairs={{0,66},{1,67},{2,64},{3,65},{64,2},{65,3},{66,0},{67,1},{4,70},{5,... | collective-permute-start | bytes 98312 | tf_op jit(solution)/shard_map/ppermute | solution.py:367
  48.4 6.7 %collective-permute-start.8 = (f32[264,128]{1,0:T(8,128)S(1)}, f32[264,128]{1,0:T(8,128)S(1)}, u32[]{:S(2)}, u32[]{:S(2)}) collective-permute-start(f32[264,128]{1,0:T(8,128)S(1)} %get-tuple-element.57), channel_id=1, source_target_pairs={{0,32},{1,9},{2,34},{3,11},{4,36},{5,13},{6,38},{7,15},{8,40},{9,1... | collective-permute-start | bytes 405512 | tf_op jit(solution)/shard_map/ppermute | solution.py:376
  49.3 7.1 %collective-permute-start.9 = (f32[264,128]{1,0:T(8,128)S(1)}, f32[264,128]{1,0:T(8,128)S(1)}, u32[]{:S(2)}, u32[]{:S(2)}) collective-permute-start(f32[264,128]{1,0:T(8,128)S(1)} %get-tuple-element.58), channel_id=1, source_target_pairs={{0,48},{1,13},{2,50},{3,15},{4,52},{5,9},{6,54},{7,11},{8,56},{9,5... | collective-permute-start | bytes 405512 | tf_op jit(solution)/shard_map/ppermute | solution.py:376
  50.6 5.8 %collective-permute-start.10 = (f32[264,128]{1,0:T(8,128)S(1)}, f32[264,128]{1,0:T(8,128)S(1)}, u32[]{:S(2)}, u32[]{:S(2)}) collective-permute-start(f32[264,128]{1,0:T(8,128)S(1)} %get-tuple-element.59), channel_id=1, source_target_pairs={{0,16},{1,5},{2,18},{3,7},{4,20},{5,1},{6,22},{7,3},{8,24},{9,13},... | collective-permute-start | bytes 405512 | tf_op jit(solution)/shard_map/ppermute | solution.py:376
  52.0 10.1 %collective-permute-start.14 = (f32[4,16384]{1,0:T(4,128)S(1)}, f32[4,16384]{1,0:T(4,128)S(1)}, u32[]{:S(2)}, u32[]{:S(2)}) collective-permute-start(f32[4,16384]{1,0:T(4,128)S(1)} %get-tuple-element.66.refs_0_), channel_id=1, source_target_pairs={{0,64},{64,0},{1,65},{65,1},{2,66},{66,2},{3,67},{67,3},{4,68},{68... | collective-permute-start | bytes 786440 | tf_op jit(solution)/shard_map/ppermute | solution.py:367
  52.6 11.0 %collective-permute-start.4 = (f32[64,1024]{1,0:T(8,128)S(1)}, f32[64,1024]{1,0:T(8,128)S(1)}, u32[]{:S(2)}, u32[]{:S(2)}) collective-permute-start(f32[64,1024]{1,0:T(8,128)S(1)} %get-tuple-element.49), channel_id=1, source_target_pairs={{0,2},{1,3},{2,0},{3,1},{4,6},{5,7},{6,4},{7,5},{8,10},{9,11},{10,... | collective-permute-start | bytes 786440 | tf_op jit(solution)/shard_map/ppermute | solution.py:367
  56.5 7.8 %collective-permute-start.11 = (f32[264,128]{1,0:T(8,128)S(1)}, f32[264,128]{1,0:T(8,128)S(1)}, u32[]{:S(2)}, u32[]{:S(2)}) collective-permute-start(f32[264,128]{1,0:T(8,128)S(1)} %get-tuple-element.61), channel_id=1, source_target_pairs={{0,8},{1,33},{2,10},{3,35},{4,12},{5,37},{6,14},{7,39},{8,0},{9,41... | collective-permute-start | bytes 405512 | tf_op jit(solution)/shard_map/ppermute | solution.py:376
  57.8 6.8 %collective-permute-start.12 = (f32[264,128]{1,0:T(8,128)S(1)}, f32[264,128]{1,0:T(8,128)S(1)}, u32[]{:S(2)}, u32[]{:S(2)}) collective-permute-start(f32[264,128]{1,0:T(8,128)S(1)} %get-tuple-element.62), channel_id=1, source_target_pairs={{0,12},{1,49},{2,14},{3,51},{4,8},{5,53},{6,10},{7,55},{8,4},{9,57... | collective-permute-start | bytes 405512 | tf_op jit(solution)/shard_map/ppermute | solution.py:376
  59.8 5.0 %collective-permute-start.13 = (f32[264,128]{1,0:T(8,128)S(1)}, f32[264,128]{1,0:T(8,128)S(1)}, u32[]{:S(2)}, u32[]{:S(2)}) collective-permute-start(f32[264,128]{1,0:T(8,128)S(1)} %get-tuple-element.63), channel_id=1, source_target_pairs={{0,4},{1,17},{2,6},{3,19},{4,0},{5,21},{6,2},{7,23},{8,12},{9,25},... | collective-permute-start | bytes 405512 | tf_op jit(solution)/shard_map/ppermute | solution.py:376
